TPU v7x, 32 devices: a whole 2x2x4 slice. The times are simulated.
32 devices in a mesh: row: 4 (over x, core), col: 8 (over z, y).
Axes of the slice: x: 2, y: 2, z: 4, core: 2. Of those that a mesh axis runs over, the one named last changes fastest.
Arguments:
- tile_data: bfloat16 [1024, 256, 256], P(('row', 'col')), may hold values from 0 to 256
- owner_ids: int32 [1024, 1], P(('row', 'col')), may hold values from 0 to 31, as said below
- tile_spot: int32 [1024], P(('row', 'col')), may hold values from 0 to 255, as said below
- w_init: float32 [16384, 128], P('row'), may hold values from 0 to 3
- h_init: float32 [32768, 128], P('col'), may hold values from 0 to 3
Outputs:
- w_new: float32 [16384, 128], P('row')
- h_new: float32 [32768, 128], P('col')
Inputs may be any that keep to these rules, and one draw needn't show every extreme that they name: `owner_ids`: owner index o names block row o // 8 and block column o % 8; among the 32 tiles of one ingest device no owner is named more than 2 times, and in every draw one owner is named exactly 2 times by every ingest device. `tile_spot`: positions may repeat within an owner's block.
All inputs are finite; a program needn't handle non-finite values.
Results may differ from a plain program's by a relative error of at most 0.0046.
Values may be sent and summed in bfloat16 or wider, within the bound.
No kernel may reach another device: no remote copies, remote signals or barrier semaphores. Data moves between devices by JAX's collectives and lax.ppermute only.
A program may use at most 192 MiB of HBM per device.

v0:
```python
import math

import jax
import jax.numpy as jnp
from jax import lax
from jax.sharding import PartitionSpec as P

RT = 16
CT = 16


EPS = 1e-06
RIDGE = 1.0
HIGH = lax.Precision.HIGHEST


def accumulate(inbox, target, source, factor, blocks, flipped):
    count = inbox.shape[0]
    tile_size = inbox.shape[1]
    rank_size = factor.shape[1]
    panels = factor.reshape(-1, tile_size, rank_size)
    stride = math.gcd(count, 32)
    levels = jnp.arange(blocks, dtype=jnp.int32)
    pattern = "bji,bjk->bik" if flipped else "bij,bjk->bik"

    def advance(running, block_id):
        start = block_id * stride
        pieces = lax.dynamic_slice_in_dim(inbox, start, stride, 0)
        picked = panels[lax.dynamic_slice_in_dim(source, start, stride, 0)]
        placed = lax.dynamic_slice_in_dim(target, start, stride, 0)
        terms = jnp.einsum(pattern, pieces, picked, preferred_element_type=jnp.float32)
        onehot = (placed[:, None] == levels[None, :]).astype(jnp.float32)
        return (running + jnp.einsum("br,bik->rik", onehot, terms, precision=HIGH), None)

    running = jnp.zeros((blocks, tile_size, rank_size), jnp.float32)
    running, _ = lax.scan(advance, running, jnp.arange(count // stride, dtype=jnp.int32))
    return running.reshape(blocks * tile_size, rank_size)


def sweep_panel(factor, product, gram_mat):
    rank_size = factor.shape[1]
    stride = 16
    current = factor
    for lead_col in range(0, rank_size, stride):
        remain = product[:, lead_col : lead_col + stride] - jnp.dot(
            current, gram_mat[:, lead_col : lead_col + stride], precision=HIGH
        )
        columns = []
        for offset in range(stride):
            column = lead_col + offset
            before_col = current[:, column]
            diag_val = gram_mat[column, column]
            updated = jnp.maximum(
                (remain[:, offset] + before_col * diag_val) / (diag_val + RIDGE), EPS
            )
            remain = (
                remain
                - (updated - before_col)[:, None]
                * gram_mat[column, lead_col : lead_col + stride][None, :]
            )
            columns.append(updated)
        current = lax.dynamic_update_slice_in_dim(current, jnp.stack(columns, axis=1), lead_col, 1)
    return current


def local(tile_data, owner_ids, tile_spot, w_init, h_init):
    row_count = lax.axis_size("row")
    col_count = lax.axis_size("col")
    devices_all = row_count * col_count
    slot_count = tile_data.shape[0]
    tile_size = tile_data.shape[1]
    capacity = max(2, 2 * slot_count // devices_all)
    target = owner_ids[:, 0]
    marks = (target[:, None] == jnp.arange(devices_all, dtype=jnp.int32)[None, :]).astype(jnp.int32)
    earlier = jnp.cumsum(marks, axis=0) - marks
    position = target * capacity + jnp.sum(earlier * marks, axis=1)
    outbox = (
        jnp.zeros((devices_all * capacity, tile_size, tile_size), tile_data.dtype)
        .at[position]
        .set(tile_data)
    )
    out_spots = jnp.zeros((devices_all * capacity,), jnp.int32).at[position].set(tile_spot)
    inbox = lax.all_to_all(
        outbox.reshape(devices_all, capacity, tile_size, tile_size),
        ("row", "col"),
        split_axis=0,
        concat_axis=0,
        tiled=True,
    )
    in_spots = lax.all_to_all(
        out_spots.reshape(devices_all, capacity),
        ("row", "col"),
        split_axis=0,
        concat_axis=0,
        tiled=True,
    )
    inbox = inbox.reshape(devices_all * capacity, tile_size, tile_size)
    in_spots = in_spots.reshape(devices_all * capacity)
    local_row = in_spots // CT
    local_col = in_spots % CT
    w_panel = w_init
    h_panel = h_init
    h_low = h_panel.astype(jnp.bfloat16)
    part_w = accumulate(inbox, local_row, local_col, h_low, RT, False)
    gram_h = jnp.dot(h_panel.T, h_panel, preferred_element_type=jnp.float32, precision=HIGH)
    summed_w, gram_hsum = lax.psum((part_w, gram_h), "col")
    w_panel = sweep_panel(w_panel, summed_w, gram_hsum)
    w_low = w_panel.astype(jnp.bfloat16)
    part_h = accumulate(inbox, local_col, local_row, w_low, CT, True)
    gram_w = jnp.dot(w_panel.T, w_panel, preferred_element_type=jnp.float32, precision=HIGH)
    summed_h, gram_wsum = lax.psum((part_h, gram_w), "row")
    h_panel = sweep_panel(h_panel, summed_h, gram_wsum)
    return (w_panel, h_panel)


def solution(mesh):
    in_specs = (
        P(("row", "col"), None, None),
        P(("row", "col"), None),
        P(("row", "col")),
        P("row", None),
        P("col", None),
    )
    out_specs = (P("row", None), P("col", None))
    return jax.shard_map(local, mesh=mesh, in_specs=in_specs, out_specs=out_specs, check_vma=False)
```

profile of v0, /device:TPU:0, one launch (start us, length us, event | category | flops | bytes accessed | tf_op | source)
XLA Modules:
  0.0 960.2 jit_solution(12686833141584139892)
XLA Ops:
  11.0 7.3 all-to-all-start
  18.3 4.3 broadcast_in_dim.12
  22.6 11.4 %scatter_fusion = bf16[64,256,256]{2,1,0:T(8,128)(2,1)} fusion(bf16[64,256,256]{2,1,0:T(8,128)(2,1)} %broadcast_in_dim.12, s32[32]{0:T(128)S(1)} %fusion.539, bf16[32,256,256]{2,1,0:T(8,128)(2,1)} %param.9), kind=kCustom, calls=%fused_computation.3 | custom fusion | bytes 12583040 | tf_op jit(solution)/shard_map/scatter | solution.py:80
  34.0 6.0 all-to-all-start.1
  40.2 4.1 fusion.798
  45.5 184.0 %all-to-all-done.1 = bf16[32,2,256,256]{3,2,1,0:T(8,128)(2,1)} async-done(((bf16[32,2,256,256]{3,2,1,0:T(8,128)(2,1)}), bf16[32,2,256,256]{3,2,1,0:T(8,128)(2,1)}, u32[]{:S(2)}, u32[]{:S(2)}) %all-to-all-start.1) | async-done | bytes 8388640 | tf_op jit(solution)/shard_map/all_to_all | solution.py:83
  229.5 30.7 %while.22 = (s32[]{:T(128)}, f32[16,256,128]{2,0,1:T(8,128)}, s32[2]{0:T(128)S(1)}, s32[64]{0:T(128)S(1)}, bf16[64,256,256]{2,1,0:T(8,128)(2,1)}, /*index=5*/s32...) while((s32[]{:T(128)}, f32[16,256,128]{2,0,1:T(8,128)}, ...), condition=%wide.region_5.6_spmd.clone, body=%wide.region_4.5_spmd.clone.sunk | while | flops 739247744 | bytes 23073852 | solution.py:36
  231.8 5.4 fusion.836
  237.3 7.3 select_add_fusion.4
  246.8 5.4 fusion.836
  252.2 8.0 select_add_fusion.4
  260.2 2.3 copy.90
  262.5 3.0 copy.131
  265.6 1.9 copy.107
  267.5 12.3 %copy.88 = bf16[32,2,256,256]{2,3,1,0:T(8,128)(2,1)} copy(bf16[32,2,256,256]{3,2,1,0:T(8,128)(2,1)} %all-to-all-done.1) | data formatting | bytes 16777216 | tf_op jit(solution)/shard_map/all_to_all | solution.py:83
  279.8 85.7 %all-reduce.5.cloned.1.call-done = (f32[4096,128]{0,1:T(8,128)}, f32[128,128]{1,0:T(8,128)}) async-done(((f32[4096,128]{0,1:T(8,128)}, f32[128,128]{1,0:T(8,128)}), (f32[4096,128]{0,1:T(8,128)}, f32[128,128]{1,0:T(8,128)})) %all-reduce.5.cloned.1.call-update) | async-done | bytes 2162704 | tf_op jit(solution)/shard_map/psum | solution.py:106
  384.7 3.4 fusion.25
  413.9 2.2 convolution_subtract_fusion.13
  441.9 2.4 convolution_subtract_fusion.12
  469.9 2.2 convolution_subtract_fusion.11
  497.4 2.2 convolution_subtract_fusion.10
  525.3 2.2 convolution_subtract_fusion.9
  552.5 2.2 convolution_subtract_fusion.8
  579.7 2.3 convolution_subtract_fusion.7
  608.1 2.4 fusion.799
  612.1 34.4 %while.23 = (s32[]{:T(128)}, f32[16,256,128]{2,0,1:T(8,128)}, s32[2]{0:T(128)S(1)}, s32[64]{0:T(128)S(1)}, bf16[64,256,256]{1,2,0:T(8,128)(2,1)}, /*index=5*/s32...) while((s32[]{:T(128)}, f32[16,256,128]{2,0,1:T(8,128)}, ...), condition=%wide.region_9.10_spmd.clone, body=%wide.region_8.9_spmd.clone.sunk | while | flops 739247744 | bytes 23073852 | solution.py:36
  613.5 2.1 gather_fusion.1
  615.6 6.0 fusion.841
  621.7 7.3 select_add_fusion.5
  630.3 2.1 gather_fusion.1
  632.5 6.0 fusion.841
  638.6 7.9 select_add_fusion.5
  646.5 3.1 copy.109
  649.6 4.6 copy.132
  654.2 2.9 copy.126
  657.1 2.2 copy.127
  659.3 47.5 %all-reduce.7.cloned.1.call-done = (f32[4096,128]{0,1:T(8,128)}, f32[128,128]{1,0:T(8,128)}) async-done(((f32[4096,128]{0,1:T(8,128)}, f32[128,128]{1,0:T(8,128)}), (f32[4096,128]{0,1:T(8,128)}, f32[128,128]{1,0:T(8,128)})) %all-reduce.7.cloned.1.call-update) | async-done | bytes 2162704 | tf_op jit(solution)/shard_map/psum | solution.py:111
  713.0 1.8 fusion.787
  715.9 1.7 fusion.786
  728.4 3.4 fusion.24
  757.2 2.2 convolution_subtract_fusion.6
  784.6 2.4 convolution_subtract_fusion.5
  812.8 2.2 convolution_subtract_fusion.4
  840.3 2.2 convolution_subtract_fusion.3
  868.2 2.2 convolution_subtract_fusion.2
  895.8 2.2 convolution_subtract_fusion.1
  923.0 2.4 convolution_subtract_fusion
  951.1 1.8 copy.128
  (604 shorter events, 293.9 us)
Async XLA Ops:
  11.0 23.0 %all-to-all-start = ((s32[32,1,2]{2,1,0:T(1,128)}), s32[32,1,2]{2,1,0:T(1,128)S(1)}, u32[]{:S(2)}, u32[]{:S(2)}) async-start(s32[32,1,2]{2,1,0:T(1,128)} %bitcast.3), calls=%async_computation | async-start | bytes 32768 | tf_op jit(solution)/shard_map/all_to_all | solution.py:90
  34.0 6.1 copy-start.1
  34.0 195.5 %all-to-all-start.1 = ((bf16[32,2,256,256]{3,2,1,0:T(8,128)(2,1)}), bf16[32,2,256,256]{3,2,1,0:T(8,128)(2,1)}, u32[]{:S(2)}, u32[]{:S(2)}) async-start(bf16[32,2,256,256]{3,2,1,0:T(8,128)(2,1)} %bitcast.1050), calls=%async_computation.1 | async-start | bytes 16777216 | tf_op jit(solution)/shard_map/all_to_all | solution.py:83
  40.0 325.5 %all-reduce.5.cloned.1.call-start = ((), (), s32[]{:S(2)}) async-start(), calls=%async_computation.2 | async-start | bytes 4325376 | tf_op jit(solution)/shard_map/psum | solution.py:106
  265.5 441.3 %all-reduce.7.cloned.1.call-start = ((), (), s32[]{:S(2)}) async-start(), calls=%async_computation.3 | async-start | bytes 4325376 | tf_op jit(solution)/shard_map/psum | solution.py:111
  408.0 5.8 copy-start.3
  659.3 83.2 %copy-start = (f32[4096,128]{0,1:T(8,128)S(1)}, f32[4096,128]{0,1:T(8,128)}, u32[]{:S(2)}) copy-start(f32[4096,128]{0,1:T(8,128)} %copy.126) | copy-start | bytes 6291460
  751.5 5.7 copy-start.2
Sparse Core Ops, SparseCore 0:
  265.6 99.8 all-reduce.4
  654.4 52.3 all-reduce.6
where the time goes:
time: 977 us; the launch traced here: 960 us
  waiting for transfers between devices  317 us (32%)
  other arithmetic  232 us (24%)
  between operations  178 us (18%)
  local copies, waits for them, and re-layouts  119 us (12%)
  matrix products  98.1 us (10%)
  starting transfers between devices  13.4 us (1%)
    all_to_all x1, waiting for transfers between devices, local(): lax.all_to_all(outbox.reshape(devices_all, capacity, tile_size, tile_size...  184 us
    sub x240, other arithmetic, sweep_panel(): updated - before_col  160 us
    psum x1, waiting for transfers between devices, local(): summed_w, gram_hsum = lax.psum((part_w, gram_h), 'col')  85.7 us
    psum x1, waiting for transfers between devices, local(): summed_h, gram_wsum = lax.psum((part_h, gram_w), 'row')  47.5 us
    sub x224, other arithmetic, sweep_panel(): remain - (updated - before_col)[:, None] * gram_mat[column, lead_col:lead...  46.5 us
    dot_general x16, matrix products, sweep_panel(): jnp.dot(current, gram_mat[:, lead_col:lead_col + stride], precision=HIGH)  38.2 us
    dot_general x4, matrix products, advance(): jnp.einsum('br,bik->rik', onehot, terms, precision=HIGH)  30.4 us
    slice x15, local copies, waits for them, and re-layouts, sweep_panel(): diag_val = gram_mat[column, column]  25.5 us
  transfers between devices with their start and end apart: 4, of which 3 were waited for; matrix products, arithmetic and copies ran while one was open for 4% of the time, Pallas kernels for 0%

commit v1 on v0

v1 whole, which is shorter than its diff:
```python
import jax
import jax.numpy as jnp
from jax import lax
from jax.experimental import pallas as pl
from jax.experimental.pallas import tpu as pltpu
from jax.sharding import Mesh
from jax.sharding import PartitionSpec as P

CT = 16
CAP = 2
EPS = 1e-06
RIDGE = 1.0
HIGH = lax.Precision.HIGHEST
F32 = jnp.float32
LINK = jnp.float16
STEP = 16
VMEM_LIMIT = 48 * 2**20


def params():
    return pltpu.CompilerParams(vmem_limit_bytes=VMEM_LIMIT)


def pack(slot, tile_data, slots):
    count, size = tile_data.shape[0], tile_data.shape[1]

    def kernel(slot_ref, tiles_ref, out_ref, sems):
        copies = [
            pltpu.make_async_copy(tiles_ref.at[s], out_ref.at[slot_ref[s]], sems.at[s])
            for s in range(count)
        ]
        for copy in copies:
            copy.start()
        for copy in copies:
            copy.wait()

    return pl.pallas_call(
        kernel,
        out_shape=jax.ShapeDtypeStruct((slots, size, size), tile_data.dtype),
        in_specs=[pl.BlockSpec(memory_space=pltpu.SMEM), pl.BlockSpec(memory_space=pl.ANY)],
        out_specs=pl.BlockSpec(memory_space=pl.ANY),
        scratch_shapes=[pltpu.SemaphoreType.DMA((count,))],
        compiler_params=params(),
    )(slot, tile_data)


def row_products(inbox, meta, first, panels, chunks):
    senders, held, size, _ = inbox.shape
    groups, rank, length = panels.shape
    width = length // chunks
    per_chunk = width // size

    def kernel(meta_ref, first_ref, tile_ref, panel_ref, out_ref):
        sender = pl.program_id(0)

        @pl.when(sender == 0)
        def _():
            out_ref[...] = jnp.zeros_like(out_ref)

        for slot in range(held):
            spot = meta_ref[sender * held + slot] - 1

            @pl.when(spot >= 0)
            def _():
                trow, tcol = spot // CT, spot % CT
                group = lax.rem(first_ref[0] + groups - slot // CAP, groups)
                panel = panel_ref[group, :, pl.ds(pl.multiple_of(tcol * size, size), size)]
                term = lax.dot_general(
                    panel, tile_ref[0, slot], (((1,), (1,)), ((), ())), preferred_element_type=F32
                )
                lanes = pl.ds(pl.multiple_of((trow % per_chunk) * size, size), size)
                out_ref[trow // per_chunk, :, lanes] += term

    return pl.pallas_call(
        kernel,
        out_shape=jax.ShapeDtypeStruct((chunks, rank, width), F32),
        grid_spec=pltpu.PrefetchScalarGridSpec(
            num_scalar_prefetch=2,
            grid=(senders,),
            in_specs=[
                pl.BlockSpec((1, held, size, size), lambda i, *_: (i, 0, 0, 0)),
                pl.BlockSpec((groups, rank, length), lambda i, *_: (0, 0, 0)),
            ],
            out_specs=pl.BlockSpec((chunks, rank, width), lambda i, *_: (0, 0, 0)),
        ),
        compiler_params=params(),
    )(meta, first, inbox, panels)


def column_products(inbox, meta, me, panels, owners):
    senders, held, size, _ = inbox.shape
    chunks, rank, width = panels.shape
    per_chunk = width // size
    length = chunks * width
    groups = held // CAP
    out_width = length // owners
    per_out = out_width // size
    half = owners // 2

    def kernel(meta_ref, me_ref, tile_ref, panel_ref, keep_ref, send_ref):
        sender = pl.program_id(0)

        @pl.when(sender == 0)
        def _():
            keep_ref[...] = jnp.zeros_like(keep_ref)
            send_ref[...] = jnp.zeros_like(send_ref)

        for slot in range(held):
            spot = meta_ref[sender * held + slot] - 1

            @pl.when(spot >= 0)
            def _():
                trow, tcol = spot // CT, spot % CT
                lanes = pl.ds(pl.multiple_of((trow % per_chunk) * size, size), size)
                panel = panel_ref[trow // per_chunk, :, lanes]
                term = lax.dot_general(
                    panel, tile_ref[0, slot], (((1,), (0,)), ((), ())), preferred_element_type=F32
                )
                owner = tcol // per_out
                far = owner // 2 ^ me_ref[0] // 2
                other = (owner ^ me_ref[0]) % 2
                place = pl.ds(pl.multiple_of((tcol % per_out) * size, size), size)

                @pl.when(other == 0)
                def _():
                    keep_ref[far, slot // CAP, :, place] += term

                @pl.when(other == 1)
                def _():
                    send_ref[far, slot // CAP, :, place] += term

    shape = (half, groups, rank, out_width)
    out_spec = pl.BlockSpec(shape, lambda i, *_: (0, 0, 0, 0))
    return pl.pallas_call(
        kernel,
        out_shape=[jax.ShapeDtypeStruct(shape, F32)] * 2,
        grid_spec=pltpu.PrefetchScalarGridSpec(
            num_scalar_prefetch=2,
            grid=(senders,),
            in_specs=[
                pl.BlockSpec((1, held, size, size), lambda i, *_: (i, 0, 0, 0)),
                pl.BlockSpec((chunks, rank, width), lambda i, *_: (0, 0, 0)),
            ],
            out_specs=[out_spec, out_spec],
        ),
        compiler_params=params(),
    )(meta, me, inbox, panels)


def sweep_block(factor, product, gram, left_ref):
    rank = factor.shape[0]
    left_ref[...] = product - lax.dot_general(
        gram, factor, (((0,), (0,)), ((), ())), precision=HIGH, preferred_element_type=F32
    )
    outs = []
    for lead in range(0, rank, STEP):
        before = factor[lead : lead + STEP]
        block = gram[lead : lead + STEP, lead : lead + STEP]
        left = left_ref[lead : lead + STEP]
        news, moves = [], []
        for k in range(STEP):
            diag = block[k : k + 1, k : k + 1]
            old = before[k : k + 1]
            new = jnp.maximum((left[k : k + 1] + old * diag) / (diag + RIDGE), EPS)
            move = new - old
            news.append(new)
            moves.append(move)
            if k + 1 < STEP:
                left = left - jnp.transpose(block[k : k + 1, :]) * move
        outs.append(jnp.concatenate(news, axis=0))
        if lead + STEP < rank:
            moved = jnp.concatenate(moves, axis=0)
            left_ref[lead + STEP :] -= lax.dot_general(
                gram[lead : lead + STEP, lead + STEP :],
                moved,
                (((0,), (0,)), ((), ())),
                precision=HIGH,
                preferred_element_type=F32,
            )
    return jnp.concatenate(outs, axis=0)


def sweep_w(factor, product, gram):
    rank, width = factor.shape

    def kernel(factor_ref, product_ref, gram_ref, low_ref, own_ref, left_ref):
        new = sweep_block(factor_ref[...], product_ref[...], gram_ref[...], left_ref)
        low_ref[...] = new.astype(jnp.bfloat16)
        own_ref[...] = lax.dot_general(
            new, new, (((1,), (1,)), ((), ())), precision=HIGH, preferred_element_type=F32
        )

    return pl.pallas_call(
        kernel,
        out_shape=[
            jax.ShapeDtypeStruct((rank, width), jnp.bfloat16),
            jax.ShapeDtypeStruct((rank, rank), F32),
        ],
        scratch_shapes=[pltpu.VMEM((rank, width), F32)],
        compiler_params=params(),
    )(factor, product, gram)


def sweep_h(factor, product, gram):
    rank, width = factor.shape

    def kernel(factor_ref, product_ref, gram_ref, low_ref, left_ref):
        new = sweep_block(factor_ref[...], product_ref[...], gram_ref[...], left_ref)
        low_ref[...] = jnp.transpose(new).astype(jnp.bfloat16)

    return pl.pallas_call(
        kernel,
        out_shape=jax.ShapeDtypeStruct((width, rank), jnp.bfloat16),
        scratch_shapes=[pltpu.VMEM((rank, width), F32)],
        compiler_params=params(),
    )(factor, product, gram)


def swap(x, axis, bit):
    size = lax.axis_size(axis)
    return lax.ppermute(x, axis, [(i, i ^ bit) for i in range(size)])


def bits(axis):
    bit = 1
    while bit < lax.axis_size(axis):
        yield bit
        bit *= 2


def everywhere(x, axes, combine):
    for axis in axes:
        for bit in bits(axis):
            x = combine(x, swap(x, axis, bit))
    return x


def local(tile_data, owner_ids, tile_spot, w_init, h_init):
    row_axes, col_axes = ("far", "core"), ("hi", "lo")
    fars, cores = lax.axis_size("far"), lax.axis_size("core")
    his, los = lax.axis_size("hi"), lax.axis_size("lo")
    rows, cols = fars * cores, his * los
    slots = rows * cols * CAP
    size, rank = tile_data.shape[1], w_init.shape[1]
    my_row, my_hi = lax.axis_index(row_axes), lax.axis_index("hi")
    my_col, core = lax.axis_index(col_axes), lax.axis_index("core")

    owner = owner_ids[:, 0]
    same = owner[:, None] == owner[None, :]
    count = owner.shape[0]
    earlier = jnp.arange(count)[None, :] < jnp.arange(count)[:, None]
    nth = jnp.sum((same & earlier).astype(jnp.int32), axis=1)
    o_row, o_col = owner // cols, owner % cols
    slot = ((o_row * los + o_col % los) * his + o_col // los) * CAP + nth
    marks = slot[:, None] == jnp.arange(slots, dtype=jnp.int32)[None, :]
    meta = jnp.sum(jnp.where(marks, tile_spot[:, None] + 1, 0), axis=0)

    plane = ("far", "core", "lo")
    peers = rows * los
    outbox = pack(slot, tile_data, slots).reshape(peers, his * CAP, size, size)
    inbox = lax.all_to_all(outbox, plane, split_axis=0, concat_axis=0, tiled=True)
    meta = lax.all_to_all(
        meta.reshape(peers, his * CAP), plane, split_axis=0, concat_axis=0, tiled=True
    ).reshape(-1)

    h_t = h_init.T
    low = h_t.astype(jnp.bfloat16)
    piece = lax.dynamic_slice_in_dim(low, core * (rank // 2), rank // 2, 0)
    pieces = [piece] + [
        lax.ppermute(piece, "hi", [(i, (i + shift) % his) for i in range(his)])
        for shift in range(1, his)
    ]
    mine = jnp.stack(pieces)
    theirs = swap(mine, "core", 1)
    panels = jnp.where(
        core == 0,
        jnp.concatenate([mine, theirs], axis=1),
        jnp.concatenate([theirs, mine], axis=1),
    )

    gram_h = lax.dot_general(h_t, h_t, (((1,), (1,)), ((), ())), precision=HIGH)
    gram_h = everywhere(gram_h, col_axes, jnp.add)
    peak = jnp.max(tile_data.astype(F32))
    peak = everywhere(jnp.full((8, 128), peak), row_axes + col_axes, jnp.maximum)[0, 0]
    peak = jnp.maximum(peak, 1e-20)

    def scale_for(gram, terms):
        norm = jnp.sqrt(jnp.maximum(jnp.max(gram), 1e-30))
        return 32768.0 / (terms * size**0.5 * peak * norm)

    up = scale_for(gram_h, slots)
    part = row_products(inbox, meta, my_hi[None].astype(jnp.int32), panels, cols)
    width = part.shape[2]
    got = lax.all_to_all((part * up).astype(LINK), col_axes, 0, 0, tiled=True)
    product_w = jnp.sum(got.astype(F32), axis=0) / up
    w_t = lax.dynamic_slice_in_dim(w_init, my_col * width, width, 0).T
    w_low, gram_w = sweep_w(w_t, product_w, gram_h)
    w_all = lax.all_to_all(
        jnp.broadcast_to(w_low[None], (cols, rank, width)), col_axes, 0, 0, tiled=True
    )
    gram_w = everywhere(gram_w, row_axes + col_axes, jnp.add)
    w_new = jnp.transpose(w_all, (0, 2, 1)).reshape(cols * width, rank).astype(F32)

    keep, send = column_products(inbox, meta, my_row[None].astype(jnp.int32), w_all, rows)
    keep = keep + swap(send, "core", 1)
    up = scale_for(gram_w, slots * rows * his)
    half = fars // 2
    while half:
        send = (keep[half:] * up).astype(LINK)
        keep = keep[:half] + swap(send, "far", half).astype(F32) / up
        half //= 2
    got = lax.all_to_all((keep[0] * up).astype(LINK), "hi", 0, 0, tiled=True)
    product_h = jnp.sum(got.astype(F32), axis=0) / up
    length = product_h.shape[1]
    own_t = lax.dynamic_slice_in_dim(h_init, my_row * length, length, 0).T
    h_low = sweep_h(own_t, product_h, gram_w)
    h_all = lax.all_to_all(
        jnp.broadcast_to(h_low[None], (rows, length, rank)), row_axes, 0, 0, tiled=True
    )
    return w_new, h_all.reshape(rows * length, rank).astype(F32)


def solution(mesh):
    rows, cols = mesh.shape["row"], mesh.shape["col"]
    his = 4 if cols % 4 == 0 else 1
    shape = (rows // 2, 2, his, cols // his)
    fine = Mesh(mesh.devices.reshape(shape), ("far", "core", "hi", "lo"))
    row, col = ("far", "core"), ("hi", "lo")
    in_specs = (P(row + col, None, None), P(row + col, None), P(row + col), P(row, None), P(col, None))
    out_specs = (P(row, None), P(col, None))
    return jax.shard_map(local, mesh=fine, in_specs=in_specs, out_specs=out_specs, check_vma=False)
```

time: 977 us -> 346 us (0.35); the launches traced: 960 us -> 346 us
  other arithmetic: 232 us -> 32.6 us
  between operations: 178 us -> 3.45 us
  waiting for transfers between devices: 317 us -> 198 us
  local copies, waits for them, and re-layouts: 119 us -> 19.4 us
  matrix products: 98.1 us -> 3.45 us
  Pallas kernels: 0 us -> 40.4 us
  starting transfers between devices: 13.4 us -> 48.8 us
    sub x464 -> x0, other arithmetic: 207 us -> none  [the longest x240 160 us: sweep_panel(): updated - before_col]
    psum x2 -> x0, waiting for transfers between devices: 133 us -> none  [the longest x1 85.7 us: local(): summed_w, gram_hsum = lax.psum((part_w, gram_h), 'col')]
    ppermute x0 -> x19, waiting for transfers between devices: none -> 118 us  [the longest x16 73.5 us: swap(): return lax.ppermute(x, axis, [(i, i ^ bit) for i in range(size)])]
    all_to_all x2 -> x6, waiting for transfers between devices: 184 us -> 80.2 us  [the longest x1 25.8 us: local(): lax.all_to_all(jnp.broadcast_to(w_low[None], (cols, rank, width)), col_ax...]
    dot_general x26 -> x1, matrix products: 98.1 us -> 3.45 us  [local(): gram_h = lax.dot_general(h_t, h_t, (((1,), (1,)), ((), ())), precision=HIGH)]
    pallas_call x0 -> x5, Pallas kernels: none -> 40.4 us  [the longest x1 11.4 us: column_products(): pl.pallas_call(kernel, out_shape=[jax.ShapeDtypeStruct(shape, F32)] * 2,...]
    slice x31 -> x1, local copies, waits for them, and re-layouts: 35 us -> 0.48 us  [local(): everywhere(jnp.full((8, 128), peak), row_axes + col_axes, jnp.maximum)[0, 0]]
    max x16 -> x5, other arithmetic: 21 us -> 0.02 us  [everywhere(): x = combine(x, swap(x, axis, bit))]
  transfers between devices with their start and end apart: 4 -> 25, of which waited for: 3 -> 16; matrix products, arithmetic and copies ran while one was open for 4% -> 9% of each run, Pallas kernels for 0% -> 1%
where the time goes in v1:
time: 346 us
  waiting for transfers between devices  198 us (57%)
  starting transfers between devices  48.8 us (14%)
  Pallas kernels  40.4 us (12%)
  other arithmetic  32.6 us (9%)
  local copies, waits for them, and re-layouts  19.4 us (6%)
    ppermute x16, waiting for transfers between devices, swap(): return lax.ppermute(x, axis, [(i, i ^ bit) for i in range(size)])  73.5 us
    ppermute x3, waiting for transfers between devices, local(): lax.ppermute(piece, 'hi', [(i, (i + shift) % his) for i in range(his)])  44.4 us
    all_to_all x1, waiting for transfers between devices, local(): lax.all_to_all(jnp.broadcast_to(w_low[None], (cols, rank, width)), col_ax...  25.8 us
    all_to_all x1, waiting for transfers between devices, local(): got = lax.all_to_all((part * up).astype(LINK), col_axes, 0, 0, tiled=True)  23.7 us
    all_to_all x1, waiting for transfers between devices, local(): got = lax.all_to_all((keep[0] * up).astype(LINK), 'hi', 0, 0, tiled=True)  20.6 us
    ppermute x16, starting transfers between devices, swap(): return lax.ppermute(x, axis, [(i, i ^ bit) for i in range(size)])  14.7 us
    pallas_call x1, Pallas kernels, column_products(): pl.pallas_call(kernel, out_shape=[jax.ShapeDtypeStruct(shape, F32)] * 2,...  11.4 us
    pallas_call x1, Pallas kernels, row_products(): pl.pallas_call(kernel, out_shape=jax.ShapeDtypeStruct((chunks, rank, widt...  10.8 us
  transfers between devices with their start and end apart: 25, of which 16 were waited for; matrix products, arithmetic and copies ran while one was open for 9% of the time, Pallas kernels for 1%

profile of v1, /device:TPU:0, one launch (start us, length us, event | category | flops | bytes accessed | tf_op | source)
XLA Modules:
  0.0 346.1 jit_solution(16044736528591097555)
XLA Ops:
  3.8 5.2 %all-to-all-start = ((s32[8,1,8]{2,1,0:T(1,128)}), s32[8,1,8]{2,1,0:T(1,128)S(1)}, u32[]{:S(2)}, u32[]{:S(2)}) async-start(s32[8,1,8]{2,1,0:T(1,128)} %bitcast.4), calls=%async_computation | async-start | bytes 8192 | tf_op jit(solution)/shard_map/all_to_all | solution.py:262
  9.7 2.2 copy-done.1
  11.9 2.8 shard_map.68
  14.7 5.0 %all-to-all-start.1 = ((bf16[8,8,256,256]{3,2,1,0:T(8,128)(2,1)}), bf16[8,8,256,256]{3,2,1,0:T(8,128)(2,1)}, u32[]{:S(2)}, u32[]{:S(2)}) async-start(bf16[8,8,256,256]{3,2,1,0:T(8,128)(2,1)} %bitcast.38), calls=%async_computation.1 | async-start | bytes 16777216 | tf_op jit(solution)/shard_map/all_to_all | solution.py:261
  21.0 1.5 copy.25
  22.5 3.7 %collective-permute-start.2 = (bf16[64,4096]{1,0:T(8,128)(2,1)S(1)}, bf16[64,4096]{1,0:T(8,128)(2,1)S(1)}, u32[]{:S(2)}, u32[]{:S(2)}) collective-permute-start(bf16[64,4096]{1,0:T(8,128)(2,1)S(1)} %bitcast.39), channel_id=1, source_target_pairs={{0,6},{2,0},{4,2},{6,4},{1,7},{3,1},{5,3},{7,5},{8,14},{10,8},{12,... | collective-permute-start | bytes 1572872 | tf_op jit(solution)/shard_map/ppermute | solution.py:270
  27.2 11.3 %collective-permute-done.2 = bf16[64,4096]{1,0:T(8,128)(2,1)S(1)} collective-permute-done((bf16[64,4096]{1,0:T(8,128)(2,1)S(1)}, bf16[64,4096]{1,0:T(8,128)(2,1)S(1)}, u32[]{:S(2)}, u32[]{:S(2)}) %collective-permute-start.2) | collective-permute-done | bytes 524320 | tf_op jit(solution)/shard_map/ppermute | solution.py:270
  38.5 33.1 %collective-permute-done.1 = bf16[64,4096]{1,0:T(8,128)(2,1)S(1)} collective-permute-done((bf16[64,4096]{1,0:T(8,128)(2,1)S(1)}, bf16[64,4096]{1,0:T(8,128)(2,1)S(1)}, u32[]{:S(2)}, u32[]{:S(2)}) %collective-permute-start.1) | collective-permute-done | bytes 524320 | tf_op jit(solution)/shard_map/ppermute | solution.py:270
  71.7 1.7 pad_maximum_fusion
  73.3 3.5 fusion.10
  77.6 4.9 %reduce_max.32 = bf16[]{:T(256)} reduce(bf16[32,256,256]{2,1,0:T(8,128)(2,1)} %tiles_ref.1, bf16[]{:T(256)} %constant.90.clone.1), dimensions={0,1,2}, to_apply=%region_2.3 | reduce | flops 2097151 | bytes 4194308 | tf_op jit(solution)/shard_map/reduce_max | solution.py:283
  83.1 1.8 collective-permute-start.4
  85.5 2.0 collective-permute-start.10
  87.5 25.5 %collective-permute-done.4 = f32[8,128]{1,0:T(8,128)S(1)} collective-permute-done((f32[8,128]{1,0:T(8,128)S(1)}, f32[8,128]{1,0:T(8,128)S(1)}, u32[]{:S(2)}, u32[]{:S(2)}) %collective-permute-start.4) | collective-permute-done | bytes 4128 | tf_op jit(solution)/shard_map/ppermute | solution.py:221
  113.0 1.6 collective-permute-start.11
  114.5 1.6 collective-permute-start.6
  116.2 2.0 collective-permute-done.6
  118.1 2.6 collective-permute-start.7
  120.8 1.9 collective-permute-done.7
  124.8 1.4 collective-permute-done.8
  128.6 6.3 %maximum_select_fusion.panel_ref = bf16[4,128,4096]{2,1,0:T(8,128)(2,1)} fusion(bf16[4,64,4096]{2,1,0:T(8,128)(2,1)} %collective-permute-done.3, bf16[1,64,4096]{2,1,0:T(8,128)(2,1)} %bitcast.46, bf16[1,64,4096]{2,1,0:T(8,128)(2,1)} %bitcast.48, bf16[1,64,4096]{2,1,0:T(8,128)(2,1)} %bitcast.50, bf16[1,64,4096]{2,1,0:T(8,128)(2,1)S(1)} %bitcast.43, pred[]{:T(512)S(6)} %eq.44), kind=kLoop, calls=%fused_computation | loop fusion | flops 44040192 | bytes 8388609 | tf_op jit(solution)/shard_map/jit(_where)/select_n | solution.py:275
  134.9 10.8 %shard_map.69 = f32[8,128,512]{2,1,0:T(8,128)S(1)} custom-call(s32[64]{0:T(128)S(1)} %reshape.36.meta_ref, s32[1]{0:T(128)} %bitcast.5.first_ref, bf16[8,8,256,256]{3,2,1,0:T(8,128)(2,1)} %all-to-all-done.1.tile_ref, bf16[4,128,4096]{2,1,0:T(8,128)(2,1)} %maximum_select_fusion.panel_ref), custom_call_target="tpu_custom_call" | custom-call | tf_op jit(solution)/shard_map/pallas_call | solution.py:74
  147.0 6.9 %all-to-all-start.2 = ((f16[8,128,512]{2,1,0:T(8,128)(2,1)}), f16[8,128,512]{2,1,0:T(8,128)(2,1)}, u32[]{:S(2)}, u32[]{:S(2)}) async-start(f16[8,128,512]{2,1,0:T(8,128)(2,1)} %multiply_convert_fusion), calls=%async_computation.2 | async-start | bytes 2097152 | tf_op jit(solution)/shard_map/all_to_all | solution.py:294
  155.0 23.7 %all-to-all-done.2 = f16[8,128,512]{2,1,0:T(8,128)(2,1)} async-done(((f16[8,128,512]{2,1,0:T(8,128)(2,1)}), f16[8,128,512]{2,1,0:T(8,128)(2,1)}, u32[]{:S(2)}, u32[]{:S(2)}) %all-to-all-start.2) | async-done | bytes 1048608 | tf_op jit(solution)/shard_map/all_to_all | solution.py:294
  178.7 1.4 convert_reduce_fusion.1
  180.2 6.6 %shard_map.70 = (bf16[128,512]{1,0:T(8,128)(2,1)S(1)}, f32[128,128]{1,0:T(8,128)S(1)}) custom-call(f32[128,512]{1,0:T(8,128)S(1)} %bitcast.37, f32[128,512]{1,0:T(8,128)S(1)} %broadcast_divide_fusion.1.product_ref, f32[128,128]{1,0:T(8,128)S(1)} %get-tuple-element.13.gram_ref), custom_call_target="tpu_custom_call" | custom-call | tf_op jit(solution)/shard_map/pallas_call | solution.py:193
  187.9 3.6 %all-to-all-start.3 = ((bf16[8,128,512]{2,1,0:T(8,128)(2,1)}), bf16[8,128,512]{2,1,0:T(8,128)(2,1)S(1)}, u32[]{:S(2)}, u32[]{:S(2)}) async-start(bf16[8,128,512]{2,1,0:T(8,128)(2,1)} %broadcast_in_dim.42), calls=%async_computation.3 | async-start | bytes 2097152 | tf_op jit(solution)/shard_map/all_to_all | solution.py:298
  191.5 25.8 %all-to-all-done.3.panel_ref = bf16[8,128,512]{2,1,0:T(8,128)(2,1)S(1)} async-done(((bf16[8,128,512]{2,1,0:T(8,128)(2,1)}), bf16[8,128,512]{2,1,0:T(8,128)(2,1)S(1)}, u32[]{:S(2)}, u32[]{:S(2)}) %all-to-all-start.3) | async-done | bytes 1048608 | tf_op jit(solution)/shard_map/all_to_all | solution.py:298
  217.3 11.4 %shard_map.71 = (f32[2,4,128,1024]{3,2,1,0:T(8,128)S(1)}, f32[2,4,128,1024]{3,2,1,0:T(8,128)}) custom-call(s32[64]{0:T(128)S(1)} %reshape.36.meta_ref, s32[1]{0:T(128)} %bitcast.16.me_ref, bf16[8,8,256,256]{3,2,1,0:T(8,128)(2,1)} %all-to-all-done.1.tile_ref, bf16[8,128,512]{2,1,0:T(8,128)(2,1)S(1)} %all-to-all-done.3.panel_ref), custom_call_target="tpu_custom_call" | custom-call | tf_op jit(solution)/shard_map/pallas_call | solution.py:134
  228.7 2.0 copy-done.2
  231.5 4.3 %collective-permute-done.13 = f32[128,128]{1,0:T(8,128)S(1)} collective-permute-done((f32[128,128]{1,0:T(8,128)S(1)}, f32[128,128]{1,0:T(8,128)S(1)}, u32[]{:S(2)}, u32[]{:S(2)}) %collective-permute-start.13) | collective-permute-done | bytes 65568 | tf_op jit(solution)/shard_map/ppermute | solution.py:221
  235.9 2.5 collective-permute-done.14
  238.5 4.4 %collective-permute-done.15 = f32[128,128]{1,0:T(8,128)S(1)} collective-permute-done((f32[128,128]{1,0:T(8,128)S(1)}, f32[128,128]{1,0:T(8,128)S(1)}, u32[]{:S(2)}, u32[]{:S(2)}) %collective-permute-start.15) | collective-permute-done | bytes 65568 | tf_op jit(solution)/shard_map/ppermute | solution.py:221
  243.1 5.7 %collective-permute-done.16 = f32[128,128]{1,0:T(8,128)S(1)} collective-permute-done((f32[128,128]{1,0:T(8,128)S(1)}, f32[128,128]{1,0:T(8,128)S(1)}, u32[]{:S(2)}, u32[]{:S(2)}) %collective-permute-start.16) | collective-permute-done | bytes 65568 | tf_op jit(solution)/shard_map/ppermute | solution.py:221
  248.8 1.9 collective-permute-start.17
  250.7 2.4 collective-permute-done.17
  254.5 4.4 %add.109 = f32[2,4,128,1024]{3,2,1,0:T(8,128)S(1)} add(f32[2,4,128,1024]{3,2,1,0:T(8,128)} %copy-done.2, f32[2,4,128,1024]{3,2,1,0:T(8,128)} %collective-permute-done.12) | non-fusion elementwise | flops 1048576 | bytes 12582912 | tf_op jit(solution)/shard_map/add | solution.py:305
  259.3 23.5 %collective-permute-done.18 = f16[1,4,128,1024]{3,2,1,0:T(8,128)(2,1)S(1)} collective-permute-done((f16[1,4,128,1024]{3,2,1,0:T(8,128)(2,1)S(1)}, f16[1,4,128,1024]{3,2,1,0:T(8,128)(2,1)S(1)}, u32[]{:S(2)}, u32[]{:S(2)}) %collective-permute-start.18) | collective-permute-done | bytes 1048608 | tf_op jit(solution)/shard_map/ppermute | solution.py:221
  284.1 4.5 %all-to-all-start.4 = ((f16[4,128,1024]{2,1,0:T(8,128)(2,1)}), f16[4,128,1024]{2,1,0:T(8,128)(2,1)}, u32[]{:S(2)}, u32[]{:S(2)}) async-start(f16[4,128,1024]{2,1,0:T(8,128)(2,1)} %fusion.3), calls=%async_computation.4 | async-start | bytes 2097152 | tf_op jit(solution)/shard_map/all_to_all | solution.py:312
  289.5 2.1 copy.26
  291.5 20.6 %all-to-all-done.4 = f16[4,128,1024]{2,1,0:T(8,128)(2,1)} async-done(((f16[4,128,1024]{2,1,0:T(8,128)(2,1)}), f16[4,128,1024]{2,1,0:T(8,128)(2,1)}, u32[]{:S(2)}, u32[]{:S(2)}) %all-to-all-start.4) | async-done | bytes 1048608 | tf_op jit(solution)/shard_map/all_to_all | solution.py:312
  312.1 1.5 convert_reduce_fusion
  314.8 8.8 %shard_map.72 = bf16[1024,128]{1,0:T(8,128)(2,1)S(1)} custom-call(f32[128,1024]{1,0:T(8,128)S(1)} %bitcast.36, f32[128,1024]{1,0:T(8,128)S(1)} %broadcast_divide_fusion.product_ref, f32[128,128]{1,0:T(8,128)S(1)} %get-tuple-element.11.gram_ref), custom_call_target="tpu_custom_call" | custom-call | tf_op jit(solution)/shard_map/pallas_call | solution.py:211
  324.7 4.2 %all-to-all-start.5 = ((bf16[4,1024,128]{2,1,0:T(8,128)(2,1)}), bf16[4,1024,128]{2,1,0:T(8,128)(2,1)}, u32[]{:S(2)}, u32[]{:S(2)}) async-start(bf16[4,1024,128]{2,1,0:T(8,128)(2,1)} %broadcast_in_dim.44), calls=%async_computation.5 | async-start | bytes 2097152 | tf_op jit(solution)/shard_map/all_to_all | solution.py:317
  328.9 1.6 convert_bitcast_fusion
  330.5 2.9 copy.22
  333.4 10.0 %all-to-all-done.5 = bf16[4,1024,128]{2,1,0:T(8,128)(2,1)} async-done(((bf16[4,1024,128]{2,1,0:T(8,128)(2,1)}), bf16[4,1024,128]{2,1,0:T(8,128)(2,1)}, u32[]{:S(2)}, u32[]{:S(2)}) %all-to-all-start.5) | async-done | bytes 1048608 | tf_op jit(solution)/shard_map/all_to_all | solution.py:317
  343.5 2.7 bitcast_convert_fusion
  (68 shorter events, 21.1 us)
Async XLA Ops:
  0.6 19.0 %copy-start = (f32[4096,128]{1,0:T(8,128)S(1)}, f32[4096,128]{1,0:T(8,128)}, u32[]{:S(2)}) copy-start(f32[4096,128]{1,0:T(8,128)} %param.9) | copy-start | bytes 6291460
  3.8 10.8 %all-to-all-start = ((s32[8,1,8]{2,1,0:T(1,128)}), s32[8,1,8]{2,1,0:T(1,128)S(1)}, u32[]{:S(2)}, u32[]{:S(2)}) async-start(s32[8,1,8]{2,1,0:T(1,128)} %bitcast.4), calls=%async_computation | async-start | bytes 8192 | tf_op jit(solution)/shard_map/all_to_all | solution.py:262
  9.7 2.2 copy-start.1
  14.7 120.3 %all-to-all-start.1 = ((bf16[8,8,256,256]{3,2,1,0:T(8,128)(2,1)}), bf16[8,8,256,256]{3,2,1,0:T(8,128)(2,1)}, u32[]{:S(2)}, u32[]{:S(2)}) async-start(bf16[8,8,256,256]{3,2,1,0:T(8,128)(2,1)} %bitcast.38), calls=%async_computation.1 | async-start | bytes 16777216 | tf_op jit(solution)/shard_map/all_to_all | solution.py:261
  22.5 16.0 %collective-permute-start.2 = (bf16[64,4096]{1,0:T(8,128)(2,1)S(1)}, bf16[64,4096]{1,0:T(8,128)(2,1)S(1)}, u32[]{:S(2)}, u32[]{:S(2)}) collective-permute-start(bf16[64,4096]{1,0:T(8,128)(2,1)S(1)} %bitcast.39), channel_id=1, source_target_pairs={{0,6},{2,0},{4,2},{6,4},{1,7},{3,1},{5,3},{7,5},{8,14},{10,8},{12,... | collective-permute-start | bytes 1572872 | tf_op jit(solution)/shard_map/ppermute | solution.py:270
  26.2 45.4 %collective-permute-start.1 = (bf16[64,4096]{1,0:T(8,128)(2,1)S(1)}, bf16[64,4096]{1,0:T(8,128)(2,1)S(1)}, u32[]{:S(2)}, u32[]{:S(2)}) collective-permute-start(bf16[64,4096]{1,0:T(8,128)(2,1)S(1)} %bitcast.40), channel_id=1, source_target_pairs={{0,4},{2,6},{4,0},{6,2},{1,5},{3,7},{5,1},{7,3},{8,12},{10,14},{12... | collective-permute-start | bytes 1572872 | tf_op jit(solution)/shard_map/ppermute | solution.py:270
  26.2 45.4 %collective-permute-start = (bf16[64,4096]{1,0:T(8,128)(2,1)S(1)}, bf16[64,4096]{1,0:T(8,128)(2,1)S(1)}, u32[]{:S(2)}, u32[]{:S(2)}) collective-permute-start(bf16[64,4096]{1,0:T(8,128)(2,1)S(1)} %bitcast.41), channel_id=1, source_target_pairs={{0,2},{2,4},{4,6},{6,0},{1,3},{3,5},{5,7},{7,1},{8,10},{10,12},{12... | collective-permute-start | bytes 1572872 | tf_op jit(solution)/shard_map/ppermute | solution.py:270
  38.5 38.2 %copy-start.4 = (bf16[64,4096]{1,0:T(8,128)(2,1)}, bf16[64,4096]{1,0:T(8,128)(2,1)S(1)}, u32[]{:S(2)}) copy-start(bf16[64,4096]{1,0:T(8,128)(2,1)S(1)} %collective-permute-done.2) | copy-start | bytes 1572868
  71.6 5.1 %copy-start.5 = (bf16[64,4096]{1,0:T(8,128)(2,1)}, bf16[64,4096]{1,0:T(8,128)(2,1)S(1)}, u32[]{:S(2)}) copy-start(bf16[64,4096]{1,0:T(8,128)(2,1)S(1)} %collective-permute-done.1) | copy-start | bytes 1572868
  71.7 5.1 %copy-start.6 = (bf16[64,4096]{1,0:T(8,128)(2,1)}, bf16[64,4096]{1,0:T(8,128)(2,1)S(1)}, u32[]{:S(2)}) copy-start(bf16[64,4096]{1,0:T(8,128)(2,1)S(1)} %collective-permute-done) | copy-start | bytes 1572868
  73.3 55.3 %collective-permute-start.3 = (bf16[4,64,4096]{2,1,0:T(8,128)(2,1)}, bf16[4,64,4096]{2,1,0:T(8,128)(2,1)}, u32[]{:S(2)}, u32[]{:S(2)}) collective-permute-start(bf16[4,64,4096]{2,1,0:T(8,128)(2,1)} %pad_maximum_fusion), channel_id=1, source_target_pairs={{0,8},{8,0},{1,9},{9,1},{2,10},{10,2},{3,11},{11,3},{4,12},{12,4},... | collective-permute-start | bytes 6291464 | tf_op jit(solution)/shard_map/ppermute | solution.py:221
  76.8 8.6 %collective-permute-start.9 = (f32[128,128]{1,0:T(8,128)S(1)}, f32[128,128]{1,0:T(8,128)S(1)}, u32[]{:S(2)}, u32[]{:S(2)}) collective-permute-start(f32[128,128]{1,0:T(8,128)S(1)} %fusion.10), channel_id=1, source_target_pairs={{0,2},{2,0},{4,6},{6,4},{1,3},{3,1},{5,7},{7,5},{8,10},{10,8},{12,... | collective-permute-start | bytes 196616 | tf_op jit(solution)/shard_map/ppermute | solution.py:221
  83.1 29.8 %collective-permute-start.4 = (f32[8,128]{1,0:T(8,128)S(1)}, f32[8,128]{1,0:T(8,128)S(1)}, u32[]{:S(2)}, u32[]{:S(2)}) collective-permute-start(f32[8,128]{1,0:T(8,128)S(1)} %broadcast_in_dim.41), channel_id=1, source_target_pairs={{0,16},{16,0},{1,17},{17,1},{2,18},{18,2},{3,19},{19,3},{4,20},{20... | collective-permute-start | bytes 12296 | tf_op jit(solution)/shard_map/ppermute | solution.py:221
  85.5 27.5 %collective-permute-start.10 = (f32[128,128]{1,0:T(8,128)S(1)}, f32[128,128]{1,0:T(8,128)S(1)}, u32[]{:S(2)}, u32[]{:S(2)}) collective-permute-start(f32[128,128]{1,0:T(8,128)S(1)} %add.104), channel_id=1, source_target_pairs={{0,4},{2,6},{4,0},{6,2},{1,5},{3,7},{5,1},{7,3},{8,12},{10,14},{12... | collective-permute-start | bytes 196616 | tf_op jit(solution)/shard_map/ppermute | solution.py:221
  112.9 1.6 collective-permute-start.5
  113.0 14.3 %collective-permute-start.11 = (f32[128,128]{1,0:T(8,128)S(1)}, f32[128,128]{1,0:T(8,128)S(1)}, u32[]{:S(2)}, u32[]{:S(2)}) collective-permute-start(f32[128,128]{1,0:T(8,128)S(1)} %add.105), channel_id=1, source_target_pairs={{0,1},{1,0},{2,3},{3,2},{4,5},{5,4},{6,7},{7,6},{8,9},{9,8},{10,11... | collective-permute-start | bytes 196616 | tf_op jit(solution)/shard_map/ppermute | solution.py:221
  114.5 3.6 %collective-permute-start.6 = (f32[8,128]{1,0:T(8,128)S(1)}, f32[8,128]{1,0:T(8,128)S(1)}, u32[]{:S(2)}, u32[]{:S(2)}) collective-permute-start(f32[8,128]{1,0:T(8,128)S(1)} %fusion.13), channel_id=1, source_target_pairs={{0,2},{2,0},{4,6},{6,4},{1,3},{3,1},{5,7},{7,5},{8,10},{10,8},{12,... | collective-permute-start | bytes 12296 | tf_op jit(solution)/shard_map/ppermute | solution.py:221
  118.1 4.5 %collective-permute-start.7 = (f32[8,128]{1,0:T(8,128)S(1)}, f32[8,128]{1,0:T(8,128)S(1)}, u32[]{:S(2)}, u32[]{:S(2)}) collective-permute-start(f32[8,128]{1,0:T(8,128)S(1)} %max.27), channel_id=1, source_target_pairs={{0,4},{2,6},{4,0},{6,2},{1,5},{3,7},{5,1},{7,3},{8,12},{10,14},{12... | collective-permute-start | bytes 12296 | tf_op jit(solution)/shard_map/ppermute | solution.py:221
  122.6 3.6 %collective-permute-start.8 = (f32[8,128]{1,0:T(8,128)S(1)}, f32[8,128]{1,0:T(8,128)S(1)}, u32[]{:S(2)}, u32[]{:S(2)}) collective-permute-start(f32[8,128]{1,0:T(8,128)S(1)} %max.28), channel_id=1, source_target_pairs={{0,1},{1,0},{2,3},{3,2},{4,5},{5,4},{6,7},{7,6},{8,9},{9,8},{10,11... | collective-permute-start | bytes 12296 | tf_op jit(solution)/shard_map/ppermute | solution.py:221
  147.0 31.8 %all-to-all-start.2 = ((f16[8,128,512]{2,1,0:T(8,128)(2,1)}), f16[8,128,512]{2,1,0:T(8,128)(2,1)}, u32[]{:S(2)}, u32[]{:S(2)}) async-start(f16[8,128,512]{2,1,0:T(8,128)(2,1)} %multiply_convert_fusion), calls=%async_computation.2 | async-start | bytes 2097152 | tf_op jit(solution)/shard_map/all_to_all | solution.py:294
  187.9 29.4 %all-to-all-start.3 = ((bf16[8,128,512]{2,1,0:T(8,128)(2,1)}), bf16[8,128,512]{2,1,0:T(8,128)(2,1)S(1)}, u32[]{:S(2)}, u32[]{:S(2)}) async-start(bf16[8,128,512]{2,1,0:T(8,128)(2,1)} %broadcast_in_dim.42), calls=%async_computation.3 | async-start | bytes 2097152 | tf_op jit(solution)/shard_map/all_to_all | solution.py:298
  228.7 2.0 copy-start.2
  230.6 23.9 %collective-permute-start.12 = (f32[2,4,128,1024]{3,2,1,0:T(8,128)}, f32[2,4,128,1024]{3,2,1,0:T(8,128)}, u32[]{:S(2)}, u32[]{:S(2)}) collective-permute-start(f32[2,4,128,1024]{3,2,1,0:T(8,128)} %get-tuple-element.8), channel_id=1, source_target_pairs={{0,8},{8,0},{1,9},{9,1},{2,10},{10,2},{3,11},{11,3},{4,12},{12,4},... | collective-permute-start | bytes 12582920 | tf_op jit(solution)/shard_map/ppermute | solution.py:221
  231.5 4.3 %collective-permute-start.13 = (f32[128,128]{1,0:T(8,128)S(1)}, f32[128,128]{1,0:T(8,128)S(1)}, u32[]{:S(2)}, u32[]{:S(2)}) collective-permute-start(f32[128,128]{1,0:T(8,128)S(1)} %get-tuple-element.9), channel_id=1, source_target_pairs={{0,16},{16,0},{1,17},{17,1},{2,18},{18,2},{3,19},{19,3},{4,20},{20... | collective-permute-start | bytes 196616 | tf_op jit(solution)/shard_map/ppermute | solution.py:221
  235.8 2.6 collective-permute-start.14
  238.4 4.4 %collective-permute-start.15 = (f32[128,128]{1,0:T(8,128)S(1)}, f32[128,128]{1,0:T(8,128)S(1)}, u32[]{:S(2)}, u32[]{:S(2)}) collective-permute-start(f32[128,128]{1,0:T(8,128)S(1)} %add.111), channel_id=1, source_target_pairs={{0,2},{2,0},{4,6},{6,4},{1,3},{3,1},{5,7},{7,5},{8,10},{10,8},{12,... | collective-permute-start | bytes 196616 | tf_op jit(solution)/shard_map/ppermute | solution.py:221
  242.9 5.9 %collective-permute-start.16 = (f32[128,128]{1,0:T(8,128)S(1)}, f32[128,128]{1,0:T(8,128)S(1)}, u32[]{:S(2)}, u32[]{:S(2)}) collective-permute-start(f32[128,128]{1,0:T(8,128)S(1)} %add.112), channel_id=1, source_target_pairs={{0,4},{2,6},{4,0},{6,2},{1,5},{3,7},{5,1},{7,3},{8,12},{10,14},{12... | collective-permute-start | bytes 196616 | tf_op jit(solution)/shard_map/ppermute | solution.py:221
  248.8 4.3 %collective-permute-start.17 = (f32[128,128]{1,0:T(8,128)S(1)}, f32[128,128]{1,0:T(8,128)S(1)}, u32[]{:S(2)}, u32[]{:S(2)}) collective-permute-start(f32[128,128]{1,0:T(8,128)S(1)} %add.113), channel_id=1, source_target_pairs={{0,1},{1,0},{2,3},{3,2},{4,5},{5,4},{6,7},{7,6},{8,9},{9,8},{10,11... | collective-permute-start | bytes 196616 | tf_op jit(solution)/shard_map/ppermute | solution.py:221
  259.2 23.6 %collective-permute-start.18 = (f16[1,4,128,1024]{3,2,1,0:T(8,128)(2,1)S(1)}, f16[1,4,128,1024]{3,2,1,0:T(8,128)(2,1)S(1)}, u32[]{:S(2)}, u32[]{:S(2)}) collective-permute-start(f16[1,4,128,1024]{3,2,1,0:T(8,128)(2,1)S(1)} %fusion), channel_id=1, source_target_pairs={{0,16},{16,0},{1,17},{17,1},{2,18},{18,2},{3,19},{19,3},{4,20},{20... | collective-permute-start | bytes 3145736 | tf_op jit(solution)/shard_map/ppermute | solution.py:221
  284.1 28.0 %all-to-all-start.4 = ((f16[4,128,1024]{2,1,0:T(8,128)(2,1)}), f16[4,128,1024]{2,1,0:T(8,128)(2,1)}, u32[]{:S(2)}, u32[]{:S(2)}) async-start(f16[4,128,1024]{2,1,0:T(8,128)(2,1)} %fusion.3), calls=%async_computation.4 | async-start | bytes 2097152 | tf_op jit(solution)/shard_map/all_to_all | solution.py:312
  313.7 1.0 copy-start.3
  324.7 18.8 %all-to-all-start.5 = ((bf16[4,1024,128]{2,1,0:T(8,128)(2,1)}), bf16[4,1024,128]{2,1,0:T(8,128)(2,1)}, u32[]{:S(2)}, u32[]{:S(2)}) async-start(bf16[4,1024,128]{2,1,0:T(8,128)(2,1)} %broadcast_in_dim.44), calls=%async_computation.5 | async-start | bytes 2097152 | tf_op jit(solution)/shard_map/all_to_all | solution.py:317

commit v2 on v1

v2 whole, which is shorter than its diff:
```python
import jax
import jax.numpy as jnp
from jax import lax
from jax.experimental import pallas as pl
from jax.experimental.pallas import tpu as pltpu
from jax.sharding import Mesh
from jax.sharding import PartitionSpec as P

CT = 16
CAP = 2
EPS = 1e-06
RIDGE = 1.0
HIGH = lax.Precision.HIGHEST
F32 = jnp.float32
LINK = jnp.float16
STEP = 16
VMEM_LIMIT = 48 * 2**20


def params():
    return pltpu.CompilerParams(vmem_limit_bytes=VMEM_LIMIT)


def pack(slot, tile_data, slots):
    count, size = tile_data.shape[0], tile_data.shape[1]

    def kernel(slot_ref, tiles_ref, out_ref, sems):
        copies = [
            pltpu.make_async_copy(tiles_ref.at[s], out_ref.at[slot_ref[s]], sems.at[s])
            for s in range(count)
        ]
        for copy in copies:
            copy.start()
        for copy in copies:
            copy.wait()

    return pl.pallas_call(
        kernel,
        out_shape=jax.ShapeDtypeStruct((slots, size, size), tile_data.dtype),
        in_specs=[pl.BlockSpec(memory_space=pltpu.SMEM), pl.BlockSpec(memory_space=pl.ANY)],
        out_specs=pl.BlockSpec(memory_space=pl.ANY),
        scratch_shapes=[pltpu.SemaphoreType.DMA((count,))],
        compiler_params=params(),
    )(slot, tile_data)


def row_products(inbox, meta, me, pieces, his, los, width):
    senders, held, size, _ = inbox.shape
    part, length = pieces[0].shape
    rank = 2 * part
    per_chunk = width // size

    def kernel(meta_ref, me_ref, tile_ref, *refs):
        piece_refs, (top_ref, bot_ref), (panel_ref, term_ref) = refs[: 2 * his], refs[-4:-2], refs[-2:]
        sender = pl.program_id(0)
        my_core, my_hi, my_lo = me_ref[1], me_ref[2], me_ref[3]

        @pl.when(sender == 0)
        def _():
            top_ref[...] = jnp.zeros_like(top_ref)
            bot_ref[...] = jnp.zeros_like(bot_ref)
            for side in range(2):
                rows = pl.ds(pl.multiple_of((my_core ^ side) * part, part), part)
                for j in range(his):
                    panel_ref[j, rows, :] = piece_refs[side * his + j][...]

        for slot in range(held):
            spot = jnp.maximum(meta_ref[sender, slot] - 1, 0)
            place = pl.ds(pl.multiple_of((spot % CT) * size, size), size)
            term_ref[slot] = lax.dot_general(
                panel_ref[slot // CAP ^ my_hi, :, place],
                tile_ref[0, slot],
                (((1,), (1,)), ((), ())),
                preferred_element_type=F32,
            )

        for slot in range(held):
            spot = meta_ref[sender, slot] - 1

            @pl.when(spot >= 0)
            def _():
                trow = spot // CT
                chunk = trow // per_chunk
                lanes = pl.ds(pl.multiple_of((trow % per_chunk) * size, size), size)
                at = (chunk % los ^ my_lo, chunk // los ^ my_hi)
                top_ref[at[0], at[1], :, lanes] += term_ref[slot, :part]
                bot_ref[at[0], at[1], :, lanes] += term_ref[slot, part:]

    shape = (los, his, part, width)
    piece_spec = pl.BlockSpec((part, length), lambda i, *_: (0, 0))
    out_spec = pl.BlockSpec(shape, lambda i, *_: (0, 0, 0, 0))
    return pl.pallas_call(
        kernel,
        out_shape=[jax.ShapeDtypeStruct(shape, F32)] * 2,
        grid_spec=pltpu.PrefetchScalarGridSpec(
            num_scalar_prefetch=2,
            grid=(senders,),
            in_specs=[pl.BlockSpec((1, held, size, size), lambda i, *_: (i, 0, 0, 0))]
            + [piece_spec] * (2 * his),
            out_specs=[out_spec] * 2,
            scratch_shapes=[
                pltpu.VMEM((his, rank, length), jnp.bfloat16),
                pltpu.VMEM((held, rank, size), F32),
            ],
        ),
        compiler_params=params(),
    )(meta, me, inbox, *pieces)


def column_products(inbox, meta, me, pieces, his, los, fars, out_width):
    senders, held, size, _ = inbox.shape
    rank, width = pieces[0].shape
    part = rank // 2
    per_chunk, per_out = width // size, out_width // size
    chunks = his * los

    def kernel(meta_ref, me_ref, tile_ref, *refs):
        piece_refs, outs, peak_ref = refs[:chunks], refs[chunks : chunks + 4], refs[chunks + 4]
        panel_ref, term_ref = refs[-2:]
        keeps, sends = outs[:2], outs[2:]
        sender = pl.program_id(0)
        my_far, my_core, my_hi, my_lo = (me_ref[i] for i in range(4))

        @pl.when(sender == 0)
        def _():
            for out in outs:
                out[...] = jnp.zeros_like(out)
            top = jnp.zeros((rank, width), jnp.bfloat16)
            for j in range(chunks):
                panel_ref[j] = piece_refs[j][...]
                top = jnp.maximum(top, piece_refs[j][...])
            peak_ref[...] = jnp.full(peak_ref.shape, jnp.max(top.astype(F32)))

        for slot in range(held):
            spot = jnp.maximum(meta_ref[sender, slot] - 1, 0)
            trow = spot // CT
            chunk = trow // per_chunk
            lanes = pl.ds(pl.multiple_of((trow % per_chunk) * size, size), size)
            at = (chunk // los ^ my_hi) * los + (chunk % los ^ my_lo)
            term_ref[slot] = lax.dot_general(
                panel_ref[at, :, lanes],
                tile_ref[0, slot],
                (((1,), (0,)), ((), ())),
                preferred_element_type=F32,
            )

        for slot in range(held):
            spot = meta_ref[sender, slot] - 1
            tcol = spot % CT
            owner = tcol // per_out
            place = pl.ds(pl.multiple_of((tcol % per_out) * size, size), size)
            at = (owner // 2 ^ my_far, slot // CAP ^ my_hi)
            for side, dests in enumerate((keeps, sends)):

                @pl.when((spot >= 0) & ((owner ^ my_core) % 2 == side))
                def _():
                    dests[0][at[0], at[1], :, place] += term_ref[slot, :part]
                    dests[1][at[0], at[1], :, place] += term_ref[slot, part:]

    shape = (fars, his, part, out_width)
    out_spec = pl.BlockSpec(shape, lambda i, *_: (0, 0, 0, 0))
    return pl.pallas_call(
        kernel,
        out_shape=[jax.ShapeDtypeStruct(shape, F32)] * 4 + [jax.ShapeDtypeStruct((8, 128), F32)],
        grid_spec=pltpu.PrefetchScalarGridSpec(
            num_scalar_prefetch=2,
            grid=(senders,),
            in_specs=[pl.BlockSpec((1, held, size, size), lambda i, *_: (i, 0, 0, 0))]
            + [pl.BlockSpec((rank, width), lambda i, *_: (0, 0))] * chunks,
            out_specs=[out_spec] * 4 + [pl.BlockSpec((8, 128), lambda i, *_: (0, 0))],
            scratch_shapes=[
                pltpu.VMEM((chunks, rank, width), jnp.bfloat16),
                pltpu.VMEM((held, rank, size), F32),
            ],
        ),
        compiler_params=params(),
    )(meta, me, inbox, *pieces)


def assemble(pieces, place, turned):
    count = len(pieces)
    rank, width = pieces[0].shape if turned else pieces[0].shape[::-1]

    def kernel(place_ref, *refs):
        for j in range(count):
            piece = refs[j][...].astype(F32)
            refs[count][j ^ place_ref[0]] = jnp.transpose(piece) if turned else piece

    return pl.pallas_call(
        kernel,
        out_shape=jax.ShapeDtypeStruct((count, width, rank), F32),
        in_specs=[pl.BlockSpec(memory_space=pltpu.SMEM)]
        + [pl.BlockSpec(memory_space=pltpu.VMEM)] * count,
        out_specs=pl.BlockSpec(memory_space=pltpu.VMEM),
        compiler_params=params(),
    )(place, *pieces).reshape(count * width, rank)


def sweep_block(factor, product, gram, left_ref):
    rank = factor.shape[0]
    left_ref[...] = product - lax.dot_general(
        gram, factor, (((0,), (0,)), ((), ())), precision=HIGH, preferred_element_type=F32
    )
    outs = []
    for lead in range(0, rank, STEP):
        before = factor[lead : lead + STEP]
        block = gram[lead : lead + STEP, lead : lead + STEP]
        left = left_ref[lead : lead + STEP]
        news, moves = [], []
        for k in range(STEP):
            diag = block[k : k + 1, k : k + 1]
            old = before[k : k + 1]
            new = jnp.maximum((left[k : k + 1] + old * diag) / (diag + RIDGE), EPS)
            move = new - old
            news.append(new)
            moves.append(move)
            if k + 1 < STEP:
                left = left - jnp.transpose(block[k : k + 1, :]) * move
        outs.append(jnp.concatenate(news, axis=0))
        if lead + STEP < rank:
            moved = jnp.concatenate(moves, axis=0)
            left_ref[lead + STEP :] -= lax.dot_general(
                gram[lead : lead + STEP, lead + STEP :],
                moved,
                (((0,), (0,)), ((), ())),
                precision=HIGH,
                preferred_element_type=F32,
            )
    return jnp.concatenate(outs, axis=0)


def sweep_w(factor, top, bottom, gram):
    rank, width = factor.shape

    def kernel(factor_ref, top_ref, bottom_ref, gram_ref, low_ref, own_ref, left_ref):
        product = jnp.concatenate([top_ref[...], bottom_ref[...]], axis=0)
        new = sweep_block(factor_ref[...], product, gram_ref[...], left_ref)
        low_ref[...] = new.astype(jnp.bfloat16)
        own_ref[...] = lax.dot_general(
            new, new, (((1,), (1,)), ((), ())), precision=HIGH, preferred_element_type=F32
        )

    return pl.pallas_call(
        kernel,
        out_shape=[
            jax.ShapeDtypeStruct((rank, width), jnp.bfloat16),
            jax.ShapeDtypeStruct((rank, rank), F32),
        ],
        scratch_shapes=[pltpu.VMEM((rank, width), F32)],
        compiler_params=params(),
    )(factor, top, bottom, gram)


def sweep_h(factor, top, bottom, gram):
    rank, width = factor.shape

    def kernel(factor_ref, top_ref, bottom_ref, gram_ref, low_ref, left_ref):
        product = jnp.concatenate([top_ref[...], bottom_ref[...]], axis=0)
        new = sweep_block(factor_ref[...], product, gram_ref[...], left_ref)
        low_ref[...] = jnp.transpose(new).astype(jnp.bfloat16)

    return pl.pallas_call(
        kernel,
        out_shape=jax.ShapeDtypeStruct((width, rank), jnp.bfloat16),
        scratch_shapes=[pltpu.VMEM((rank, width), F32)],
        compiler_params=params(),
    )(factor, top, bottom, gram)


def swap(x, axis, bit):
    size = lax.axis_size(axis)
    return lax.ppermute(x, axis, [(i, i ^ bit) for i in range(size)])


def bits(axis):
    bit = 1
    while bit < lax.axis_size(axis):
        yield bit
        bit *= 2


def everywhere(x, axes, combine):
    for axis in axes:
        for bit in bits(axis):
            x = combine(x, swap(x, axis, bit))
    return x


def spread(pieces, axis):
    return [
        piece if j == 0 else swap(piece, axis, j)
        for piece in pieces
        for j in range(lax.axis_size(axis))
    ]


def gather(sums, axis, up, down):
    total = sums[0]
    for j in range(1, lax.axis_size(axis)):
        total = total + swap((sums[j] * up).astype(LINK), axis, j).astype(F32) * down
    return total


def local(tile_data, owner_ids, tile_spot, w_init, h_init):
    row_axes, col_axes = ("far", "core"), ("hi", "lo")
    fars, cores = lax.axis_size("far"), lax.axis_size("core")
    his, los = lax.axis_size("hi"), lax.axis_size("lo")
    rows, cols = fars * cores, his * los
    slots = rows * cols * CAP
    size, rank = tile_data.shape[1], w_init.shape[1]
    width, length = w_init.shape[0] // cols, h_init.shape[0] // rows
    my_row, my_col = lax.axis_index(row_axes), lax.axis_index(col_axes)
    core = lax.axis_index("core")
    me = jnp.stack([lax.axis_index(a) for a in row_axes + col_axes]).astype(jnp.int32)

    owner = owner_ids[:, 0]
    count = owner.shape[0]
    same = owner[:, None] == owner[None, :]
    earlier = jnp.arange(count)[None, :] < jnp.arange(count)[:, None]
    nth = jnp.sum((same & earlier).astype(jnp.int32), axis=1)
    o_row, o_col = owner // cols, owner % cols
    slot = ((o_row * los + o_col % los) * his + o_col // los) * CAP + nth

    plane = ("far", "core", "lo")
    peers, held = rows * los, his * CAP
    outbox = pack(slot, tile_data, slots).reshape(peers, held, size, size)
    inbox = lax.all_to_all(outbox, plane, split_axis=0, concat_axis=0, tiled=True)

    h_t = h_init.T
    piece = lax.dynamic_slice_in_dim(h_t, core * (rank // 2), rank // 2, 0).astype(jnp.bfloat16)
    pieces = spread([piece], "hi")
    pieces += [swap(piece, "core", 1) for piece in pieces]

    gram_h = lax.dot_general(h_t, h_t, (((1,), (1,)), ((), ())), precision=HIGH)
    gram_h = everywhere(gram_h, col_axes, jnp.add)
    peak = everywhere(jnp.full((8, 128), jnp.max(tile_data).astype(F32)), ("hi",), jnp.maximum)[0, 0]
    peak = jnp.ceil(jnp.log2(jnp.maximum(peak, 1e-20))).astype(jnp.int32)
    marks = slot[:, None] == jnp.arange(slots, dtype=jnp.int32)[None, :]
    meta = jnp.sum(jnp.where(marks, tile_spot[:, None] + 1, 0), axis=0).reshape(peers, held)
    meta = jnp.concatenate([meta, jnp.broadcast_to(peak, (peers, 1))], axis=1)
    meta = lax.all_to_all(meta, plane, split_axis=0, concat_axis=0, tiled=True)
    peak = jnp.exp2(jnp.max(meta[:, held]).astype(F32))

    norm = jnp.sqrt(jnp.maximum(jnp.max(gram_h), 1e-30))
    down = slots * size**0.5 * los / 32768.0 * peak * norm
    up = 1.0 / down
    parts = row_products(inbox, meta, me, pieces, his, los, width)
    sums = [gather(gather(part, "lo", up, down), "hi", up, down) for part in parts]
    w_t = lax.dynamic_slice_in_dim(w_init, my_col * width, width, 0).T
    w_low, gram_w = sweep_w(w_t, *sums, gram_h)
    pieces = spread(spread([w_low], "hi"), "lo")
    gram_w = everywhere(gram_w, row_axes + col_axes, jnp.add)

    *parts, high = column_products(inbox, meta, me, pieces, his, los, fars, length)
    w_new = assemble(pieces, my_col[None].astype(jnp.int32), True)
    high = jnp.maximum(everywhere(high, row_axes, jnp.maximum)[0, 0], 1e-20)
    down = slots * rows * size / 32768.0 * peak * high
    up = 1.0 / down
    sums = []
    for keep, send in zip(parts[:2], parts[2:]):
        keep = keep + swap(send, "core", 1)
        half = fars // 2
        while half:
            keep = keep[:half] + swap((keep[half:] * up).astype(LINK), "far", half).astype(F32) * down
            half //= 2
        sums.append(gather(keep[0], "hi", up, down))
    own_t = lax.dynamic_slice_in_dim(h_init, my_row * length, length, 0).T
    h_low = sweep_h(own_t, *sums, gram_w)
    h_new = assemble(spread(spread([h_low], "far"), "core"), my_row[None].astype(jnp.int32), False)
    return w_new, h_new


def solution(mesh):
    rows, cols = mesh.shape["row"], mesh.shape["col"]
    his = 4 if cols % 4 == 0 else 1
    shape = (rows // 2, 2, his, cols // his)
    fine = Mesh(mesh.devices.reshape(shape), ("far", "core", "hi", "lo"))
    row, col = ("far", "core"), ("hi", "lo")
    in_specs = (P(row + col, None, None), P(row + col, None), P(row + col), P(row, None), P(col, None))
    out_specs = (P(row, None), P(col, None))
    return jax.shard_map(local, mesh=fine, in_specs=in_specs, out_specs=out_specs, check_vma=False)
```

time: 346 us -> 283 us (0.82)
  waiting for transfers between devices: 198 us -> 119 us
  starting transfers between devices: 48.8 us -> 73.3 us
  other arithmetic: 32.6 us -> 19.8 us
  Pallas kernels: 40.4 us -> 44.8 us
    all_to_all x5 -> x1, waiting for transfers between devices: 80.2 us -> 0.01 us  [local(): meta = lax.all_to_all(meta, plane, split_axis=0, concat_axis=0, tiled=True)]
    ppermute x16 -> x47, starting transfers between devices: 14.7 us -> 64.3 us  [swap(): return lax.ppermute(x, axis, [(i, i ^ bit) for i in range(size)])]
    ppermute x16 -> x47, waiting for transfers between devices: 73.5 us -> 119 us  [swap(): return lax.ppermute(x, axis, [(i, i ^ bit) for i in range(size)])]
    ppermute x3 -> x0, waiting for transfers between devices: 44.4 us -> none  [local(): lax.ppermute(piece, 'hi', [(i, (i + shift) % his) for i in range(his)])]
    all_to_all x5 -> x1, starting transfers between devices: 24.4 us -> 4.06 us  [local(): meta = lax.all_to_all(meta, plane, split_axis=0, concat_axis=0, tiled=True)]
    select_n x1 -> x0, other arithmetic: 6.34 us -> none  [local(): jnp.where(core == 0, jnp.concatenate([mine, theirs], axis=1), jnp.concate...]
    ppermute x3 -> x0, starting transfers between devices: 4.68 us -> none  [local(): lax.ppermute(piece, 'hi', [(i, (i + shift) % his) for i in range(his)])]
    pallas_call x2 -> x4, Pallas kernels: 22.2 us -> 26.6 us  [the longest x1 11.8 us: column_products(): pl.pallas_call(kernel, out_shape=[jax.ShapeDtypeStruct(shape, F32)] * 4 +...]
  transfers between devices with their start and end apart: 25 -> 49, of which waited for: 16 -> 25; matrix products, arithmetic and copies ran while one was open for 9% -> 9% of each run, Pallas kernels for 1% -> 2%
where the time goes in v2:
time: 283 us; the launch traced here: 282 us
  waiting for transfers between devices  119 us (42%)
  starting transfers between devices  73.3 us (26%)
  Pallas kernels  44.8 us (16%)
  other arithmetic  19.8 us (7%)
  local copies, waits for them, and re-layouts  17.4 us (6%)
  between operations  4.53 us (2%)
  matrix products  3.45 us (1%)
    ppermute x47, waiting for transfers between devices, swap(): return lax.ppermute(x, axis, [(i, i ^ bit) for i in range(size)])  119 us
    ppermute x47, starting transfers between devices, swap(): return lax.ppermute(x, axis, [(i, i ^ bit) for i in range(size)])  64.3 us
    pallas_call x1, Pallas kernels, column_products(): pl.pallas_call(kernel, out_shape=[jax.ShapeDtypeStruct(shape, F32)] * 4 +...  11.8 us
    pallas_call x1, Pallas kernels, row_products(): pl.pallas_call(kernel, out_shape=[jax.ShapeDtypeStruct(shape, F32)] * 2,...  11.6 us
    unnamed x29, local copies, waits for them, and re-layouts  11.1 us
    pallas_call x1, Pallas kernels, sweep_h(): pl.pallas_call(kernel, out_shape=jax.ShapeDtypeStruct((width, rank), jnp....  8.8 us
    pallas_call x1, Pallas kernels, sweep_w(): pl.pallas_call(kernel, out_shape=[jax.ShapeDtypeStruct((rank, width), jnp...  6.64 us
  transfers between devices with their start and end apart: 49, of which 25 were waited for; matrix products, arithmetic and copies ran while one was open for 9% of the time, Pallas kernels for 2%

profile of v2, /device:TPU:0, one launch (start us, length us, event | category | flops | bytes accessed | tf_op | source)
XLA Modules:
  0.0 282.1 jit_solution(11540405503737090587)
XLA Ops:
  0.7 5.1 %reduce_max.27 = bf16[]{:T(256)} reduce(bf16[32,256,256]{2,1,0:T(8,128)(2,1)} %tiles_ref.1, bf16[]{:T(256)} %constant.89.clone.1), dimensions={0,1,2}, to_apply=%region_2.3 | reduce | flops 2097151 | bytes 4194308 | tf_op jit(solution)/shard_map/reduce_max | solution.py:336
  6.4 3.1 %collective-permute-start = (f32[8,128]{1,0:T(8,128)S(1)}, f32[8,128]{1,0:T(8,128)S(1)}, u32[]{:S(2)}, u32[]{:S(2)}) collective-permute-start(f32[8,128]{1,0:T(8,128)S(1)} %broadcast_in_dim.30), channel_id=1, source_target_pairs={{0,2},{2,0},{4,6},{6,4},{1,3},{3,1},{5,7},{7,5},{8,10},{10,8},{12,... | collective-permute-start | bytes 12296 | tf_op jit(solution)/shard_map/ppermute | solution.py:272
  11.1 3.0 %collective-permute-start.1 = (f32[8,128]{1,0:T(8,128)S(1)}, f32[8,128]{1,0:T(8,128)S(1)}, u32[]{:S(2)}, u32[]{:S(2)}) collective-permute-start(f32[8,128]{1,0:T(8,128)S(1)} %broadcast_maximum_fusion), channel_id=1, source_target_pairs={{0,4},{2,6},{4,0},{6,2},{1,5},{3,7},{5,1},{7,3},{8,12},{10,14},{12... | collective-permute-start | bytes 12296 | tf_op jit(solution)/shard_map/ppermute | solution.py:272
  17.5 4.1 %all-to-all-start = ((s32[8,1,9]{2,1,0:T(1,128)}), s32[8,1,9]{2,1,0:T(1,128)S(1)}, u32[]{:S(2)}, u32[]{:S(2)}) async-start(s32[8,1,9]{2,1,0:T(1,128)} %bitcast.7), calls=%async_computation | async-start | bytes 8192 | tf_op jit(solution)/shard_map/all_to_all | solution.py:341
  21.6 2.2 copy-done.1
  23.8 2.8 shard_map.68
  26.6 5.0 %all-to-all-start.1 = ((bf16[8,8,256,256]{3,2,1,0:T(8,128)(2,1)}), bf16[8,8,256,256]{3,2,1,0:T(8,128)(2,1)}, u32[]{:S(2)}, u32[]{:S(2)}) async-start(bf16[8,8,256,256]{3,2,1,0:T(8,128)(2,1)} %bitcast.104), calls=%async_computation.1 | async-start | bytes 16777216 | tf_op jit(solution)/shard_map/all_to_all | solution.py:327
  36.1 2.6 collective-permute-start.3
  38.9 20.8 %collective-permute-done.2.refs_1_ = bf16[64,4096]{1,0:T(8,128)(2,1)S(1)} collective-permute-done((bf16[64,4096]{1,0:T(8,128)(2,1)S(1)}, bf16[64,4096]{1,0:T(8,128)(2,1)S(1)}, u32[]{:S(2)}, u32[]{:S(2)}) %collective-permute-start.2) | collective-permute-done | bytes 524320 | tf_op jit(solution)/shard_map/ppermute | solution.py:272
  59.7 14.7 %collective-permute-done.3.refs_2_ = bf16[64,4096]{1,0:T(8,128)(2,1)} collective-permute-done((bf16[64,4096]{1,0:T(8,128)(2,1)S(1)}, bf16[64,4096]{1,0:T(8,128)(2,1)}, u32[]{:S(2)}, u32[]{:S(2)}) %collective-permute-start.3) | collective-permute-done | bytes 524320 | tf_op jit(solution)/shard_map/ppermute | solution.py:272
  74.9 3.5 %fusion.45 = f32[128,128]{1,0:T(8,128)S(1)} fusion(f32[4096,128]{1,0:T(8,128)S(1)} %copy-done), kind=kOutput, calls=%fused_computation.103 | convolution fusion | flops 805306368 | bytes 2162688 | tf_op jit(solution)/shard_map/dot_general | solution.py:334
  78.4 10.6 %collective-permute-start.9 = (f32[128,128]{1,0:T(8,128)S(1)}, f32[128,128]{1,0:T(8,128)S(1)}, u32[]{:S(2)}, u32[]{:S(2)}) collective-permute-start(f32[128,128]{1,0:T(8,128)S(1)} %fusion.45), channel_id=1, source_target_pairs={{0,2},{2,0},{4,6},{6,4},{1,3},{3,1},{5,7},{7,5},{8,10},{10,8},{12,... | collective-permute-start | bytes 196616 | tf_op jit(solution)/shard_map/ppermute | solution.py:272
  89.0 2.8 collective-permute-done.9
  91.7 2.8 %collective-permute-start.10 = (f32[128,128]{1,0:T(8,128)S(1)}, f32[128,128]{1,0:T(8,128)S(1)}, u32[]{:S(2)}, u32[]{:S(2)}) collective-permute-start(f32[128,128]{1,0:T(8,128)S(1)} %add.154), channel_id=1, source_target_pairs={{0,4},{2,6},{4,0},{6,2},{1,5},{3,7},{5,1},{7,3},{8,12},{10,14},{12... | collective-permute-start | bytes 196616 | tf_op jit(solution)/shard_map/ppermute | solution.py:272
  94.6 3.7 %collective-permute-done.10 = f32[128,128]{1,0:T(8,128)S(1)} collective-permute-done((f32[128,128]{1,0:T(8,128)S(1)}, f32[128,128]{1,0:T(8,128)S(1)}, u32[]{:S(2)}, u32[]{:S(2)}) %collective-permute-start.10) | collective-permute-done | bytes 65568 | tf_op jit(solution)/shard_map/ppermute | solution.py:272
  98.4 1.8 collective-permute-start.11
  101.5 24.5 %collective-permute-done.11 = f32[128,128]{1,0:T(8,128)S(1)} collective-permute-done((f32[128,128]{1,0:T(8,128)S(1)}, f32[128,128]{1,0:T(8,128)S(1)}, u32[]{:S(2)}, u32[]{:S(2)}) %collective-permute-start.11) | collective-permute-done | bytes 65568 | tf_op jit(solution)/shard_map/ppermute | solution.py:272
  127.4 11.6 %shard_map.69 = (f32[2,4,64,512]{3,2,1,0:T(8,128)S(1)}, f32[2,4,64,512]{3,2,1,0:T(8,128)}) custom-call(s32[8,9]{1,0:T(8,128)S(1)} %bitcast.102, s32[4]{0:T(128)S(1)} %pad_add_fusion.me_ref, bf16[8,8,256,256]{3,2,1,0:T(8,128)(2,1)} %all-to-all-done.1.tile_ref, bf16[64,4096]{1,0:T(8,128)(2,1)S(1)} %bitcast.98, ...), custom_call_target="tpu_custom_call" | custom-call | tf_op jit(solution)/shard_map/pallas_call | solution.py:92
  144.9 1.9 collective-permute-start.16
  146.8 3.5 %collective-permute-done.12 = f16[4,64,512]{2,1,0:T(8,128)(2,1)} collective-permute-done((f16[4,64,512]{2,1,0:T(8,128)(2,1)}, f16[4,64,512]{2,1,0:T(8,128)(2,1)}, u32[]{:S(2)}, u32[]{:S(2)}) %collective-permute-start.12) | collective-permute-done | bytes 262176 | tf_op jit(solution)/shard_map/ppermute | solution.py:272
  151.4 3.7 %collective-permute-start.15 = (f16[64,512]{1,0:T(8,128)(2,1)S(1)}, f16[64,512]{1,0:T(8,128)(2,1)S(1)}, u32[]{:S(2)}, u32[]{:S(2)}) collective-permute-start(f16[64,512]{1,0:T(8,128)(2,1)S(1)} %get-tuple-element.32), channel_id=1, source_target_pairs={{0,6},{2,4},{4,2},{6,0},{1,7},{3,5},{5,3},{7,1},{8,14},{10,12},{12... | collective-permute-start | bytes 196616 | tf_op jit(solution)/shard_map/ppermute | solution.py:272
  156.0 3.7 %collective-permute-start.19 = (f16[64,512]{1,0:T(8,128)(2,1)S(1)}, f16[64,512]{1,0:T(8,128)(2,1)S(1)}, u32[]{:S(2)}, u32[]{:S(2)}) collective-permute-start(f16[64,512]{1,0:T(8,128)(2,1)S(1)} %get-tuple-element.29), channel_id=1, source_target_pairs={{0,6},{2,4},{4,2},{6,0},{1,7},{3,5},{5,3},{7,1},{8,14},{10,12},{12... | collective-permute-start | bytes 196616 | tf_op jit(solution)/shard_map/ppermute | solution.py:272
  163.2 1.7 collective-permute-done.18
  165.0 6.6 %shard_map.70 = (bf16[128,512]{1,0:T(8,128)(2,1)S(1)}, f32[128,128]{1,0:T(8,128)S(1)}) custom-call(f32[128,512]{1,0:T(8,128)S(1)} %bitcast.100, f32[64,512]{1,0:T(8,128)S(1)} %fusion.33.top_ref, f32[64,512]{1,0:T(8,128)S(1)} %fusion.27.bottom_ref, f32[128,128]{1,0:T(8,128)S(1)} %get-tuple-element.21.gram_ref), custom_call_target="tpu_custom_call" | custom-call | tf_op jit(solution)/shard_map/pallas_call | solution.py:243
  172.2 2.1 collective-permute-start.23
  174.3 1.7 collective-permute-start.25
  176.1 3.3 %collective-permute-done.21.refs_2_ = bf16[128,512]{1,0:T(8,128)(2,1)S(1)} collective-permute-done((bf16[128,512]{1,0:T(8,128)(2,1)S(1)}, bf16[128,512]{1,0:T(8,128)(2,1)S(1)}, u32[]{:S(2)}, u32[]{:S(2)}) %collective-permute-start.21) | collective-permute-done | bytes 131104 | tf_op jit(solution)/shard_map/ppermute | solution.py:272
  179.3 3.3 %collective-permute-done.23.refs_4_ = bf16[128,512]{1,0:T(8,128)(2,1)S(1)} collective-permute-done((bf16[128,512]{1,0:T(8,128)(2,1)S(1)}, bf16[128,512]{1,0:T(8,128)(2,1)S(1)}, u32[]{:S(2)}, u32[]{:S(2)}) %collective-permute-start.23) | collective-permute-done | bytes 131104 | tf_op jit(solution)/shard_map/ppermute | solution.py:272
  185.2 2.4 collective-permute-done.24.refs_5_
  189.2 11.8 %shard_map.72 = (f32[2,4,64,1024]{3,2,1,0:T(8,128)S(1)}, f32[2,4,64,1024]{3,2,1,0:T(8,128)S(1)}, f32[2,4,64,1024]{3,2,1,0:T(8,128)}, f32[2,4,64,1024]{3,2,1,0:T(8,128)}, f32[8,128]{1,0:T(8,128)S(1)}) custom-call(s32[8,9]{1,0:T(8,128)S(1)} %bitcast.103, s32[4]{0:T(128)S(1)} %pad_add_fusion.me_ref, bf16[8,8,256,256]{3,2,1,0:T(8,128)(2,1)} %all-to-all-done.1.tile_ref, ...), custom_call_target="tpu_custom_call" | custom-call | tf_op jit(solution)/shard_map/pallas_call | solution.py:162
  204.3 3.0 %collective-permute-start.39 = (f32[128,128]{1,0:T(8,128)S(1)}, f32[128,128]{1,0:T(8,128)S(1)}, u32[]{:S(2)}, u32[]{:S(2)}) collective-permute-start(f32[128,128]{1,0:T(8,128)S(1)} %get-tuple-element.19), channel_id=1, source_target_pairs={{0,16},{16,0},{1,17},{17,1},{2,18},{18,2},{3,19},{19,3},{4,20},{20... | collective-permute-start | bytes 196616 | tf_op jit(solution)/shard_map/ppermute | solution.py:272
  207.3 3.6 %collective-permute-done.28 = f32[8,128]{1,0:T(8,128)S(1)} collective-permute-done((f32[8,128]{1,0:T(8,128)S(1)}, f32[8,128]{1,0:T(8,128)S(1)}, u32[]{:S(2)}, u32[]{:S(2)}) %collective-permute-start.28) | collective-permute-done | bytes 4128 | tf_op jit(solution)/shard_map/ppermute | solution.py:272
  213.3 2.6 add.167
  218.2 1.9 collective-permute-start.30
  221.3 3.1 %collective-permute-done.41 = f32[128,128]{1,0:T(8,128)S(1)} collective-permute-done((f32[128,128]{1,0:T(8,128)S(1)}, f32[128,128]{1,0:T(8,128)S(1)}, u32[]{:S(2)}, u32[]{:S(2)}) %collective-permute-start.41) | collective-permute-done | bytes 65568 | tf_op jit(solution)/shard_map/ppermute | solution.py:272
  226.1 4.2 %collective-permute-done.42 = f32[128,128]{1,0:T(8,128)S(1)} collective-permute-done((f32[128,128]{1,0:T(8,128)S(1)}, f32[128,128]{1,0:T(8,128)S(1)}, u32[]{:S(2)}, u32[]{:S(2)}) %collective-permute-start.42) | collective-permute-done | bytes 65568 | tf_op jit(solution)/shard_map/ppermute | solution.py:272
  233.8 1.7 collective-permute-done.43
  236.4 2.8 %add.172 = f32[2,4,64,1024]{3,2,1,0:T(8,128)S(1)} add(f32[2,4,64,1024]{3,2,1,0:T(8,128)} %copy-done.2, f32[2,4,64,1024]{3,2,1,0:T(8,128)} %collective-permute-done.34) | non-fusion elementwise | flops 524288 | bytes 6291456 | tf_op jit(solution)/shard_map/add | solution.py:361
  240.9 2.6 collective-permute-start.33
  243.6 1.8 collective-permute-start.31
  245.4 5.0 %collective-permute-done.35 = f16[1,4,64,1024]{3,2,1,0:T(8,128)(2,1)S(1)} collective-permute-done((f16[1,4,64,1024]{3,2,1,0:T(8,128)(2,1)S(1)}, f16[1,4,64,1024]{3,2,1,0:T(8,128)(2,1)S(1)}, u32[]{:S(2)}, u32[]{:S(2)}) %collective-permute-start.35) | collective-permute-done | bytes 524320 | tf_op jit(solution)/shard_map/ppermute | solution.py:272
  250.7 2.6 collective-permute-start.38
  253.3 1.8 collective-permute-start.36
  255.1 4.2 %collective-permute-done.32 = f16[64,1024]{1,0:T(8,128)(2,1)S(1)} collective-permute-done((f16[64,1024]{1,0:T(8,128)(2,1)S(1)}, f16[64,1024]{1,0:T(8,128)(2,1)S(1)}, u32[]{:S(2)}, u32[]{:S(2)}) %collective-permute-start.32) | collective-permute-done | bytes 131104 | tf_op jit(solution)/shard_map/ppermute | solution.py:272
  259.4 4.0 %collective-permute-done.37 = f16[64,1024]{1,0:T(8,128)(2,1)S(1)} collective-permute-done((f16[64,1024]{1,0:T(8,128)(2,1)S(1)}, f16[64,1024]{1,0:T(8,128)(2,1)S(1)}, u32[]{:S(2)}, u32[]{:S(2)}) %collective-permute-start.37) | collective-permute-done | bytes 131104 | tf_op jit(solution)/shard_map/ppermute | solution.py:272
  263.5 8.8 %shard_map.73.refs_0_ = bf16[1024,128]{1,0:T(8,128)(2,1)S(1)} custom-call(f32[128,1024]{1,0:T(8,128)S(1)} %bitcast.99, f32[64,1024]{1,0:T(8,128)S(1)} %fusion.15.top_ref, f32[64,1024]{1,0:T(8,128)S(1)} %fusion.9.bottom_ref, f32[128,128]{1,0:T(8,128)S(1)} %add.181.gram_ref), custom_call_target="tpu_custom_call" | custom-call | tf_op jit(solution)/shard_map/pallas_call | solution.py:262
  272.3 1.8 collective-permute-start.45
  274.1 4.8 %collective-permute-done.45.refs_2_ = bf16[1024,128]{1,0:T(8,128)(2,1)S(1)} collective-permute-done((bf16[1024,128]{1,0:T(8,128)(2,1)S(1)}, bf16[1024,128]{1,0:T(8,128)(2,1)S(1)}, u32[]{:S(2)}, u32[]{:S(2)}) %collective-permute-start.45) | collective-permute-done | bytes 262176 | tf_op jit(solution)/shard_map/ppermute | solution.py:272
  (133 shorter events, 46.6 us)
Async XLA Ops:
  6.4 4.7 %collective-permute-start = (f32[8,128]{1,0:T(8,128)S(1)}, f32[8,128]{1,0:T(8,128)S(1)}, u32[]{:S(2)}, u32[]{:S(2)}) collective-permute-start(f32[8,128]{1,0:T(8,128)S(1)} %broadcast_in_dim.30), channel_id=1, source_target_pairs={{0,2},{2,0},{4,6},{6,4},{1,3},{3,1},{5,7},{7,5},{8,10},{10,8},{12,... | collective-permute-start | bytes 12296 | tf_op jit(solution)/shard_map/ppermute | solution.py:272
  11.1 4.6 %collective-permute-start.1 = (f32[8,128]{1,0:T(8,128)S(1)}, f32[8,128]{1,0:T(8,128)S(1)}, u32[]{:S(2)}, u32[]{:S(2)}) collective-permute-start(f32[8,128]{1,0:T(8,128)S(1)} %broadcast_maximum_fusion), channel_id=1, source_target_pairs={{0,4},{2,6},{4,0},{6,2},{1,5},{3,7},{5,1},{7,3},{8,12},{10,14},{12... | collective-permute-start | bytes 12296 | tf_op jit(solution)/shard_map/ppermute | solution.py:272
  17.5 9.1 %all-to-all-start = ((s32[8,1,9]{2,1,0:T(1,128)}), s32[8,1,9]{2,1,0:T(1,128)S(1)}, u32[]{:S(2)}, u32[]{:S(2)}) async-start(s32[8,1,9]{2,1,0:T(1,128)} %bitcast.7), calls=%async_computation | async-start | bytes 8192 | tf_op jit(solution)/shard_map/all_to_all | solution.py:341
  26.6 100.8 %all-to-all-start.1 = ((bf16[8,8,256,256]{3,2,1,0:T(8,128)(2,1)}), bf16[8,8,256,256]{3,2,1,0:T(8,128)(2,1)}, u32[]{:S(2)}, u32[]{:S(2)}) async-start(bf16[8,8,256,256]{3,2,1,0:T(8,128)(2,1)} %bitcast.104), calls=%async_computation.1 | async-start | bytes 16777216 | tf_op jit(solution)/shard_map/all_to_all | solution.py:327
  34.5 25.2 %collective-permute-start.2 = (bf16[64,4096]{1,0:T(8,128)(2,1)S(1)}, bf16[64,4096]{1,0:T(8,128)(2,1)S(1)}, u32[]{:S(2)}, u32[]{:S(2)}) collective-permute-start(bf16[64,4096]{1,0:T(8,128)(2,1)S(1)} %bitcast.94), channel_id=1, source_target_pairs={{0,2},{2,0},{4,6},{6,4},{1,3},{3,1},{5,7},{7,5},{8,10},{10,8},{12,... | collective-permute-start | bytes 1572872 | tf_op jit(solution)/shard_map/ppermute | solution.py:272
  36.1 38.3 %collective-permute-start.3 = (bf16[64,4096]{1,0:T(8,128)(2,1)S(1)}, bf16[64,4096]{1,0:T(8,128)(2,1)}, u32[]{:S(2)}, u32[]{:S(2)}) collective-permute-start(bf16[64,4096]{1,0:T(8,128)(2,1)S(1)} %bitcast.95), channel_id=1, source_target_pairs={{0,4},{2,6},{4,0},{6,2},{1,5},{3,7},{5,1},{7,3},{8,12},{10,14},{12... | collective-permute-start | bytes 1572872 | tf_op jit(solution)/shard_map/ppermute | solution.py:272
  38.7 35.6 %collective-permute-start.4 = (bf16[64,4096]{1,0:T(8,128)(2,1)S(1)}, bf16[64,4096]{1,0:T(8,128)(2,1)}, u32[]{:S(2)}, u32[]{:S(2)}) collective-permute-start(bf16[64,4096]{1,0:T(8,128)(2,1)S(1)} %bitcast.96), channel_id=1, source_target_pairs={{0,6},{2,4},{4,2},{6,0},{1,7},{3,5},{5,3},{7,1},{8,14},{10,12},{12... | collective-permute-start | bytes 1572872 | tf_op jit(solution)/shard_map/ppermute | solution.py:272
  38.9 88.4 %collective-permute-start.5 = (bf16[64,4096]{1,0:T(8,128)(2,1)S(1)}, bf16[64,4096]{1,0:T(8,128)(2,1)}, u32[]{:S(2)}, u32[]{:S(2)}) collective-permute-start(bf16[64,4096]{1,0:T(8,128)(2,1)S(1)} %bitcast.97), channel_id=1, source_target_pairs={{0,8},{8,0},{1,9},{9,1},{2,10},{10,2},{3,11},{11,3},{4,12},{12,4},... | collective-permute-start | bytes 1572872 | tf_op jit(solution)/shard_map/ppermute | solution.py:272
  59.7 67.6 %collective-permute-start.6 = (bf16[64,4096]{1,0:T(8,128)(2,1)S(1)}, bf16[64,4096]{1,0:T(8,128)(2,1)}, u32[]{:S(2)}, u32[]{:S(2)}) collective-permute-start(bf16[64,4096]{1,0:T(8,128)(2,1)S(1)} %collective-permute-done.2.refs_1_), channel_id=1, source_target_pairs={{0,8},{8,0},{1,9},{9,1},{2,10},{10,2},{3,11},{11,3},{4,12},{12,4},... | collective-permute-start | bytes 1572872 | tf_op jit(solution)/shard_map/ppermute | solution.py:272
  74.4 53.0 %collective-permute-start.7 = (bf16[64,4096]{1,0:T(8,128)(2,1)}, bf16[64,4096]{1,0:T(8,128)(2,1)}, u32[]{:S(2)}, u32[]{:S(2)}) collective-permute-start(bf16[64,4096]{1,0:T(8,128)(2,1)} %collective-permute-done.3.refs_2_), channel_id=1, source_target_pairs={{0,8},{8,0},{1,9},{9,1},{2,10},{10,2},{3,11},{11,3},{4,12},{12,4},... | collective-permute-start | bytes 1572872 | tf_op jit(solution)/shard_map/ppermute | solution.py:272
  74.4 53.0 %collective-permute-start.8 = (bf16[64,4096]{1,0:T(8,128)(2,1)}, bf16[64,4096]{1,0:T(8,128)(2,1)}, u32[]{:S(2)}, u32[]{:S(2)}) collective-permute-start(bf16[64,4096]{1,0:T(8,128)(2,1)} %collective-permute-done.4.refs_3_), channel_id=1, source_target_pairs={{0,8},{8,0},{1,9},{9,1},{2,10},{10,2},{3,11},{11,3},{4,12},{12,4},... | collective-permute-start | bytes 1572872 | tf_op jit(solution)/shard_map/ppermute | solution.py:272
  78.4 13.4 %collective-permute-start.9 = (f32[128,128]{1,0:T(8,128)S(1)}, f32[128,128]{1,0:T(8,128)S(1)}, u32[]{:S(2)}, u32[]{:S(2)}) collective-permute-start(f32[128,128]{1,0:T(8,128)S(1)} %fusion.45), channel_id=1, source_target_pairs={{0,2},{2,0},{4,6},{6,4},{1,3},{3,1},{5,7},{7,5},{8,10},{10,8},{12,... | collective-permute-start | bytes 196616 | tf_op jit(solution)/shard_map/ppermute | solution.py:272
  91.7 6.6 %collective-permute-start.10 = (f32[128,128]{1,0:T(8,128)S(1)}, f32[128,128]{1,0:T(8,128)S(1)}, u32[]{:S(2)}, u32[]{:S(2)}) collective-permute-start(f32[128,128]{1,0:T(8,128)S(1)} %add.154), channel_id=1, source_target_pairs={{0,4},{2,6},{4,0},{6,2},{1,5},{3,7},{5,1},{7,3},{8,12},{10,14},{12... | collective-permute-start | bytes 196616 | tf_op jit(solution)/shard_map/ppermute | solution.py:272
  98.4 27.6 %collective-permute-start.11 = (f32[128,128]{1,0:T(8,128)S(1)}, f32[128,128]{1,0:T(8,128)S(1)}, u32[]{:S(2)}, u32[]{:S(2)}) collective-permute-start(f32[128,128]{1,0:T(8,128)S(1)} %add.155), channel_id=1, source_target_pairs={{0,1},{1,0},{2,3},{3,2},{4,5},{5,4},{6,7},{7,6},{8,9},{9,8},{10,11... | collective-permute-start | bytes 196616 | tf_op jit(solution)/shard_map/ppermute | solution.py:272
  140.8 9.6 %collective-permute-start.12 = (f16[4,64,512]{2,1,0:T(8,128)(2,1)}, f16[4,64,512]{2,1,0:T(8,128)(2,1)}, u32[]{:S(2)}, u32[]{:S(2)}) collective-permute-start(f16[4,64,512]{2,1,0:T(8,128)(2,1)} %fusion.2), channel_id=1, source_target_pairs={{0,1},{1,0},{2,3},{3,2},{4,5},{5,4},{6,7},{7,6},{8,9},{9,8},{10,11... | collective-permute-start | bytes 786440 | tf_op jit(solution)/shard_map/ppermute | solution.py:272
  144.9 11.0 %collective-permute-start.16 = (f16[4,64,512]{2,1,0:T(8,128)(2,1)S(1)}, f16[4,64,512]{2,1,0:T(8,128)(2,1)S(1)}, u32[]{:S(2)}, u32[]{:S(2)}) collective-permute-start(f16[4,64,512]{2,1,0:T(8,128)(2,1)S(1)} %fusion.3), channel_id=1, source_target_pairs={{0,1},{1,0},{2,3},{3,2},{4,5},{5,4},{6,7},{7,6},{8,9},{9,8},{10,11... | collective-permute-start | bytes 786440 | tf_op jit(solution)/shard_map/ppermute | solution.py:272
  151.4 8.3 %collective-permute-start.15 = (f16[64,512]{1,0:T(8,128)(2,1)S(1)}, f16[64,512]{1,0:T(8,128)(2,1)S(1)}, u32[]{:S(2)}, u32[]{:S(2)}) collective-permute-start(f16[64,512]{1,0:T(8,128)(2,1)S(1)} %get-tuple-element.32), channel_id=1, source_target_pairs={{0,6},{2,4},{4,2},{6,0},{1,7},{3,5},{5,3},{7,1},{8,14},{10,12},{12... | collective-permute-start | bytes 196616 | tf_op jit(solution)/shard_map/ppermute | solution.py:272
  155.1 6.3 %collective-permute-start.14 = (f16[64,512]{1,0:T(8,128)(2,1)S(1)}, f16[64,512]{1,0:T(8,128)(2,1)S(1)}, u32[]{:S(2)}, u32[]{:S(2)}) collective-permute-start(f16[64,512]{1,0:T(8,128)(2,1)S(1)} %get-tuple-element.33), channel_id=1, source_target_pairs={{0,4},{2,6},{4,0},{6,2},{1,5},{3,7},{5,1},{7,3},{8,12},{10,14},{12... | collective-permute-start | bytes 196616 | tf_op jit(solution)/shard_map/ppermute | solution.py:272
  155.1 6.3 %collective-permute-start.13 = (f16[64,512]{1,0:T(8,128)(2,1)S(1)}, f16[64,512]{1,0:T(8,128)(2,1)S(1)}, u32[]{:S(2)}, u32[]{:S(2)}) collective-permute-start(f16[64,512]{1,0:T(8,128)(2,1)S(1)} %get-tuple-element.31), channel_id=1, source_target_pairs={{0,2},{2,0},{4,6},{6,4},{1,3},{3,1},{5,7},{7,5},{8,10},{10,8},{12,... | collective-permute-start | bytes 196616 | tf_op jit(solution)/shard_map/ppermute | solution.py:272
  156.0 7.2 %collective-permute-start.19 = (f16[64,512]{1,0:T(8,128)(2,1)S(1)}, f16[64,512]{1,0:T(8,128)(2,1)S(1)}, u32[]{:S(2)}, u32[]{:S(2)}) collective-permute-start(f16[64,512]{1,0:T(8,128)(2,1)S(1)} %get-tuple-element.29), channel_id=1, source_target_pairs={{0,6},{2,4},{4,2},{6,0},{1,7},{3,5},{5,3},{7,1},{8,14},{10,12},{12... | collective-permute-start | bytes 196616 | tf_op jit(solution)/shard_map/ppermute | solution.py:272
  159.7 5.2 %collective-permute-start.18 = (f16[64,512]{1,0:T(8,128)(2,1)S(1)}, f16[64,512]{1,0:T(8,128)(2,1)S(1)}, u32[]{:S(2)}, u32[]{:S(2)}) collective-permute-start(f16[64,512]{1,0:T(8,128)(2,1)S(1)} %get-tuple-element.30), channel_id=1, source_target_pairs={{0,4},{2,6},{4,0},{6,2},{1,5},{3,7},{5,1},{7,3},{8,12},{10,14},{12... | collective-permute-start | bytes 196616 | tf_op jit(solution)/shard_map/ppermute | solution.py:272
  159.7 5.2 %collective-permute-start.17 = (f16[64,512]{1,0:T(8,128)(2,1)S(1)}, f16[64,512]{1,0:T(8,128)(2,1)S(1)}, u32[]{:S(2)}, u32[]{:S(2)}) collective-permute-start(f16[64,512]{1,0:T(8,128)(2,1)S(1)} %get-tuple-element.28), channel_id=1, source_target_pairs={{0,2},{2,0},{4,6},{6,4},{1,3},{3,1},{5,7},{7,5},{8,10},{10,8},{12,... | collective-permute-start | bytes 196616 | tf_op jit(solution)/shard_map/ppermute | solution.py:272
  171.6 7.7 %collective-permute-start.21 = (bf16[128,512]{1,0:T(8,128)(2,1)S(1)}, bf16[128,512]{1,0:T(8,128)(2,1)S(1)}, u32[]{:S(2)}, u32[]{:S(2)}) collective-permute-start(bf16[128,512]{1,0:T(8,128)(2,1)S(1)} %get-tuple-element.13.refs_0_), channel_id=1, source_target_pairs={{0,2},{2,0},{4,6},{6,4},{1,3},{3,1},{5,7},{7,5},{8,10},{10,8},{12,... | collective-permute-start | bytes 393224 | tf_op jit(solution)/shard_map/ppermute | solution.py:272
  172.2 10.5 %collective-permute-start.23 = (bf16[128,512]{1,0:T(8,128)(2,1)S(1)}, bf16[128,512]{1,0:T(8,128)(2,1)S(1)}, u32[]{:S(2)}, u32[]{:S(2)}) collective-permute-start(bf16[128,512]{1,0:T(8,128)(2,1)S(1)} %get-tuple-element.13.refs_0_), channel_id=1, source_target_pairs={{0,4},{2,6},{4,0},{6,2},{1,5},{3,7},{5,1},{7,3},{8,12},{10,14},{12... | collective-permute-start | bytes 393224 | tf_op jit(solution)/shard_map/ppermute | solution.py:272
  174.3 9.9 %collective-permute-start.25 = (bf16[128,512]{1,0:T(8,128)(2,1)S(1)}, bf16[128,512]{1,0:T(8,128)(2,1)S(1)}, u32[]{:S(2)}, u32[]{:S(2)}) collective-permute-start(bf16[128,512]{1,0:T(8,128)(2,1)S(1)} %get-tuple-element.13.refs_0_), channel_id=1, source_target_pairs={{0,6},{2,4},{4,2},{6,0},{1,7},{3,5},{5,3},{7,1},{8,14},{10,12},{12... | collective-permute-start | bytes 393224 | tf_op jit(solution)/shard_map/ppermute | solution.py:272
  176.0 8.7 %collective-permute-start.20 = (bf16[128,512]{1,0:T(8,128)(2,1)S(1)}, bf16[128,512]{1,0:T(8,128)(2,1)S(1)}, u32[]{:S(2)}, u32[]{:S(2)}) collective-permute-start(bf16[128,512]{1,0:T(8,128)(2,1)S(1)} %get-tuple-element.13.refs_0_), channel_id=1, source_target_pairs={{0,1},{1,0},{2,3},{3,2},{4,5},{5,4},{6,7},{7,6},{8,9},{9,8},{10,11... | collective-permute-start | bytes 393224 | tf_op jit(solution)/shard_map/ppermute | solution.py:272
  179.3 5.9 %collective-permute-start.22 = (bf16[128,512]{1,0:T(8,128)(2,1)S(1)}, bf16[128,512]{1,0:T(8,128)(2,1)S(1)}, u32[]{:S(2)}, u32[]{:S(2)}) collective-permute-start(bf16[128,512]{1,0:T(8,128)(2,1)S(1)} %collective-permute-done.21.refs_2_), channel_id=1, source_target_pairs={{0,1},{1,0},{2,3},{3,2},{4,5},{5,4},{6,7},{7,6},{8,9},{9,8},{10,11... | collective-permute-start | bytes 393224 | tf_op jit(solution)/shard_map/ppermute | solution.py:272
  182.7 5.0 %collective-permute-start.24 = (bf16[128,512]{1,0:T(8,128)(2,1)S(1)}, bf16[128,512]{1,0:T(8,128)(2,1)S(1)}, u32[]{:S(2)}, u32[]{:S(2)}) collective-permute-start(bf16[128,512]{1,0:T(8,128)(2,1)S(1)} %collective-permute-done.23.refs_4_), channel_id=1, source_target_pairs={{0,1},{1,0},{2,3},{3,2},{4,5},{5,4},{6,7},{7,6},{8,9},{9,8},{10,11... | collective-permute-start | bytes 393224 | tf_op jit(solution)/shard_map/ppermute | solution.py:272
  184.2 5.0 %collective-permute-start.26 = (bf16[128,512]{1,0:T(8,128)(2,1)S(1)}, bf16[128,512]{1,0:T(8,128)(2,1)S(1)}, u32[]{:S(2)}, u32[]{:S(2)}) collective-permute-start(bf16[128,512]{1,0:T(8,128)(2,1)S(1)} %collective-permute-done.25.refs_6_), channel_id=1, source_target_pairs={{0,1},{1,0},{2,3},{3,2},{4,5},{5,4},{6,7},{7,6},{8,9},{9,8},{10,11... | collective-permute-start | bytes 393224 | tf_op jit(solution)/shard_map/ppermute | solution.py:272
  203.7 9.6 %collective-permute-start.27 = (f32[2,4,64,1024]{3,2,1,0:T(8,128)}, f32[2,4,64,1024]{3,2,1,0:T(8,128)}, u32[]{:S(2)}, u32[]{:S(2)}) collective-permute-start(f32[2,4,64,1024]{3,2,1,0:T(8,128)} %get-tuple-element.15), channel_id=1, source_target_pairs={{0,8},{8,0},{1,9},{9,1},{2,10},{10,2},{3,11},{11,3},{4,12},{12,4},... | collective-permute-start | bytes 6291464 | tf_op jit(solution)/shard_map/ppermute | solution.py:272
  203.8 32.7 %collective-permute-start.34 = (f32[2,4,64,1024]{3,2,1,0:T(8,128)}, f32[2,4,64,1024]{3,2,1,0:T(8,128)}, u32[]{:S(2)}, u32[]{:S(2)}) collective-permute-start(f32[2,4,64,1024]{3,2,1,0:T(8,128)} %get-tuple-element.18), channel_id=1, source_target_pairs={{0,8},{8,0},{1,9},{9,1},{2,10},{10,2},{3,11},{11,3},{4,12},{12,4},... | collective-permute-start | bytes 6291464 | tf_op jit(solution)/shard_map/ppermute | solution.py:272
  204.3 6.6 %collective-permute-start.39 = (f32[128,128]{1,0:T(8,128)S(1)}, f32[128,128]{1,0:T(8,128)S(1)}, u32[]{:S(2)}, u32[]{:S(2)}) collective-permute-start(f32[128,128]{1,0:T(8,128)S(1)} %get-tuple-element.19), channel_id=1, source_target_pairs={{0,16},{16,0},{1,17},{17,1},{2,18},{18,2},{3,19},{19,3},{4,20},{20... | collective-permute-start | bytes 196616 | tf_op jit(solution)/shard_map/ppermute | solution.py:272
  207.3 3.6 %collective-permute-start.28 = (f32[8,128]{1,0:T(8,128)S(1)}, f32[8,128]{1,0:T(8,128)S(1)}, u32[]{:S(2)}, u32[]{:S(2)}) collective-permute-start(f32[8,128]{1,0:T(8,128)S(1)} %get-tuple-element.16), channel_id=1, source_target_pairs={{0,16},{16,0},{1,17},{17,1},{2,18},{18,2},{3,19},{19,3},{4,20},{20... | collective-permute-start | bytes 12296 | tf_op jit(solution)/shard_map/ppermute | solution.py:272
  210.9 9.1 %collective-permute-start.40 = (f32[128,128]{1,0:T(8,128)S(1)}, f32[128,128]{1,0:T(8,128)S(1)}, u32[]{:S(2)}, u32[]{:S(2)}) collective-permute-start(f32[128,128]{1,0:T(8,128)S(1)} %add.177), channel_id=1, source_target_pairs={{0,8},{8,0},{1,9},{9,1},{2,10},{10,2},{3,11},{11,3},{4,12},{12,4},... | collective-permute-start | bytes 196616 | tf_op jit(solution)/shard_map/ppermute | solution.py:272
  218.2 21.5 %collective-permute-start.30 = (f16[1,4,64,1024]{3,2,1,0:T(8,128)(2,1)}, f16[1,4,64,1024]{3,2,1,0:T(8,128)(2,1)}, u32[]{:S(2)}, u32[]{:S(2)}) collective-permute-start(f16[1,4,64,1024]{3,2,1,0:T(8,128)(2,1)} %fusion.1), channel_id=1, source_target_pairs={{0,16},{16,0},{1,17},{17,1},{2,18},{18,2},{3,19},{19,3},{4,20},{20... | collective-permute-start | bytes 1572872 | tf_op jit(solution)/shard_map/ppermute | solution.py:272
  220.1 4.3 %collective-permute-start.41 = (f32[128,128]{1,0:T(8,128)S(1)}, f32[128,128]{1,0:T(8,128)S(1)}, u32[]{:S(2)}, u32[]{:S(2)}) collective-permute-start(f32[128,128]{1,0:T(8,128)S(1)} %add.178), channel_id=1, source_target_pairs={{0,2},{2,0},{4,6},{6,4},{1,3},{3,1},{5,7},{7,5},{8,10},{10,8},{12,... | collective-permute-start | bytes 196616 | tf_op jit(solution)/shard_map/ppermute | solution.py:272
  224.4 5.9 %collective-permute-start.42 = (f32[128,128]{1,0:T(8,128)S(1)}, f32[128,128]{1,0:T(8,128)S(1)}, u32[]{:S(2)}, u32[]{:S(2)}) collective-permute-start(f32[128,128]{1,0:T(8,128)S(1)} %add.179), channel_id=1, source_target_pairs={{0,4},{2,6},{4,0},{6,2},{1,5},{3,7},{5,1},{7,3},{8,12},{10,14},{12... | collective-permute-start | bytes 196616 | tf_op jit(solution)/shard_map/ppermute | solution.py:272
  231.0 4.6 %collective-permute-start.43 = (f32[128,128]{1,0:T(8,128)}, f32[128,128]{1,0:T(8,128)}, u32[]{:S(2)}, u32[]{:S(2)}) collective-permute-start(f32[128,128]{1,0:T(8,128)} %add.180), channel_id=1, source_target_pairs={{0,1},{1,0},{2,3},{3,2},{4,5},{5,4},{6,7},{7,6},{8,9},{9,8},{10,11... | collective-permute-start | bytes 196616 | tf_op jit(solution)/shard_map/ppermute | solution.py:272
  239.4 11.0 %collective-permute-start.35 = (f16[1,4,64,1024]{3,2,1,0:T(8,128)(2,1)S(1)}, f16[1,4,64,1024]{3,2,1,0:T(8,128)(2,1)S(1)}, u32[]{:S(2)}, u32[]{:S(2)}) collective-permute-start(f16[1,4,64,1024]{3,2,1,0:T(8,128)(2,1)S(1)} %fusion), channel_id=1, source_target_pairs={{0,16},{16,0},{1,17},{17,1},{2,18},{18,2},{3,19},{19,3},{4,20},{20... | collective-permute-start | bytes 1572872 | tf_op jit(solution)/shard_map/ppermute | solution.py:272
  240.9 12.4 %collective-permute-start.33 = (f16[64,1024]{1,0:T(8,128)(2,1)S(1)}, f16[64,1024]{1,0:T(8,128)(2,1)S(1)}, u32[]{:S(2)}, u32[]{:S(2)}) collective-permute-start(f16[64,1024]{1,0:T(8,128)(2,1)S(1)} %get-tuple-element.26), channel_id=1, source_target_pairs={{0,6},{2,4},{4,2},{6,0},{1,7},{3,5},{5,3},{7,1},{8,14},{10,12},{12... | collective-permute-start | bytes 393224 | tf_op jit(solution)/shard_map/ppermute | solution.py:272
  243.5 15.8 %collective-permute-start.32 = (f16[64,1024]{1,0:T(8,128)(2,1)S(1)}, f16[64,1024]{1,0:T(8,128)(2,1)S(1)}, u32[]{:S(2)}, u32[]{:S(2)}) collective-permute-start(f16[64,1024]{1,0:T(8,128)(2,1)S(1)} %get-tuple-element.27), channel_id=1, source_target_pairs={{0,4},{2,6},{4,0},{6,2},{1,5},{3,7},{5,1},{7,3},{8,12},{10,14},{12... | collective-permute-start | bytes 393224 | tf_op jit(solution)/shard_map/ppermute | solution.py:272
  243.6 15.8 %collective-permute-start.31 = (f16[64,1024]{1,0:T(8,128)(2,1)S(1)}, f16[64,1024]{1,0:T(8,128)(2,1)S(1)}, u32[]{:S(2)}, u32[]{:S(2)}) collective-permute-start(f16[64,1024]{1,0:T(8,128)(2,1)S(1)} %get-tuple-element.25), channel_id=1, source_target_pairs={{0,2},{2,0},{4,6},{6,4},{1,3},{3,1},{5,7},{7,5},{8,10},{10,8},{12,... | collective-permute-start | bytes 393224 | tf_op jit(solution)/shard_map/ppermute | solution.py:272
  250.7 8.7 %collective-permute-start.38 = (f16[64,1024]{1,0:T(8,128)(2,1)S(1)}, f16[64,1024]{1,0:T(8,128)(2,1)S(1)}, u32[]{:S(2)}, u32[]{:S(2)}) collective-permute-start(f16[64,1024]{1,0:T(8,128)(2,1)S(1)} %get-tuple-element.23), channel_id=1, source_target_pairs={{0,6},{2,4},{4,2},{6,0},{1,7},{3,5},{5,3},{7,1},{8,14},{10,12},{12... | collective-permute-start | bytes 393224 | tf_op jit(solution)/shard_map/ppermute | solution.py:272
  253.3 10.1 %collective-permute-start.37 = (f16[64,1024]{1,0:T(8,128)(2,1)S(1)}, f16[64,1024]{1,0:T(8,128)(2,1)S(1)}, u32[]{:S(2)}, u32[]{:S(2)}) collective-permute-start(f16[64,1024]{1,0:T(8,128)(2,1)S(1)} %get-tuple-element.24), channel_id=1, source_target_pairs={{0,4},{2,6},{4,0},{6,2},{1,5},{3,7},{5,1},{7,3},{8,12},{10,14},{12... | collective-permute-start | bytes 393224 | tf_op jit(solution)/shard_map/ppermute | solution.py:272
  253.3 10.1 %collective-permute-start.36 = (f16[64,1024]{1,0:T(8,128)(2,1)S(1)}, f16[64,1024]{1,0:T(8,128)(2,1)S(1)}, u32[]{:S(2)}, u32[]{:S(2)}) collective-permute-start(f16[64,1024]{1,0:T(8,128)(2,1)S(1)} %get-tuple-element.22), channel_id=1, source_target_pairs={{0,2},{2,0},{4,6},{6,4},{1,3},{3,1},{5,7},{7,5},{8,10},{10,8},{12,... | collective-permute-start | bytes 393224 | tf_op jit(solution)/shard_map/ppermute | solution.py:272
  272.3 6.6 %collective-permute-start.45 = (bf16[1024,128]{1,0:T(8,128)(2,1)S(1)}, bf16[1024,128]{1,0:T(8,128)(2,1)S(1)}, u32[]{:S(2)}, u32[]{:S(2)}) collective-permute-start(bf16[1024,128]{1,0:T(8,128)(2,1)S(1)} %shard_map.73.refs_0_), channel_id=1, source_target_pairs={{0,16},{16,0},{1,17},{17,1},{2,18},{18,2},{3,19},{19,3},{4,20},{20... | collective-permute-start | bytes 786440 | tf_op jit(solution)/shard_map/ppermute | solution.py:272
  274.1 6.5 %collective-permute-start.44 = (bf16[1024,128]{1,0:T(8,128)(2,1)S(1)}, bf16[1024,128]{1,0:T(8,128)(2,1)S(1)}, u32[]{:S(2)}, u32[]{:S(2)}) collective-permute-start(bf16[1024,128]{1,0:T(8,128)(2,1)S(1)} %shard_map.73.refs_0_), channel_id=1, source_target_pairs={{0,8},{8,0},{1,9},{9,1},{2,10},{10,2},{3,11},{11,3},{4,12},{12,4},... | collective-permute-start | bytes 786440 | tf_op jit(solution)/shard_map/ppermute | solution.py:272
  279.0 1.7 collective-permute-start.46
  (14 other events, 122.3 us)

commit v3 on v2

v3 whole, which is shorter than its diff:
```python
import jax
import jax.numpy as jnp
from jax import lax
from jax.experimental import pallas as pl
from jax.experimental.pallas import tpu as pltpu
from jax.sharding import Mesh
from jax.sharding import PartitionSpec as P

CT = 16
CAP = 2
EPS = 1e-06
RIDGE = 1.0
HIGH = lax.Precision.HIGHEST
F32 = jnp.float32
LINK = jnp.float16
STEP = 32
BATCH = 2
PEAK = 256.0
VMEM_LIMIT = 48 * 2**20


def params():
    return pltpu.CompilerParams(vmem_limit_bytes=VMEM_LIMIT)


def pack(slot, tile_data, notes, held):
    count, size = tile_data.shape[0], tile_data.shape[1]
    peers, extra = notes.shape[0], notes.shape[1]

    def kernel(slot_ref, tiles_ref, notes_ref, out_ref, sems):
        copies = []
        for s in range(count):
            rows = pl.ds(pl.multiple_of((slot_ref[s] % held) * size, size), size)
            dest = out_ref.at[slot_ref[s] // held, rows]
            copies.append(pltpu.make_async_copy(tiles_ref.at[s], dest, sems.at[s]))
        dest = out_ref.at[:, pl.ds(held * size, extra)]
        copies.append(pltpu.make_async_copy(notes_ref, dest, sems.at[count]))
        for copy in copies:
            copy.start()
        for copy in copies:
            copy.wait()

    return pl.pallas_call(
        kernel,
        out_shape=jax.ShapeDtypeStruct((peers, held * size + extra, size), tile_data.dtype),
        in_specs=[
            pl.BlockSpec(memory_space=pltpu.SMEM),
            pl.BlockSpec(memory_space=pl.ANY),
            pl.BlockSpec(memory_space=pltpu.VMEM),
        ],
        out_specs=pl.BlockSpec(memory_space=pl.ANY),
        scratch_shapes=[pltpu.SemaphoreType.DMA((count + 1,))],
        compiler_params=params(),
    )(slot, tile_data, notes)


def row_products(inbox, meta, me, pieces, his, los, width):
    senders, size = inbox.shape[0], inbox.shape[2]
    held = meta.shape[1]
    part, length = pieces[0].shape
    rank = 2 * part
    per_chunk = width // size

    def kernel(meta_ref, me_ref, tile_ref, *refs):
        piece_refs, (top_ref, bot_ref), (panel_ref, term_ref) = refs[: 2 * his], refs[-4:-2], refs[-2:]
        step = pl.program_id(0)
        my_core, my_hi, my_lo = me_ref[1], me_ref[2], me_ref[3]

        @pl.when(step == 0)
        def _():
            top_ref[...] = jnp.zeros_like(top_ref)
            bot_ref[...] = jnp.zeros_like(bot_ref)
            for side in range(2):
                rows = pl.ds(pl.multiple_of((my_core ^ side) * part, part), part)
                for j in range(his):
                    panel_ref[j, rows, :] = piece_refs[side * his + j][...]

        for item in range(BATCH * held):
            sub, slot = item // held, item % held
            spot = jnp.maximum(meta_ref[step * BATCH + sub, slot] - 1, 0)
            place = pl.ds(pl.multiple_of((spot % CT) * size, size), size)
            term_ref[item] = lax.dot_general(
                panel_ref[slot // CAP ^ my_hi, :, place],
                tile_ref[sub, slot * size : (slot + 1) * size],
                (((1,), (1,)), ((), ())),
                preferred_element_type=F32,
            )

        for item in range(BATCH * held):
            sub, slot = item // held, item % held
            spot = meta_ref[step * BATCH + sub, slot] - 1

            @pl.when(spot >= 0)
            def _():
                trow = spot // CT
                chunk = trow // per_chunk
                lanes = pl.ds(pl.multiple_of((trow % per_chunk) * size, size), size)
                at = (chunk % los ^ my_lo, chunk // los ^ my_hi)
                top_ref[at[0], at[1], :, lanes] += term_ref[item, :part]
                bot_ref[at[0], at[1], :, lanes] += term_ref[item, part:]

    shape = (los, his, part, width)
    piece_spec = pl.BlockSpec((part, length), lambda i, *_: (0, 0))
    out_spec = pl.BlockSpec(shape, lambda i, *_: (0, 0, 0, 0))
    return pl.pallas_call(
        kernel,
        out_shape=[jax.ShapeDtypeStruct(shape, F32)] * 2,
        grid_spec=pltpu.PrefetchScalarGridSpec(
            num_scalar_prefetch=2,
            grid=(senders // BATCH,),
            in_specs=[pl.BlockSpec((BATCH, inbox.shape[1], size), lambda i, *_: (i, 0, 0))]
            + [piece_spec] * (2 * his),
            out_specs=[out_spec] * 2,
            scratch_shapes=[
                pltpu.VMEM((his, rank, length), jnp.bfloat16),
                pltpu.VMEM((BATCH * held, rank, size), F32),
            ],
        ),
        compiler_params=params(),
    )(meta, me, inbox, *pieces)


def column_products(inbox, meta, me, pieces, his, los, fars, out_width):
    senders, size = inbox.shape[0], inbox.shape[2]
    held = meta.shape[1]
    rank, width = pieces[0].shape
    part = rank // 2
    per_chunk, per_out = width // size, out_width // size
    chunks = his * los

    def kernel(meta_ref, me_ref, tile_ref, *refs):
        piece_refs, outs, gram_ref = refs[:chunks], refs[chunks : chunks + 4], refs[chunks + 4]
        panel_ref, term_ref = refs[-2:]
        keeps, sends = outs[:2], outs[2:]
        step = pl.program_id(0)
        my_far, my_core, my_hi, my_lo = (me_ref[i] for i in range(4))

        @pl.when(step == 0)
        def _():
            for out in outs:
                out[...] = jnp.zeros_like(out)
            gram = jnp.zeros((rank, rank), F32)
            for j in range(chunks):
                piece = piece_refs[j][...]
                panel_ref[j] = piece
                gram += lax.dot_general(
                    piece, piece, (((1,), (1,)), ((), ())), preferred_element_type=F32
                )
            gram_ref[...] = gram

        for item in range(BATCH * held):
            sub, slot = item // held, item % held
            spot = jnp.maximum(meta_ref[step * BATCH + sub, slot] - 1, 0)
            trow = spot // CT
            chunk = trow // per_chunk
            lanes = pl.ds(pl.multiple_of((trow % per_chunk) * size, size), size)
            at = (chunk // los ^ my_hi) * los + (chunk % los ^ my_lo)
            term_ref[item] = lax.dot_general(
                panel_ref[at, :, lanes],
                tile_ref[sub, slot * size : (slot + 1) * size],
                (((1,), (0,)), ((), ())),
                preferred_element_type=F32,
            )

        for item in range(BATCH * held):
            sub, slot = item // held, item % held
            spot = meta_ref[step * BATCH + sub, slot] - 1
            tcol = spot % CT
            owner = tcol // per_out
            place = pl.ds(pl.multiple_of((tcol % per_out) * size, size), size)
            at = (owner // 2 ^ my_far, slot // CAP ^ my_hi)
            for side, dests in enumerate((keeps, sends)):

                @pl.when((spot >= 0) & ((owner ^ my_core) % 2 == side))
                def _():
                    dests[0][at[0], at[1], :, place] += term_ref[item, :part]
                    dests[1][at[0], at[1], :, place] += term_ref[item, part:]

    shape = (fars, his, part, out_width)
    out_spec = pl.BlockSpec(shape, lambda i, *_: (0, 0, 0, 0))
    return pl.pallas_call(
        kernel,
        out_shape=[jax.ShapeDtypeStruct(shape, F32)] * 4
        + [jax.ShapeDtypeStruct((rank, rank), F32)],
        grid_spec=pltpu.PrefetchScalarGridSpec(
            num_scalar_prefetch=2,
            grid=(senders // BATCH,),
            in_specs=[pl.BlockSpec((BATCH, inbox.shape[1], size), lambda i, *_: (i, 0, 0))]
            + [pl.BlockSpec((rank, width), lambda i, *_: (0, 0))] * chunks,
            out_specs=[out_spec] * 4 + [pl.BlockSpec((rank, rank), lambda i, *_: (0, 0))],
            scratch_shapes=[
                pltpu.VMEM((chunks, rank, width), jnp.bfloat16),
                pltpu.VMEM((BATCH * held, rank, size), F32),
            ],
        ),
        compiler_params=params(),
    )(meta, me, inbox, *pieces)


def assemble(pieces, place, turned):
    count = len(pieces)
    rank, width = pieces[0].shape if turned else pieces[0].shape[::-1]

    def kernel(place_ref, *refs):
        for j in range(count):
            piece = refs[j][...].astype(F32)
            refs[count][j ^ place_ref[0]] = jnp.transpose(piece) if turned else piece

    return pl.pallas_call(
        kernel,
        out_shape=jax.ShapeDtypeStruct((count, width, rank), F32),
        in_specs=[pl.BlockSpec(memory_space=pltpu.SMEM)]
        + [pl.BlockSpec(memory_space=pltpu.VMEM)] * count,
        out_specs=pl.BlockSpec(memory_space=pltpu.VMEM),
        compiler_params=params(),
    )(place, *pieces).reshape(count * width, rank)


def prepare(factor, gram):
    rank, width = factor.shape

    def kernel(factor_ref, gram_ref, part_ref, mixed_ref, over_ref):
        gram = gram_ref[...]
        shape = (rank, rank)
        diag = lax.broadcasted_iota(jnp.int32, shape, 0) == lax.broadcasted_iota(jnp.int32, shape, 1)
        over = 1.0 / (jnp.sum(jnp.where(diag, gram, 0.0), axis=1, keepdims=True) + RIDGE)
        mixed = gram * over
        mixed_ref[...] = mixed
        over_ref[...] = jnp.broadcast_to(over, shape)
        part_ref[...] = jnp.dot(
            jnp.where(diag, 0.0, mixed), factor_ref[...], precision=HIGH, preferred_element_type=F32
        )

    return pl.pallas_call(
        kernel,
        out_shape=[
            jax.ShapeDtypeStruct((rank, width), F32),
            jax.ShapeDtypeStruct((rank, rank), F32),
            jax.ShapeDtypeStruct((rank, rank), F32),
        ],
        compiler_params=params(),
    )(factor, gram)


def sweep_block(factor, top, bottom, part, mixed, over):
    rank, half = factor.shape[0], factor.shape[0] // 2
    over = over[:, :1]
    ahead = []
    for lead in range(0, rank, STEP):
        product = top[lead : lead + STEP] if lead < half else bottom[lead - half : lead - half + STEP]
        ahead.append(product * over[lead : lead + STEP] - part[lead : lead + STEP])
    outs = []
    for b in range(rank // STEP):
        here = slice(b * STEP, (b + 1) * STEP)
        before, block, left = factor[here], mixed[here, here], ahead[b]
        news, moves = [], []
        for k in range(STEP):
            new = jnp.maximum(left[k : k + 1], EPS)
            move = new - before[k : k + 1]
            news.append(new)
            moves.append(move)
            if k + 1 < STEP:
                left = left - block[:, k : k + 1] * move
        outs.append(jnp.concatenate(news, axis=0))
        moved = jnp.concatenate(moves, axis=0)
        for c in range(b + 1, rank // STEP):
            ahead[c] -= jnp.dot(
                mixed[c * STEP : (c + 1) * STEP, here], moved, precision=HIGH, preferred_element_type=F32
            )
    return jnp.concatenate(outs, axis=0)


def sweep(factor, top, bottom, prepared, turned):
    rank, width = factor.shape

    def kernel(*refs):
        new = sweep_block(*(ref[...] for ref in refs[:-1]))
        refs[-1][...] = (jnp.transpose(new) if turned else new).astype(jnp.bfloat16)

    shape = (width, rank) if turned else (rank, width)
    return pl.pallas_call(
        kernel, out_shape=jax.ShapeDtypeStruct(shape, jnp.bfloat16), compiler_params=params()
    )(factor, top, bottom, *prepared)


def swap(x, axis, bit):
    size = lax.axis_size(axis)
    return lax.ppermute(x, axis, [(i, i ^ bit) for i in range(size)])


def bits(axis):
    bit = 1
    while bit < lax.axis_size(axis):
        yield bit
        bit *= 2


def everywhere(x, axes, combine):
    for axis in axes:
        for bit in bits(axis):
            x = combine(x, swap(x, axis, bit))
    return x


def spread(pieces, axis):
    return [
        piece if j == 0 else swap(piece, axis, j)
        for piece in pieces
        for j in range(lax.axis_size(axis))
    ]


def pull(total, sums, axis, up, down):
    for j in range(1, lax.axis_size(axis)):
        total = total + swap((sums[j - 1] * up).astype(LINK), axis, j).astype(F32) * down
    return total


def gather(sums, axis, up, down):
    return pull(sums[0], sums[1:], axis, up, down)


def scales(gram, terms, size):
    rank = gram.shape[0]
    norm = jnp.sqrt(jnp.maximum(jnp.sum(gram * jnp.eye(rank, dtype=F32), axis=1, keepdims=True), 1e-24))
    down = norm * (terms * PEAK * size**0.5 / 32768.0)
    half = rank // 2
    return [(1.0 / d, d) for d in (down[:half], down[half:])]


def local(tile_data, owner_ids, tile_spot, w_init, h_init):
    row_axes, col_axes = ("far", "core"), ("hi", "lo")
    fars, cores = lax.axis_size("far"), lax.axis_size("core")
    his, los = lax.axis_size("hi"), lax.axis_size("lo")
    rows, cols = fars * cores, his * los
    slots = rows * cols * CAP
    size, rank = tile_data.shape[1], w_init.shape[1]
    width, length = w_init.shape[0] // cols, h_init.shape[0] // rows
    my_row, my_col = lax.axis_index(row_axes), lax.axis_index(col_axes)
    core = lax.axis_index("core")
    me = jnp.stack([lax.axis_index(a) for a in row_axes + col_axes]).astype(jnp.int32)

    owner = owner_ids[:, 0]
    count = owner.shape[0]
    same = owner[:, None] == owner[None, :]
    earlier = jnp.arange(count)[None, :] < jnp.arange(count)[:, None]
    nth = jnp.sum((same & earlier).astype(jnp.int32), axis=1)
    o_row, o_col = owner // cols, owner % cols
    slot = ((o_row * los + o_col % los) * his + o_col // los) * CAP + nth

    plane = ("far", "core", "lo")
    peers, held = rows * los, his * CAP
    marks = slot[:, None] == jnp.arange(slots, dtype=jnp.int32)[None, :]
    meta = jnp.sum(jnp.where(marks, tile_spot[:, None] + 1, 0), axis=0).reshape(peers, held)
    notes = jnp.broadcast_to(meta.astype(tile_data.dtype)[:, None, :], (peers, 16, held))
    notes = jnp.pad(notes, ((0, 0), (0, 0), (0, size - held)))
    outbox = pack(slot, tile_data, notes, held)
    outbox, h_init = lax.optimization_barrier((outbox, h_init))
    inbox = lax.all_to_all(outbox, plane, split_axis=0, concat_axis=0, tiled=True)
    meta = inbox[:, held * size, :held].astype(F32).astype(jnp.int32)

    h_t = h_init.T
    piece = lax.dynamic_slice_in_dim(h_t, core * (rank // 2), rank // 2, 0).astype(jnp.bfloat16)
    pieces = spread([piece], "hi")
    pieces += [swap(piece, "core", 1) for piece in pieces]

    gram_h = lax.dot_general(h_t, h_t, (((1,), (1,)), ((), ())), precision=HIGH)
    gram_h = everywhere(gram_h, col_axes, jnp.add)
    w_t = lax.dynamic_slice_in_dim(w_init, my_col * width, width, 0).T
    prepared = prepare(w_t, gram_h)
    parts = row_products(inbox, meta, me, pieces, his, los, width)
    sums = []
    for part, scale in zip(parts, scales(gram_h, slots * los, size)):
        sums.append(gather(gather(part, "lo", *scale), "hi", *scale))
    w_low = sweep(w_t, *sums, prepared, False)
    pieces = spread(spread([w_low], "hi"), "lo")

    *parts, gram_w = column_products(inbox, meta, me, pieces, his, los, fars, length)
    gram_w = everywhere(gram_w, row_axes, jnp.add)
    w_new = assemble(pieces, my_col[None].astype(jnp.int32), True)
    own_t = lax.dynamic_slice_in_dim(h_init, my_row * length, length, 0).T
    prepared = prepare(own_t, gram_w)
    sums = []
    for keep, send, scale in zip(parts[:2], parts[2:], scales(gram_w, slots * rows, size)):
        keep = keep + swap(send, "core", 1)
        half = fars // 2
        while half:
            up, down = scale
            away = swap((keep[half:] * up).astype(LINK), "far", half)
            keep = keep[:half] + away.astype(F32) * down
            half //= 2
        sums.append(gather(keep[0], "hi", *scale))
    h_low = sweep(own_t, *sums, prepared, True)
    h_new = assemble(spread(spread([h_low], "far"), "core"), my_row[None].astype(jnp.int32), False)
    return w_new, h_new


def solution(mesh):
    rows, cols = mesh.shape["row"], mesh.shape["col"]
    his = 4 if cols % 4 == 0 else 1
    shape = (rows // 2, 2, his, cols // his)
    fine = Mesh(mesh.devices.reshape(shape), ("far", "core", "hi", "lo"))
    row, col = ("far", "core"), ("hi", "lo")
    in_specs = (P(row + col, None, None), P(row + col, None), P(row + col), P(row, None), P(col, None))
    out_specs = (P(row, None), P(col, None))
    return jax.shard_map(local, mesh=fine, in_specs=in_specs, out_specs=out_specs, check_vma=False)
```

time: 283 us -> 250 us (0.88)
  starting transfers between devices: 73.3 us -> 50.4 us
  waiting for transfers between devices: 119 us -> 137 us
  Pallas kernels: 44.8 us -> 31.3 us
  local copies, waits for them, and re-layouts: 17.4 us -> 9.98 us
  other arithmetic: 19.8 us -> 14.1 us
  between operations: 4.53 us -> 0.98 us
    ppermute x47 -> x40, starting transfers between devices: 64.3 us -> 45.3 us  [swap(): return lax.ppermute(x, axis, [(i, i ^ bit) for i in range(size)])]
    ppermute x47 -> x40, waiting for transfers between devices: 119 us -> 137 us  [swap(): return lax.ppermute(x, axis, [(i, i ^ bit) for i in range(size)])]
    pallas_call x3 -> x5, Pallas kernels: 18.2 us -> 7.56 us  [the longest x2 3.61 us: sweep(): pl.pallas_call(kernel, out_shape=jax.ShapeDtypeStruct(shape, jnp.bfloat16...]
    unnamed x29 -> x15, local copies, waits for them, and re-layouts: 11.1 us -> 4.61 us
    reduce_max x3 -> x0, other arithmetic: 6.41 us -> none  [the longest x1 5.1 us: local(): jnp.max(tile_data).astype(F32)]
    all_to_all x1 -> x0, starting transfers between devices: 4.06 us -> none  [local(): meta = lax.all_to_all(meta, plane, split_axis=0, concat_axis=0, tiled=True)]
    optimization_barrier x0 -> x1, local copies, waits for them, and re-layouts: none -> 2.88 us  [local(): outbox, h_init = lax.optimization_barrier((outbox, h_init))]
  transfers between devices with their start and end apart: 49 -> 41, of which waited for: 25 -> 21; matrix products, arithmetic and copies ran while one was open for 9% -> 8% of each run, Pallas kernels for 2% -> 1%
where the time goes in v3:
time: 250 us; the launch traced here: 249 us
  waiting for transfers between devices  137 us (55%)
  starting transfers between devices  50.4 us (20%)
  Pallas kernels  31.3 us (13%)
  other arithmetic  14.1 us (6%)
  local copies, waits for them, and re-layouts  9.98 us (4%)
  matrix products  5.66 us (2%)
    ppermute x40, waiting for transfers between devices, swap(): return lax.ppermute(x, axis, [(i, i ^ bit) for i in range(size)])  137 us
    ppermute x40, starting transfers between devices, swap(): return lax.ppermute(x, axis, [(i, i ^ bit) for i in range(size)])  45.3 us
    pallas_call x1, Pallas kernels, column_products(): pl.pallas_call(kernel, out_shape=[jax.ShapeDtypeStruct(shape, F32)] * 4 +...  10.5 us
    pallas_call x1, Pallas kernels, row_products(): pl.pallas_call(kernel, out_shape=[jax.ShapeDtypeStruct(shape, F32)] * 2,...  10.2 us
    dot_general x1, matrix products, local(): gram_h = lax.dot_general(h_t, h_t, (((1,), (1,)), ((), ())), precision=HIGH)  5.66 us
    all_to_all x1, starting transfers between devices, local(): lax.all_to_all(outbox, plane, split_axis=0, concat_axis=0, tiled=True)  5.15 us
  transfers between devices with their start and end apart: 41, of which 21 were waited for; matrix products, arithmetic and copies ran while one was open for 8% of the time, Pallas kernels for 1%

profile of v3, /device:TPU:0, one launch (start us, length us, event | category | flops | bytes accessed | tf_op | source)
XLA Modules:
  0.0 249.1 jit_solution(13962644733093403153)
XLA Ops:
  3.9 2.2 copy-done.2
  6.1 2.9 %shard_map.68 = bf16[8,2064,256]{2,1,0:T(8,128)(2,1)} custom-call(s32[32]{0:T(128)S(1)} %multiply_add_fusion.slot_ref, bf16[32,256,256]{2,1,0:T(8,128)(2,1)S(1)} %copy-done.2, bf16[8,16,256]{2,1,0:T(8,128)(2,1)S(1)} %pad.4.notes_ref), custom_call_target="tpu_custom_call" | custom-call | tf_op jit(solution)/shard_map/pallas_call | solution.py:43
  9.0 5.2 %all-to-all-start = ((bf16[8,2064,256]{2,1,0:T(8,128)(2,1)}), bf16[8,2064,256]{2,1,0:T(8,128)(2,1)}, u32[]{:S(2)}, u32[]{:S(2)}) async-start(bf16[8,2064,256]{2,1,0:T(8,128)(2,1)} %shard_map.68), calls=%async_computation | async-start | bytes 16908288 | tf_op jit(solution)/shard_map/all_to_all | solution.py:359
  14.1 2.9 %copy.13 = f32[4096,128]{0,1:T(8,128)} copy(f32[4096,128]{1,0:T(8,128)} %param.9) | data formatting | bytes 4194304 | tf_op jit(solution)/shard_map/optimization_barrier | solution.py:358
  18.3 5.0 %collective-permute-start.2 = (bf16[64,4096]{1,0:T(8,128)(2,1)S(1)}, bf16[64,4096]{1,0:T(8,128)(2,1)S(1)}, u32[]{:S(2)}, u32[]{:S(2)}) collective-permute-start(bf16[64,4096]{1,0:T(8,128)(2,1)S(1)} %fusion.2.refs_0_), channel_id=1, source_target_pairs={{0,6},{2,4},{4,2},{6,0},{1,7},{3,5},{5,3},{7,1},{8,14},{10,12},{12... | collective-permute-start | bytes 1572872 | tf_op jit(solution)/shard_map/ppermute | solution.py:288
  23.9 5.7 %fusion.48 = f32[128,128]{1,0:T(8,128)S(1)} fusion(f32[4096,128]{1,0:T(8,128)} %param.9), kind=kOutput, calls=%fused_computation.113 | convolution fusion | flops 805306368 | bytes 2162688 | tf_op jit(solution)/shard_map/dot_general | solution.py:367
  29.6 1.5 collective-permute-start.7
  31.0 27.9 %collective-permute-done.7 = f32[128,128]{1,0:T(8,128)S(1)} collective-permute-done((f32[128,128]{1,0:T(8,128)S(1)}, f32[128,128]{1,0:T(8,128)S(1)}, u32[]{:S(2)}, u32[]{:S(2)}) %collective-permute-start.7) | collective-permute-done | bytes 65568 | tf_op jit(solution)/shard_map/ppermute | solution.py:288
  60.3 11.0 %collective-permute-done.8 = f32[128,128]{1,0:T(8,128)S(1)} collective-permute-done((f32[128,128]{1,0:T(8,128)S(1)}, f32[128,128]{1,0:T(8,128)S(1)}, u32[]{:S(2)}, u32[]{:S(2)}) %collective-permute-start.8) | collective-permute-done | bytes 65568 | tf_op jit(solution)/shard_map/ppermute | solution.py:288
  71.3 1.7 collective-permute-start.9
  73.1 36.5 %collective-permute-done.9 = f32[128,128]{1,0:T(8,128)S(1)} collective-permute-done((f32[128,128]{1,0:T(8,128)S(1)}, f32[128,128]{1,0:T(8,128)S(1)}, u32[]{:S(2)}, u32[]{:S(2)}) %collective-permute-start.9) | collective-permute-done | bytes 65568 | tf_op jit(solution)/shard_map/ppermute | solution.py:288
  113.6 10.2 %shard_map.69 = (f32[2,4,64,512]{3,2,1,0:T(8,128)S(1)}, f32[2,4,64,512]{3,2,1,0:T(8,128)}) custom-call(s32[8,8]{1,0:T(8,128)S(1)} %bitcast.142, s32[4]{0:T(128)S(1)} %pad_add_fusion.me_ref, bf16[8,2064,256]{2,1,0:T(8,128)(2,1)} %all-to-all-done.tile_ref, bf16[64,4096]{1,0:T(8,128)(2,1)S(1)} %fusion.2.refs_0_, bf16[64,4096]{1,0:T(8,128)(2,1)} %collective-permute-done.refs_1_, ...), custom_call_target="tpu_custom_call" | custom-call | tf_op jit(solution)/shard_map/pallas_call | solution.py:105
  124.7 1.9 fusion.3
  127.4 2.1 collective-permute-start.10
  129.5 6.7 %collective-permute-done.14 = f16[4,64,512]{2,1,0:T(8,128)(2,1)} collective-permute-done((f16[4,64,512]{2,1,0:T(8,128)(2,1)}, f16[4,64,512]{2,1,0:T(8,128)(2,1)}, u32[]{:S(2)}, u32[]{:S(2)}) %collective-permute-start.14) | collective-permute-done | bytes 262176 | tf_op jit(solution)/shard_map/ppermute | solution.py:288
  137.6 2.3 collective-permute-start.15
  139.9 2.5 %collective-permute-start.17 = (f16[64,512]{1,0:T(8,128)(2,1)S(1)}, f16[64,512]{1,0:T(8,128)(2,1)S(1)}, u32[]{:S(2)}, u32[]{:S(2)}) collective-permute-start(f16[64,512]{1,0:T(8,128)(2,1)S(1)} %get-tuple-element.43), channel_id=1, source_target_pairs={{0,6},{2,4},{4,2},{6,0},{1,7},{3,5},{5,3},{7,1},{8,14},{10,12},{12... | collective-permute-start | bytes 196616 | tf_op jit(solution)/shard_map/ppermute | solution.py:288
  142.8 1.8 collective-permute-start.11
  144.6 2.5 %collective-permute-start.13 = (f16[64,512]{1,0:T(8,128)(2,1)S(1)}, f16[64,512]{1,0:T(8,128)(2,1)S(1)}, u32[]{:S(2)}, u32[]{:S(2)}) collective-permute-start(f16[64,512]{1,0:T(8,128)(2,1)S(1)} %get-tuple-element.46), channel_id=1, source_target_pairs={{0,6},{2,4},{4,2},{6,0},{1,7},{3,5},{5,3},{7,1},{8,14},{10,12},{12... | collective-permute-start | bytes 196616 | tf_op jit(solution)/shard_map/ppermute | solution.py:288
  147.1 2.6 %collective-permute-done.16 = f16[64,512]{1,0:T(8,128)(2,1)S(1)} collective-permute-done((f16[64,512]{1,0:T(8,128)(2,1)S(1)}, f16[64,512]{1,0:T(8,128)(2,1)S(1)}, u32[]{:S(2)}, u32[]{:S(2)}) %collective-permute-start.16) | collective-permute-done | bytes 65568 | tf_op jit(solution)/shard_map/ppermute | solution.py:288
  150.7 1.8 collective-permute-done.12
  152.6 1.4 shard_map.71.refs_0_
  154.1 3.0 %collective-permute-start.23 = (bf16[128,512]{1,0:T(8,128)(2,1)S(1)}, bf16[128,512]{1,0:T(8,128)(2,1)S(1)}, u32[]{:S(2)}, u32[]{:S(2)}) collective-permute-start(bf16[128,512]{1,0:T(8,128)(2,1)S(1)} %shard_map.71.refs_0_), channel_id=1, source_target_pairs={{0,6},{2,4},{4,2},{6,0},{1,7},{3,5},{5,3},{7,1},{8,14},{10,12},{12... | collective-permute-start | bytes 393224 | tf_op jit(solution)/shard_map/ppermute | solution.py:288
  157.1 1.5 collective-permute-start.19
  158.5 1.4 collective-permute-start.18
  159.9 1.8 collective-permute-done.23.refs_6_
  161.8 2.0 collective-permute-start.24
  163.8 2.6 %collective-permute-done.21.refs_4_ = bf16[128,512]{1,0:T(8,128)(2,1)S(1)} collective-permute-done((bf16[128,512]{1,0:T(8,128)(2,1)S(1)}, bf16[128,512]{1,0:T(8,128)(2,1)S(1)}, u32[]{:S(2)}, u32[]{:S(2)}) %collective-permute-start.21) | collective-permute-done | bytes 131104 | tf_op jit(solution)/shard_map/ppermute | solution.py:288
  166.4 1.8 collective-permute-start.22
  168.5 4.3 %collective-permute-done.22.refs_5_ = bf16[128,512]{1,0:T(8,128)(2,1)S(1)} collective-permute-done((bf16[128,512]{1,0:T(8,128)(2,1)S(1)}, bf16[128,512]{1,0:T(8,128)(2,1)S(1)}, u32[]{:S(2)}, u32[]{:S(2)}) %collective-permute-start.22) | collective-permute-done | bytes 131104 | tf_op jit(solution)/shard_map/ppermute | solution.py:288
  172.8 1.4 collective-permute-done.20.refs_3_
  174.2 10.5 %shard_map.73 = (f32[2,4,64,1024]{3,2,1,0:T(8,128)S(1)}, f32[2,4,64,1024]{3,2,1,0:T(8,128)S(1)}, f32[2,4,64,1024]{3,2,1,0:T(8,128)}, f32[2,4,64,1024]{3,2,1,0:T(8,128)}, f32[128,128]{1,0:T(8,128)S(1)}) custom-call(s32[8,8]{1,0:T(8,128)S(1)} %bitcast.143, s32[4]{0:T(128)S(1)} %pad_add_fusion.me_ref, bf16[8,2064,256]{2,1,0:T(8,128)(2,1)} %all-to-all-done.tile_ref, ...), custom_call_target="tpu_custom_call" | custom-call | tf_op jit(solution)/shard_map/pallas_call | solution.py:181
  185.2 1.7 collective-permute-start.26
  186.9 2.6 %collective-permute-done.26 = f32[128,128]{1,0:T(8,128)S(1)} collective-permute-done((f32[128,128]{1,0:T(8,128)S(1)}, f32[128,128]{1,0:T(8,128)S(1)}, u32[]{:S(2)}, u32[]{:S(2)}) %collective-permute-start.26) | collective-permute-done | bytes 65568 | tf_op jit(solution)/shard_map/ppermute | solution.py:288
  189.5 2.4 collective-permute-done.27
  195.0 1.7 collective-permute-start.28
  198.4 2.1 add.162
  201.1 8.9 %collective-permute-done.28 = f16[1,4,64,1024]{3,2,1,0:T(8,128)(2,1)} collective-permute-done((f16[1,4,64,1024]{3,2,1,0:T(8,128)(2,1)}, f16[1,4,64,1024]{3,2,1,0:T(8,128)(2,1)}, u32[]{:S(2)}, u32[]{:S(2)}) %collective-permute-start.28) | collective-permute-done | bytes 524320 | tf_op jit(solution)/shard_map/ppermute | solution.py:288
  212.6 1.6 collective-permute-start.31
  215.1 5.3 %collective-permute-done.33 = f16[1,4,64,1024]{3,2,1,0:T(8,128)(2,1)S(1)} collective-permute-done((f16[1,4,64,1024]{3,2,1,0:T(8,128)(2,1)S(1)}, f16[1,4,64,1024]{3,2,1,0:T(8,128)(2,1)S(1)}, u32[]{:S(2)}, u32[]{:S(2)}) %collective-permute-start.33) | collective-permute-done | bytes 524320 | tf_op jit(solution)/shard_map/ppermute | solution.py:288
  221.9 1.6 collective-permute-start.36
  224.4 7.8 %collective-permute-done.30 = f16[64,1024]{1,0:T(8,128)(2,1)S(1)} collective-permute-done((f16[64,1024]{1,0:T(8,128)(2,1)S(1)}, f16[64,1024]{1,0:T(8,128)(2,1)S(1)}, u32[]{:S(2)}, u32[]{:S(2)}) %collective-permute-start.30) | collective-permute-done | bytes 131104 | tf_op jit(solution)/shard_map/ppermute | solution.py:288
  232.3 4.2 %collective-permute-done.35 = f16[64,1024]{1,0:T(8,128)(2,1)S(1)} collective-permute-done((f16[64,1024]{1,0:T(8,128)(2,1)S(1)}, f16[64,1024]{1,0:T(8,128)(2,1)S(1)}, u32[]{:S(2)}, u32[]{:S(2)}) %collective-permute-start.35) | collective-permute-done | bytes 131104 | tf_op jit(solution)/shard_map/ppermute | solution.py:288
  236.7 2.2 shard_map.75.refs_0_
  238.8 1.7 collective-permute-start.38
  240.6 5.4 %collective-permute-done.38.refs_2_ = bf16[1024,128]{1,0:T(8,128)(2,1)S(1)} collective-permute-done((bf16[1024,128]{1,0:T(8,128)(2,1)S(1)}, bf16[1024,128]{1,0:T(8,128)(2,1)S(1)}, u32[]{:S(2)}, u32[]{:S(2)}) %collective-permute-start.38) | collective-permute-done | bytes 262176 | tf_op jit(solution)/shard_map/ppermute | solution.py:288
  246.0 1.7 shard_map.72
  247.6 1.5 shard_map.76
  (101 shorter events, 27.3 us)
Async XLA Ops:
  0.6 126.1 %copy-start = (f32[4096,128]{1,0:T(8,128)S(1)}, f32[4096,128]{1,0:T(8,128)}, u32[]{:S(2)}) copy-start(f32[4096,128]{1,0:T(8,128)} %param.8) | copy-start | bytes 6291460
  3.9 2.2 copy-start.2
  9.0 101.5 %all-to-all-start = ((bf16[8,2064,256]{2,1,0:T(8,128)(2,1)}), bf16[8,2064,256]{2,1,0:T(8,128)(2,1)}, u32[]{:S(2)}, u32[]{:S(2)}) async-start(bf16[8,2064,256]{2,1,0:T(8,128)(2,1)} %shard_map.68), calls=%async_computation | async-start | bytes 16908288 | tf_op jit(solution)/shard_map/all_to_all | solution.py:359
  18.3 91.5 %collective-permute-start.2 = (bf16[64,4096]{1,0:T(8,128)(2,1)S(1)}, bf16[64,4096]{1,0:T(8,128)(2,1)S(1)}, u32[]{:S(2)}, u32[]{:S(2)}) collective-permute-start(bf16[64,4096]{1,0:T(8,128)(2,1)S(1)} %fusion.2.refs_0_), channel_id=1, source_target_pairs={{0,6},{2,4},{4,2},{6,0},{1,7},{3,5},{5,3},{7,1},{8,14},{10,12},{12... | collective-permute-start | bytes 1572872 | tf_op jit(solution)/shard_map/ppermute | solution.py:288
  23.3 86.6 %collective-permute-start.1 = (bf16[64,4096]{1,0:T(8,128)(2,1)S(1)}, bf16[64,4096]{1,0:T(8,128)(2,1)}, u32[]{:S(2)}, u32[]{:S(2)}) collective-permute-start(bf16[64,4096]{1,0:T(8,128)(2,1)S(1)} %fusion.2.refs_0_), channel_id=1, source_target_pairs={{0,4},{2,6},{4,0},{6,2},{1,5},{3,7},{5,1},{7,3},{8,12},{10,14},{12... | collective-permute-start | bytes 1572872 | tf_op jit(solution)/shard_map/ppermute | solution.py:288
  23.3 87.1 %collective-permute-start = (bf16[64,4096]{1,0:T(8,128)(2,1)S(1)}, bf16[64,4096]{1,0:T(8,128)(2,1)}, u32[]{:S(2)}, u32[]{:S(2)}) collective-permute-start(bf16[64,4096]{1,0:T(8,128)(2,1)S(1)} %fusion.2.refs_0_), channel_id=1, source_target_pairs={{0,2},{2,0},{4,6},{6,4},{1,3},{3,1},{5,7},{7,5},{8,10},{10,8},{12,... | collective-permute-start | bytes 1572872 | tf_op jit(solution)/shard_map/ppermute | solution.py:288
  29.6 29.4 %collective-permute-start.7 = (f32[128,128]{1,0:T(8,128)S(1)}, f32[128,128]{1,0:T(8,128)S(1)}, u32[]{:S(2)}, u32[]{:S(2)}) collective-permute-start(f32[128,128]{1,0:T(8,128)S(1)} %fusion.48), channel_id=1, source_target_pairs={{0,2},{2,0},{4,6},{6,4},{1,3},{3,1},{5,7},{7,5},{8,10},{10,8},{12,... | collective-permute-start | bytes 196616 | tf_op jit(solution)/shard_map/ppermute | solution.py:288
  58.9 12.4 %collective-permute-start.8 = (f32[128,128]{1,0:T(8,128)S(1)}, f32[128,128]{1,0:T(8,128)S(1)}, u32[]{:S(2)}, u32[]{:S(2)}) collective-permute-start(f32[128,128]{1,0:T(8,128)S(1)} %add.142), channel_id=1, source_target_pairs={{0,4},{2,6},{4,0},{6,2},{1,5},{3,7},{5,1},{7,3},{8,12},{10,14},{12... | collective-permute-start | bytes 196616 | tf_op jit(solution)/shard_map/ppermute | solution.py:288
  60.3 50.9 %collective-permute-start.3 = (bf16[64,4096]{1,0:T(8,128)(2,1)S(1)}, bf16[64,4096]{1,0:T(8,128)(2,1)}, u32[]{:S(2)}, u32[]{:S(2)}) collective-permute-start(bf16[64,4096]{1,0:T(8,128)(2,1)S(1)} %fusion.2.refs_0_), channel_id=1, source_target_pairs={{0,8},{8,0},{1,9},{9,1},{2,10},{10,2},{3,11},{11,3},{4,12},{12,4},... | collective-permute-start | bytes 1572872 | tf_op jit(solution)/shard_map/ppermute | solution.py:288
  71.3 38.3 %collective-permute-start.9 = (f32[128,128]{1,0:T(8,128)S(1)}, f32[128,128]{1,0:T(8,128)S(1)}, u32[]{:S(2)}, u32[]{:S(2)}) collective-permute-start(f32[128,128]{1,0:T(8,128)S(1)} %add.143), channel_id=1, source_target_pairs={{0,1},{1,0},{2,3},{3,2},{4,5},{5,4},{6,7},{7,6},{8,9},{9,8},{10,11... | collective-permute-start | bytes 196616 | tf_op jit(solution)/shard_map/ppermute | solution.py:288
  109.8 2.1 collective-permute-start.6
  109.9 3.0 %collective-permute-start.5 = (bf16[64,4096]{1,0:T(8,128)(2,1)}, bf16[64,4096]{1,0:T(8,128)(2,1)}, u32[]{:S(2)}, u32[]{:S(2)}) collective-permute-start(bf16[64,4096]{1,0:T(8,128)(2,1)} %collective-permute-done.1.refs_2_), channel_id=1, source_target_pairs={{0,8},{8,0},{1,9},{9,1},{2,10},{10,2},{3,11},{11,3},{4,12},{12,4},... | collective-permute-start | bytes 1572872 | tf_op jit(solution)/shard_map/ppermute | solution.py:288
  110.4 3.2 %collective-permute-start.4 = (bf16[64,4096]{1,0:T(8,128)(2,1)}, bf16[64,4096]{1,0:T(8,128)(2,1)}, u32[]{:S(2)}, u32[]{:S(2)}) collective-permute-start(bf16[64,4096]{1,0:T(8,128)(2,1)} %collective-permute-done.refs_1_), channel_id=1, source_target_pairs={{0,8},{8,0},{1,9},{9,1},{2,10},{10,2},{3,11},{11,3},{4,12},{12,4},... | collective-permute-start | bytes 1572872 | tf_op jit(solution)/shard_map/ppermute | solution.py:288
  123.8 1.0 copy-start.3
  124.7 2.5 %copy-start.4 = (f32[2,4,64,512]{3,2,1,0:T(8,128)S(1)}, f32[2,4,64,512]{3,2,1,0:T(8,128)}, u32[]{:S(2)}) copy-start(f32[2,4,64,512]{3,2,1,0:T(8,128)} %copy-done.3) | copy-start | bytes 3145732
  126.7 9.6 %collective-permute-start.14 = (f16[4,64,512]{2,1,0:T(8,128)(2,1)}, f16[4,64,512]{2,1,0:T(8,128)(2,1)}, u32[]{:S(2)}, u32[]{:S(2)}) collective-permute-start(f16[4,64,512]{2,1,0:T(8,128)(2,1)} %fusion.3), channel_id=1, source_target_pairs={{0,1},{1,0},{2,3},{3,2},{4,5},{5,4},{6,7},{7,6},{8,9},{9,8},{10,11... | collective-permute-start | bytes 786440 | tf_op jit(solution)/shard_map/ppermute | solution.py:288
  127.4 15.2 %collective-permute-start.10 = (f16[4,64,512]{2,1,0:T(8,128)(2,1)S(1)}, f16[4,64,512]{2,1,0:T(8,128)(2,1)S(1)}, u32[]{:S(2)}, u32[]{:S(2)}) collective-permute-start(f16[4,64,512]{2,1,0:T(8,128)(2,1)S(1)} %fusion.4), channel_id=1, source_target_pairs={{0,1},{1,0},{2,3},{3,2},{4,5},{5,4},{6,7},{7,6},{8,9},{9,8},{10,11... | collective-permute-start | bytes 786440 | tf_op jit(solution)/shard_map/ppermute | solution.py:288
  137.6 9.5 %collective-permute-start.15 = (f16[64,512]{1,0:T(8,128)(2,1)S(1)}, f16[64,512]{1,0:T(8,128)(2,1)S(1)}, u32[]{:S(2)}, u32[]{:S(2)}) collective-permute-start(f16[64,512]{1,0:T(8,128)(2,1)S(1)} %get-tuple-element.42), channel_id=1, source_target_pairs={{0,2},{2,0},{4,6},{6,4},{1,3},{3,1},{5,7},{7,5},{8,10},{10,8},{12,... | collective-permute-start | bytes 196616 | tf_op jit(solution)/shard_map/ppermute | solution.py:288
  139.9 7.2 %collective-permute-start.17 = (f16[64,512]{1,0:T(8,128)(2,1)S(1)}, f16[64,512]{1,0:T(8,128)(2,1)S(1)}, u32[]{:S(2)}, u32[]{:S(2)}) collective-permute-start(f16[64,512]{1,0:T(8,128)(2,1)S(1)} %get-tuple-element.43), channel_id=1, source_target_pairs={{0,6},{2,4},{4,2},{6,0},{1,7},{3,5},{5,3},{7,1},{8,14},{10,12},{12... | collective-permute-start | bytes 196616 | tf_op jit(solution)/shard_map/ppermute | solution.py:288
  142.4 7.3 %collective-permute-start.16 = (f16[64,512]{1,0:T(8,128)(2,1)S(1)}, f16[64,512]{1,0:T(8,128)(2,1)S(1)}, u32[]{:S(2)}, u32[]{:S(2)}) collective-permute-start(f16[64,512]{1,0:T(8,128)(2,1)S(1)} %get-tuple-element.44), channel_id=1, source_target_pairs={{0,4},{2,6},{4,0},{6,2},{1,5},{3,7},{5,1},{7,3},{8,12},{10,14},{12... | collective-permute-start | bytes 196616 | tf_op jit(solution)/shard_map/ppermute | solution.py:288
  142.8 7.0 %collective-permute-start.11 = (f16[64,512]{1,0:T(8,128)(2,1)S(1)}, f16[64,512]{1,0:T(8,128)(2,1)S(1)}, u32[]{:S(2)}, u32[]{:S(2)}) collective-permute-start(f16[64,512]{1,0:T(8,128)(2,1)S(1)} %get-tuple-element.45), channel_id=1, source_target_pairs={{0,2},{2,0},{4,6},{6,4},{1,3},{3,1},{5,7},{7,5},{8,10},{10,8},{12,... | collective-permute-start | bytes 196616 | tf_op jit(solution)/shard_map/ppermute | solution.py:288
  144.6 6.2 %collective-permute-start.13 = (f16[64,512]{1,0:T(8,128)(2,1)S(1)}, f16[64,512]{1,0:T(8,128)(2,1)S(1)}, u32[]{:S(2)}, u32[]{:S(2)}) collective-permute-start(f16[64,512]{1,0:T(8,128)(2,1)S(1)} %get-tuple-element.46), channel_id=1, source_target_pairs={{0,6},{2,4},{4,2},{6,0},{1,7},{3,5},{5,3},{7,1},{8,14},{10,12},{12... | collective-permute-start | bytes 196616 | tf_op jit(solution)/shard_map/ppermute | solution.py:288
  147.1 5.4 %collective-permute-start.12 = (f16[64,512]{1,0:T(8,128)(2,1)S(1)}, f16[64,512]{1,0:T(8,128)(2,1)S(1)}, u32[]{:S(2)}, u32[]{:S(2)}) collective-permute-start(f16[64,512]{1,0:T(8,128)(2,1)S(1)} %get-tuple-element.47), channel_id=1, source_target_pairs={{0,4},{2,6},{4,0},{6,2},{1,5},{3,7},{5,1},{7,3},{8,12},{10,14},{12... | collective-permute-start | bytes 196616 | tf_op jit(solution)/shard_map/ppermute | solution.py:288
  154.1 7.7 %collective-permute-start.23 = (bf16[128,512]{1,0:T(8,128)(2,1)S(1)}, bf16[128,512]{1,0:T(8,128)(2,1)S(1)}, u32[]{:S(2)}, u32[]{:S(2)}) collective-permute-start(bf16[128,512]{1,0:T(8,128)(2,1)S(1)} %shard_map.71.refs_0_), channel_id=1, source_target_pairs={{0,6},{2,4},{4,2},{6,0},{1,7},{3,5},{5,3},{7,1},{8,14},{10,12},{12... | collective-permute-start | bytes 393224 | tf_op jit(solution)/shard_map/ppermute | solution.py:288
  157.1 9.3 %collective-permute-start.21 = (bf16[128,512]{1,0:T(8,128)(2,1)S(1)}, bf16[128,512]{1,0:T(8,128)(2,1)S(1)}, u32[]{:S(2)}, u32[]{:S(2)}) collective-permute-start(bf16[128,512]{1,0:T(8,128)(2,1)S(1)} %shard_map.71.refs_0_), channel_id=1, source_target_pairs={{0,4},{2,6},{4,0},{6,2},{1,5},{3,7},{5,1},{7,3},{8,12},{10,14},{12... | collective-permute-start | bytes 393224 | tf_op jit(solution)/shard_map/ppermute | solution.py:288
  157.1 11.2 %collective-permute-start.19 = (bf16[128,512]{1,0:T(8,128)(2,1)S(1)}, bf16[128,512]{1,0:T(8,128)(2,1)S(1)}, u32[]{:S(2)}, u32[]{:S(2)}) collective-permute-start(bf16[128,512]{1,0:T(8,128)(2,1)S(1)} %shard_map.71.refs_0_), channel_id=1, source_target_pairs={{0,2},{2,0},{4,6},{6,4},{1,3},{3,1},{5,7},{7,5},{8,10},{10,8},{12,... | collective-permute-start | bytes 393224 | tf_op jit(solution)/shard_map/ppermute | solution.py:288
  158.5 9.9 %collective-permute-start.18 = (bf16[128,512]{1,0:T(8,128)(2,1)S(1)}, bf16[128,512]{1,0:T(8,128)(2,1)S(1)}, u32[]{:S(2)}, u32[]{:S(2)}) collective-permute-start(bf16[128,512]{1,0:T(8,128)(2,1)S(1)} %shard_map.71.refs_0_), channel_id=1, source_target_pairs={{0,1},{1,0},{2,3},{3,2},{4,5},{5,4},{6,7},{7,6},{8,9},{9,8},{10,11... | collective-permute-start | bytes 393224 | tf_op jit(solution)/shard_map/ppermute | solution.py:288
  161.8 6.7 %collective-permute-start.24 = (bf16[128,512]{1,0:T(8,128)(2,1)S(1)}, bf16[128,512]{1,0:T(8,128)(2,1)S(1)}, u32[]{:S(2)}, u32[]{:S(2)}) collective-permute-start(bf16[128,512]{1,0:T(8,128)(2,1)S(1)} %collective-permute-done.23.refs_6_), channel_id=1, source_target_pairs={{0,1},{1,0},{2,3},{3,2},{4,5},{5,4},{6,7},{7,6},{8,9},{9,8},{10,11... | collective-permute-start | bytes 393224 | tf_op jit(solution)/shard_map/ppermute | solution.py:288
  166.4 6.4 %collective-permute-start.22 = (bf16[128,512]{1,0:T(8,128)(2,1)S(1)}, bf16[128,512]{1,0:T(8,128)(2,1)S(1)}, u32[]{:S(2)}, u32[]{:S(2)}) collective-permute-start(bf16[128,512]{1,0:T(8,128)(2,1)S(1)} %collective-permute-done.21.refs_4_), channel_id=1, source_target_pairs={{0,1},{1,0},{2,3},{3,2},{4,5},{5,4},{6,7},{7,6},{8,9},{9,8},{10,11... | collective-permute-start | bytes 393224 | tf_op jit(solution)/shard_map/ppermute | solution.py:288
  168.3 5.9 %collective-permute-start.20 = (bf16[128,512]{1,0:T(8,128)(2,1)S(1)}, bf16[128,512]{1,0:T(8,128)(2,1)S(1)}, u32[]{:S(2)}, u32[]{:S(2)}) collective-permute-start(bf16[128,512]{1,0:T(8,128)(2,1)S(1)} %collective-permute-done.19.refs_2_), channel_id=1, source_target_pairs={{0,1},{1,0},{2,3},{3,2},{4,5},{5,4},{6,7},{7,6},{8,9},{9,8},{10,11... | collective-permute-start | bytes 393224 | tf_op jit(solution)/shard_map/ppermute | solution.py:288
  184.7 7.5 %collective-permute-start.25 = (f32[2,4,64,1024]{3,2,1,0:T(8,128)}, f32[2,4,64,1024]{3,2,1,0:T(8,128)S(1)}, u32[]{:S(2)}, u32[]{:S(2)}) collective-permute-start(f32[2,4,64,1024]{3,2,1,0:T(8,128)} %get-tuple-element.25), channel_id=1, source_target_pairs={{0,8},{8,0},{1,9},{9,1},{2,10},{10,2},{3,11},{11,3},{4,12},{12,4},... | collective-permute-start | bytes 6291464 | tf_op jit(solution)/shard_map/ppermute | solution.py:288
  184.7 13.8 %collective-permute-start.32 = (f32[2,4,64,1024]{3,2,1,0:T(8,128)}, f32[2,4,64,1024]{3,2,1,0:T(8,128)}, u32[]{:S(2)}, u32[]{:S(2)}) collective-permute-start(f32[2,4,64,1024]{3,2,1,0:T(8,128)} %get-tuple-element.28), channel_id=1, source_target_pairs={{0,8},{8,0},{1,9},{9,1},{2,10},{10,2},{3,11},{11,3},{4,12},{12,4},... | collective-permute-start | bytes 6291464 | tf_op jit(solution)/shard_map/ppermute | solution.py:288
  185.2 4.3 %collective-permute-start.26 = (f32[128,128]{1,0:T(8,128)S(1)}, f32[128,128]{1,0:T(8,128)S(1)}, u32[]{:S(2)}, u32[]{:S(2)}) collective-permute-start(f32[128,128]{1,0:T(8,128)S(1)} %get-tuple-element.26), channel_id=1, source_target_pairs={{0,16},{16,0},{1,17},{17,1},{2,18},{18,2},{3,19},{19,3},{4,20},{20... | collective-permute-start | bytes 196616 | tf_op jit(solution)/shard_map/ppermute | solution.py:288
  189.5 2.5 collective-permute-start.27
  192.7 1.3 copy-start.5
  195.0 15.1 %collective-permute-start.28 = (f16[1,4,64,1024]{3,2,1,0:T(8,128)(2,1)}, f16[1,4,64,1024]{3,2,1,0:T(8,128)(2,1)}, u32[]{:S(2)}, u32[]{:S(2)}) collective-permute-start(f16[1,4,64,1024]{3,2,1,0:T(8,128)(2,1)} %fusion.1), channel_id=1, source_target_pairs={{0,16},{16,0},{1,17},{17,1},{2,18},{18,2},{3,19},{19,3},{4,20},{20... | collective-permute-start | bytes 1572872 | tf_op jit(solution)/shard_map/ppermute | solution.py:288
  198.4 11.6 %copy-start.6 = (f32[2,4,64,1024]{3,2,1,0:T(8,128)S(1)}, f32[2,4,64,1024]{3,2,1,0:T(8,128)}, u32[]{:S(2)}) copy-start(f32[2,4,64,1024]{3,2,1,0:T(8,128)} %copy-done.5) | copy-start | bytes 6291460
  200.8 19.7 %collective-permute-start.33 = (f16[1,4,64,1024]{3,2,1,0:T(8,128)(2,1)S(1)}, f16[1,4,64,1024]{3,2,1,0:T(8,128)(2,1)S(1)}, u32[]{:S(2)}, u32[]{:S(2)}) collective-permute-start(f16[1,4,64,1024]{3,2,1,0:T(8,128)(2,1)S(1)} %fusion), channel_id=1, source_target_pairs={{0,16},{16,0},{1,17},{17,1},{2,18},{18,2},{3,19},{19,3},{4,20},{20... | collective-permute-start | bytes 1572872 | tf_op jit(solution)/shard_map/ppermute | solution.py:288
  211.5 11.9 %collective-permute-start.29 = (f16[64,1024]{1,0:T(8,128)(2,1)S(1)}, f16[64,1024]{1,0:T(8,128)(2,1)S(1)}, u32[]{:S(2)}, u32[]{:S(2)}) collective-permute-start(f16[64,1024]{1,0:T(8,128)(2,1)S(1)} %get-tuple-element.39), channel_id=1, source_target_pairs={{0,2},{2,0},{4,6},{6,4},{1,3},{3,1},{5,7},{7,5},{8,10},{10,8},{12,... | collective-permute-start | bytes 393224 | tf_op jit(solution)/shard_map/ppermute | solution.py:288
  212.6 11.8 %collective-permute-start.31 = (f16[64,1024]{1,0:T(8,128)(2,1)S(1)}, f16[64,1024]{1,0:T(8,128)(2,1)S(1)}, u32[]{:S(2)}, u32[]{:S(2)}) collective-permute-start(f16[64,1024]{1,0:T(8,128)(2,1)S(1)} %get-tuple-element.40), channel_id=1, source_target_pairs={{0,6},{2,4},{4,2},{6,0},{1,7},{3,5},{5,3},{7,1},{8,14},{10,12},{12... | collective-permute-start | bytes 393224 | tf_op jit(solution)/shard_map/ppermute | solution.py:288
  214.2 17.9 %collective-permute-start.30 = (f16[64,1024]{1,0:T(8,128)(2,1)S(1)}, f16[64,1024]{1,0:T(8,128)(2,1)S(1)}, u32[]{:S(2)}, u32[]{:S(2)}) collective-permute-start(f16[64,1024]{1,0:T(8,128)(2,1)S(1)} %get-tuple-element.41), channel_id=1, source_target_pairs={{0,4},{2,6},{4,0},{6,2},{1,5},{3,7},{5,1},{7,3},{8,12},{10,14},{12... | collective-permute-start | bytes 393224 | tf_op jit(solution)/shard_map/ppermute | solution.py:288
  220.8 11.5 %collective-permute-start.34 = (f16[64,1024]{1,0:T(8,128)(2,1)S(1)}, f16[64,1024]{1,0:T(8,128)(2,1)S(1)}, u32[]{:S(2)}, u32[]{:S(2)}) collective-permute-start(f16[64,1024]{1,0:T(8,128)(2,1)S(1)} %get-tuple-element.36), channel_id=1, source_target_pairs={{0,2},{2,0},{4,6},{6,4},{1,3},{3,1},{5,7},{7,5},{8,10},{10,8},{12,... | collective-permute-start | bytes 393224 | tf_op jit(solution)/shard_map/ppermute | solution.py:288
  221.9 10.4 %collective-permute-start.36 = (f16[64,1024]{1,0:T(8,128)(2,1)S(1)}, f16[64,1024]{1,0:T(8,128)(2,1)S(1)}, u32[]{:S(2)}, u32[]{:S(2)}) collective-permute-start(f16[64,1024]{1,0:T(8,128)(2,1)S(1)} %get-tuple-element.37), channel_id=1, source_target_pairs={{0,6},{2,4},{4,2},{6,0},{1,7},{3,5},{5,3},{7,1},{8,14},{10,12},{12... | collective-permute-start | bytes 393224 | tf_op jit(solution)/shard_map/ppermute | solution.py:288
  223.5 13.0 %collective-permute-start.35 = (f16[64,1024]{1,0:T(8,128)(2,1)S(1)}, f16[64,1024]{1,0:T(8,128)(2,1)S(1)}, u32[]{:S(2)}, u32[]{:S(2)}) collective-permute-start(f16[64,1024]{1,0:T(8,128)(2,1)S(1)} %get-tuple-element.38), channel_id=1, source_target_pairs={{0,4},{2,6},{4,0},{6,2},{1,5},{3,7},{5,1},{7,3},{8,12},{10,14},{12... | collective-permute-start | bytes 393224 | tf_op jit(solution)/shard_map/ppermute | solution.py:288
  238.8 7.1 %collective-permute-start.38 = (bf16[1024,128]{1,0:T(8,128)(2,1)S(1)}, bf16[1024,128]{1,0:T(8,128)(2,1)S(1)}, u32[]{:S(2)}, u32[]{:S(2)}) collective-permute-start(bf16[1024,128]{1,0:T(8,128)(2,1)S(1)} %shard_map.75.refs_0_), channel_id=1, source_target_pairs={{0,16},{16,0},{1,17},{17,1},{2,18},{18,2},{3,19},{19,3},{4,20},{20... | collective-permute-start | bytes 786440 | tf_op jit(solution)/shard_map/ppermute | solution.py:288
  240.6 7.1 %collective-permute-start.37 = (bf16[1024,128]{1,0:T(8,128)(2,1)S(1)}, bf16[1024,128]{1,0:T(8,128)(2,1)S(1)}, u32[]{:S(2)}, u32[]{:S(2)}) collective-permute-start(bf16[1024,128]{1,0:T(8,128)(2,1)S(1)} %shard_map.75.refs_0_), channel_id=1, source_target_pairs={{0,8},{8,0},{1,9},{9,1},{2,10},{10,2},{3,11},{11,3},{4,12},{12,4},... | collective-permute-start | bytes 786440 | tf_op jit(solution)/shard_map/ppermute | solution.py:288
  246.0 1.7 collective-permute-start.39
  246.0 3.1 %copy-start.1 = (f32[4096,128]{1,0:T(8,128)S(1)}, f32[4096,128]{1,0:T(8,128)}, u32[]{:S(2)}) copy-start(f32[4096,128]{1,0:T(8,128)} %param.8) | copy-start | bytes 6291460

commit v4 on v3

v4 whole, which is shorter than its diff:
```python
import jax
import jax.numpy as jnp
from jax import lax
from jax.experimental import pallas as pl
from jax.experimental.pallas import tpu as pltpu
from jax.sharding import Mesh
from jax.sharding import PartitionSpec as P

CT = 16
CAP = 2
EPS = 1e-06
RIDGE = 1.0
HIGH = lax.Precision.HIGHEST
F32 = jnp.float32
LINK = jnp.float16
STEP = 32
DEPTH = 8
PEAK = 256.0
CUT = 80
VMEM_LIMIT = 32 * 2**20


def params(limit=VMEM_LIMIT):
    return pltpu.CompilerParams(vmem_limit_bytes=limit)


def pack(owner, spot, tile_data, rows, his, los):
    count, size = tile_data.shape[0], tile_data.shape[1]
    peers, held, extra = rows * los, his * CAP, 16

    def kernel(owner_ref, spot_ref, tiles_ref, out_ref, held_ref, notes_ref, seen_ref, sems):
        ins = [
            pltpu.make_async_copy(tiles_ref.at[s], held_ref.at[s], sems.at[s]) for s in range(count)
        ]
        for copy in ins:
            copy.start()

        def clear(i, carry):
            seen_ref[i] = 0
            return carry

        lax.fori_loop(0, rows * his * los, clear, 0)
        shape = (peers, size)
        peer_of = lax.broadcasted_iota(jnp.int32, shape, 0)
        slot_of = lax.broadcasted_iota(jnp.int32, shape, 1)
        notes = jnp.zeros(shape, F32)
        outs = []
        for s in range(count):
            one = owner_ref[s]
            row, col = one // (his * los), one % (his * los)
            peer, slot = row * los + col % los, col // los * CAP + seen_ref[one]
            seen_ref[one] += 1
            notes = jnp.where((peer_of == peer) & (slot_of == slot), (spot_ref[s] + 1).astype(F32), notes)
            dest = out_ref.at[peer, pl.ds(pl.multiple_of(slot * size, size), size)]
            ins[s].wait()
            outs.append(pltpu.make_async_copy(held_ref.at[s], dest, sems.at[count + s]))
            outs[-1].start()
        for peer in range(peers):
            line = jnp.broadcast_to(notes[peer : peer + 1], (extra, size))
            notes_ref[peer] = line.astype(notes_ref.dtype)
        dest = out_ref.at[:, pl.ds(held * size, extra)]
        outs.append(pltpu.make_async_copy(notes_ref, dest, sems.at[2 * count]))
        outs[-1].start()
        for copy in outs:
            copy.wait()

    smem = pl.BlockSpec(memory_space=pltpu.SMEM)
    return pl.pallas_call(
        kernel,
        out_shape=jax.ShapeDtypeStruct((peers, held * size + extra, size), tile_data.dtype),
        in_specs=[smem, smem, pl.BlockSpec(memory_space=pltpu.HBM)],
        out_specs=pl.BlockSpec(memory_space=pltpu.HBM),
        scratch_shapes=[
            pltpu.VMEM(tile_data.shape, tile_data.dtype),
            pltpu.VMEM((peers, extra, size), tile_data.dtype),
            pltpu.SMEM((rows * his * los,), jnp.int32),
            pltpu.SemaphoreType.DMA((2 * count + 1,)),
        ],
        compiler_params=params(60 * 2**20),
    )(owner, spot, tile_data)


def each_tile(meta_ref, inbox_ref, tiles_ref, terms_ref, sems, product, add, ready):
    held, size, depth = meta_ref.shape[1], terms_ref.shape[2], tiles_ref.shape[0]
    peers = meta_ref.shape[0]

    def copy(peer):
        at = peer % depth
        rows = pl.ds(0, held * size)
        return pltpu.make_async_copy(inbox_ref.at[peer, rows], tiles_ref.at[at], sems.at[at])

    if sems is not None:
        for peer in range(depth):
            copy(peer).start()
    ready()

    def step(peer, carry):
        if sems is not None:
            copy(peer).wait()
        for slot in range(held):
            spot = jnp.maximum(meta_ref[peer, slot] - 1, 0)
            tile = tiles_ref[peer % depth, slot * size : (slot + 1) * size]
            terms_ref[slot] = product(slot, spot, tile)
        for slot in range(held):
            spot = meta_ref[peer, slot] - 1

            @pl.when(spot >= 0)
            def _():
                add(slot, spot)

        if depth < peers:

            @pl.when(peer + depth < peers)
            def _():
                copy(peer + depth).start()

        return carry

    lax.fori_loop(0, peers, step, 0)


def hbm():
    return pl.BlockSpec(memory_space=pltpu.HBM)


def vmem():
    return pl.BlockSpec(memory_space=pltpu.VMEM)


def smem():
    return pl.BlockSpec(memory_space=pltpu.SMEM)


def row_products(inbox, meta, me, pieces, his, los, width):
    peers, size, held = inbox.shape[0], inbox.shape[2], meta.shape[1]
    part, length = pieces[0].shape
    rank = 2 * part
    per_chunk = width // size
    keep = peers <= DEPTH

    def kernel(meta_ref, me_ref, inbox_ref, *refs):
        piece_refs, (top_ref, bot_ref) = refs[: 2 * his], refs[2 * his : 2 * his + 2]
        tiles_ref, panel_ref, terms_ref, sems, more_sems = refs[2 * his + 2 :]
        my_core, my_hi, my_lo = me_ref[1], me_ref[2], me_ref[3]
        copies = []
        for side in range(2):
            rows = pl.ds(pl.multiple_of((my_core ^ side) * part, part), part)
            for j in range(his):
                at = side * his + j
                copies.append(
                    pltpu.make_async_copy(piece_refs[at], panel_ref.at[j, rows], more_sems.at[at])
                )
        for copy in copies:
            copy.start()

        def ready():
            top_ref[...] = jnp.zeros_like(top_ref)
            bot_ref[...] = jnp.zeros_like(bot_ref)
            for copy in copies:
                copy.wait()

        def product(slot, spot, tile):
            place = pl.ds(pl.multiple_of((spot % CT) * size, size), size)
            panel = panel_ref[slot // CAP ^ my_hi, :, place]
            return lax.dot_general(panel, tile, (((1,), (1,)), ((), ())), preferred_element_type=F32)

        def add(slot, spot):
            trow = spot // CT
            chunk = trow // per_chunk
            lanes = pl.ds(pl.multiple_of((trow % per_chunk) * size, size), size)
            hi, lo = chunk // los ^ my_hi, chunk % los ^ my_lo
            top_ref[lo, hi, :, lanes] += terms_ref[slot, :CUT]
            bot_ref[hi, lo, :, lanes] += terms_ref[slot, CUT:]

        each_tile(meta_ref, inbox_ref, tiles_ref, terms_ref, sems, product, add, ready)

    out_shape = [
        jax.ShapeDtypeStruct((los, his, CUT, width), F32),
        jax.ShapeDtypeStruct((his, los, rank - CUT, width), F32),
    ]
    tiles = (min(peers, DEPTH), held * size, size)
    out_tiles = [jax.ShapeDtypeStruct(tiles, inbox.dtype)] if keep else []
    return pl.pallas_call(
        kernel,
        out_shape=out_shape + out_tiles,
        in_specs=[smem(), smem(), hbm()] + [hbm()] * len(pieces),
        out_specs=[vmem()] * (2 + keep),
        scratch_shapes=([] if keep else [pltpu.VMEM(tiles, inbox.dtype)])
        + [
            pltpu.VMEM((his, rank, length), jnp.bfloat16),
            pltpu.VMEM((held, rank, size), F32),
            pltpu.SemaphoreType.DMA((tiles[0],)),
            pltpu.SemaphoreType.DMA((2 * his,)),
        ],
        compiler_params=params(),
    )(meta, me, inbox, *pieces)


def column_products(inbox, kept, meta, me, pieces, his, los, fars, out_width):
    peers, size, held = inbox.shape[0], inbox.shape[2], meta.shape[1]
    rank, width = pieces[0].shape
    per_chunk, per_out = width // size, out_width // size
    chunks = his * los

    def kernel(meta_ref, me_ref, source_ref, *refs):
        piece_refs, outs, gram_ref = refs[:chunks], refs[chunks : chunks + 4], refs[chunks + 4]
        panel_ref, terms_ref, *rest = refs[chunks + 5 :]
        tiles_ref, sems = (source_ref, None) if kept else rest
        my_far, my_core, my_hi, my_lo = (me_ref[i] for i in range(4))

        def ready():
            for out in outs:
                out[...] = jnp.zeros_like(out)
            gram = jnp.zeros((rank, rank), F32)
            for j in range(chunks):
                piece = piece_refs[j][...]
                panel_ref[j] = piece
                gram += lax.dot_general(
                    piece, piece, (((1,), (1,)), ((), ())), preferred_element_type=F32
                )
            gram_ref[...] = gram

        def product(slot, spot, tile):
            trow = spot // CT
            chunk = trow // per_chunk
            lanes = pl.ds(pl.multiple_of((trow % per_chunk) * size, size), size)
            panel = panel_ref[(chunk // los ^ my_hi) * los + (chunk % los ^ my_lo), :, lanes]
            return lax.dot_general(panel, tile, (((1,), (0,)), ((), ())), preferred_element_type=F32)

        def add(slot, spot):
            tcol = spot % CT
            owner = tcol // per_out
            place = pl.ds(pl.multiple_of((tcol % per_out) * size, size), size)
            far, hi = owner // 2 ^ my_far, slot // CAP ^ my_hi
            for side, (top_ref, bot_ref) in enumerate((outs[:2], outs[2:])):

                @pl.when((owner ^ my_core) % 2 == side)
                def _():
                    top_ref[far, hi, :, place] += terms_ref[slot, :CUT]
                    bot_ref[hi, far, :, place] += terms_ref[slot, CUT:]

        each_tile(meta_ref, source_ref, tiles_ref, terms_ref, sems, product, add, ready)

    tops, bots = (fars, his, CUT, out_width), (his, fars, rank - CUT, out_width)
    out_shape = [tops, bots, tops, bots, (rank, rank)]
    scratch = [
        pltpu.VMEM((chunks, rank, width), jnp.bfloat16),
        pltpu.VMEM((held, rank, size), F32),
    ]
    if not kept:
        scratch.append(pltpu.VMEM((DEPTH, held * size, size), inbox.dtype))
        scratch.append(pltpu.SemaphoreType.DMA((DEPTH,)))
    return pl.pallas_call(
        kernel,
        out_shape=[jax.ShapeDtypeStruct(shape, F32) for shape in out_shape],
        in_specs=[smem(), smem(), vmem() if kept else hbm()] + [vmem()] * chunks,
        out_specs=[vmem()] * len(out_shape),
        scratch_shapes=scratch,
        compiler_params=params(),
    )(meta, me, *(kept or [inbox]), *pieces)


def assemble(pieces, place, turned):
    count = len(pieces)
    rank, width = pieces[0].shape if turned else pieces[0].shape[::-1]

    def kernel(place_ref, *refs):
        for j in range(count):
            piece = refs[j][...].astype(F32)
            refs[count][j ^ place_ref[0]] = jnp.transpose(piece) if turned else piece

    return pl.pallas_call(
        kernel,
        out_shape=jax.ShapeDtypeStruct((count, width, rank), F32),
        in_specs=[pl.BlockSpec(memory_space=pltpu.SMEM)]
        + [pl.BlockSpec(memory_space=pltpu.VMEM)] * count,
        out_specs=pl.BlockSpec(memory_space=pltpu.VMEM),
        compiler_params=params(),
    )(place, *pieces).reshape(count * width, rank)


def prepare(factor, gram):
    rank, width = factor.shape

    def kernel(factor_ref, gram_ref, part_ref, mixed_ref, over_ref):
        gram = gram_ref[...]
        shape = (rank, rank)
        diag = lax.broadcasted_iota(jnp.int32, shape, 0) == lax.broadcasted_iota(jnp.int32, shape, 1)
        over = 1.0 / (jnp.sum(jnp.where(diag, gram, 0.0), axis=1, keepdims=True) + RIDGE)
        mixed = gram * over
        mixed_ref[...] = mixed
        over_ref[...] = jnp.broadcast_to(over, shape)
        part_ref[...] = jnp.dot(
            jnp.where(diag, 0.0, mixed), factor_ref[...], precision=HIGH, preferred_element_type=F32
        )

    return pl.pallas_call(
        kernel,
        out_shape=[
            jax.ShapeDtypeStruct((rank, width), F32),
            jax.ShapeDtypeStruct((rank, rank), F32),
            jax.ShapeDtypeStruct((rank, rank), F32),
        ],
        compiler_params=params(),
    )(factor, gram)


def sweep_block(factor, top, bottom, part, mixed, over):
    rank = factor.shape[0]
    product = jnp.concatenate([top, bottom], axis=0)
    over = over[:, :1]
    ahead = []
    for lead in range(0, rank, STEP):
        here = slice(lead, lead + STEP)
        ahead.append(product[here] * over[here] - part[here])
    outs = []
    for b in range(rank // STEP):
        here = slice(b * STEP, (b + 1) * STEP)
        before, block, left = factor[here], mixed[here, here], ahead[b]
        news, moves = [], []
        for k in range(STEP):
            new = jnp.maximum(left[k : k + 1], EPS)
            move = new - before[k : k + 1]
            news.append(new)
            moves.append(move)
            if k + 1 < STEP:
                left = left - block[:, k : k + 1] * move
        outs.append(jnp.concatenate(news, axis=0))
        moved = jnp.concatenate(moves, axis=0)
        for c in range(b + 1, rank // STEP):
            ahead[c] -= jnp.dot(
                mixed[c * STEP : (c + 1) * STEP, here], moved, precision=HIGH, preferred_element_type=F32
            )
    return jnp.concatenate(outs, axis=0)


def sweep(factor, top, bottom, prepared, turned):
    rank, width = factor.shape

    def kernel(*refs):
        new = sweep_block(*(ref[...] for ref in refs[:-1]))
        refs[-1][...] = (jnp.transpose(new) if turned else new).astype(jnp.bfloat16)

    shape = (width, rank) if turned else (rank, width)
    return pl.pallas_call(
        kernel, out_shape=jax.ShapeDtypeStruct(shape, jnp.bfloat16), compiler_params=params()
    )(factor, top, bottom, *prepared)


def swap(x, axis, bit):
    size = lax.axis_size(axis)
    return lax.ppermute(x, axis, [(i, i ^ bit) for i in range(size)])


def bits(axis):
    bit = 1
    while bit < lax.axis_size(axis):
        yield bit
        bit *= 2


def everywhere(x, axes, combine):
    for axis in axes:
        for bit in bits(axis):
            x = combine(x, swap(x, axis, bit))
    return x


def spread(pieces, axis):
    return [
        piece if j == 0 else swap(piece, axis, j)
        for piece in pieces
        for j in range(lax.axis_size(axis))
    ]


def gather(sums, axis, up, down):
    total = sums[0]
    for j in range(1, lax.axis_size(axis)):
        total = total + swap((sums[j] * up).astype(LINK), axis, j).astype(F32) * down
    return total


def scales(gram, terms, size):
    rank = gram.shape[0]
    norm = jnp.sqrt(jnp.maximum(jnp.sum(gram * jnp.eye(rank, dtype=F32), axis=1, keepdims=True), 1e-24))
    down = norm * (terms * PEAK * size**0.5 / 32768.0)
    return [(1.0 / d, d) for d in (down[:CUT], down[CUT:])]


def local(tile_data, owner_ids, tile_spot, w_init, h_init):
    row_axes, col_axes = ("far", "core"), ("hi", "lo")
    fars, cores = lax.axis_size("far"), lax.axis_size("core")
    his, los = lax.axis_size("hi"), lax.axis_size("lo")
    rows, cols = fars * cores, his * los
    slots = rows * cols * CAP
    size, rank = tile_data.shape[1], w_init.shape[1]
    width, length = w_init.shape[0] // cols, h_init.shape[0] // rows
    my_row, my_col = lax.axis_index(row_axes), lax.axis_index(col_axes)
    core = lax.axis_index("core")
    me = jnp.stack([lax.axis_index(a) for a in row_axes + col_axes]).astype(jnp.int32)

    plane = ("far", "core", "lo")
    held = his * CAP
    outbox = pack(owner_ids[:, 0], tile_spot, tile_data, rows, his, los)
    outbox, h_init = lax.optimization_barrier((outbox, h_init))
    inbox = lax.all_to_all(outbox, plane, split_axis=0, concat_axis=0, tiled=True)
    meta = inbox[:, held * size, :held].astype(F32).astype(jnp.int32)

    h_t = h_init.T
    piece = lax.dynamic_slice_in_dim(h_t, core * (rank // 2), rank // 2, 0).astype(jnp.bfloat16)
    pieces = spread([piece], "hi")
    pieces += [swap(piece, "core", 1) for piece in pieces]

    gram_h = lax.dot_general(h_t, h_t, (((1,), (1,)), ((), ())), precision=HIGH)
    gram_h = everywhere(gram_h, col_axes, jnp.add)
    w_t = lax.dynamic_slice_in_dim(w_init, my_col * width, width, 0).T
    prepared = prepare(w_t, gram_h)
    parts = row_products(inbox, meta, me, pieces, his, los, width)
    parts, kept = parts[:2], parts[2:]
    high, low = scales(gram_h, slots * cols, size)
    top = gather(gather(parts[0], "lo", *high), "hi", *high)
    bottom = gather(gather(parts[1], "hi", *low), "lo", *low)
    w_low = sweep(w_t, top, bottom, prepared, False)
    pieces = spread(spread([w_low], "hi"), "lo")

    *parts, gram_w = column_products(inbox, kept, meta, me, pieces, his, los, fars, length)
    gram_w = everywhere(gram_w, row_axes, jnp.add)
    w_new = assemble(pieces, my_col[None].astype(jnp.int32), True)
    own_t = lax.dynamic_slice_in_dim(h_init, my_row * length, length, 0).T
    prepared = prepare(own_t, gram_w)
    high, low = scales(gram_w, slots * rows * his, size)
    bottom = parts[1] + swap(parts[3], "core", 1)
    top = parts[0] + swap(parts[2], "core", 1)
    bottom = gather(gather(bottom, "hi", *low), "far", *low)
    top = gather(top, "far", *high)
    top, w_new = lax.optimization_barrier((top, w_new))
    top = gather(top, "hi", *high)
    h_low = sweep(own_t, top, bottom, prepared, True)
    h_new = assemble(spread(spread([h_low], "far"), "core"), my_row[None].astype(jnp.int32), False)
    return w_new, h_new


def solution(mesh):
    rows, cols = mesh.shape["row"], mesh.shape["col"]
    his = 4 if cols % 4 == 0 else 1
    shape = (rows // 2, 2, his, cols // his)
    fine = Mesh(mesh.devices.reshape(shape), ("far", "core", "hi", "lo"))
    row, col = ("far", "core"), ("hi", "lo")
    in_specs = (P(row + col, None, None), P(row + col, None), P(row + col), P(row, None), P(col, None))
    out_specs = (P(row, None), P(col, None))
    return jax.shard_map(local, mesh=fine, in_specs=in_specs, out_specs=out_specs, check_vma=False)
```

time: 250 us -> 238 us (0.952)
  other arithmetic: 14.1 us -> 7.71 us
  Pallas kernels: 31.3 us -> 27.5 us
  starting transfers between devices: 50.4 us -> 47.7 us
    pallas_call x2, Pallas kernels: 20.7 us -> 14.4 us  [the longest x1 8.09 us: row_products(): pl.pallas_call(kernel, out_shape=out_shape + out_tiles, in_specs=[smem(),...]
    add x12 -> x10, other arithmetic: 7.44 us -> 4.09 us  [the longest x8 3.25 us: gather(): total + swap((sums[j] * up).astype(LINK), axis, j).astype(F32) * down]
    ppermute x40, starting transfers between devices: 45.3 us -> 42.5 us  [swap(): return lax.ppermute(x, axis, [(i, i ^ bit) for i in range(size)])]
  transfers between devices with their start and end apart: 41 -> 41, of which waited for: 21 -> 23; matrix products, arithmetic and copies ran while one was open for 8% -> 8% of each run, Pallas kernels for 1% -> 1%
where the time goes in v4:
time: 238 us; the launch traced here: 237 us
  waiting for transfers between devices  139 us (58%)
  starting transfers between devices  47.7 us (20%)
  Pallas kernels  27.5 us (12%)
  local copies, waits for them, and re-layouts  8.71 us (4%)
  other arithmetic  7.71 us (3%)
  matrix products  5.66 us (2%)
    ppermute x40, waiting for transfers between devices, swap(): return lax.ppermute(x, axis, [(i, i ^ bit) for i in range(size)])  139 us
    ppermute x40, starting transfers between devices, swap(): return lax.ppermute(x, axis, [(i, i ^ bit) for i in range(size)])  42.5 us
    pallas_call x1, Pallas kernels, row_products(): pl.pallas_call(kernel, out_shape=out_shape + out_tiles, in_specs=[smem(),...  8.09 us
    pallas_call x1, Pallas kernels, column_products(): pl.pallas_call(kernel, out_shape=[jax.ShapeDtypeStruct(shape, F32) for sh...  6.31 us
    dot_general x1, matrix products, local(): gram_h = lax.dot_general(h_t, h_t, (((1,), (1,)), ((), ())), precision=HIGH)  5.66 us
    pallas_call x1, Pallas kernels, pack(): pl.pallas_call(kernel, out_shape=jax.ShapeDtypeStruct((peers, held * size...  5.36 us
    all_to_all x1, starting transfers between devices, local(): lax.all_to_all(outbox, plane, split_axis=0, concat_axis=0, tiled=True)  5.18 us
  transfers between devices with their start and end apart: 41, of which 23 were waited for; matrix products, arithmetic and copies ran while one was open for 8% of the time, Pallas kernels for 1%

profile of v4, /device:TPU:0, one launch (start us, length us, event | category | flops | bytes accessed | tf_op | source)
XLA Modules:
  0.0 237.0 jit_solution(2365771026792353344)
XLA Ops:
  0.6 5.4 %shard_map.68 = bf16[8,2064,256]{2,1,0:T(8,128)(2,1)} custom-call(s32[32]{0:T(128)} %bitcast.147, s32[32]{0:T(128)} %spot_ref.1, bf16[32,256,256]{2,1,0:T(8,128)(2,1)} %tiles_ref.1), custom_call_target="tpu_custom_call" | custom-call | tf_op jit(solution)/shard_map/pallas_call | solution.py:68
  6.0 5.2 %all-to-all-start = ((bf16[8,2064,256]{2,1,0:T(8,128)(2,1)}), bf16[8,2064,256]{2,1,0:T(8,128)(2,1)}, u32[]{:S(2)}, u32[]{:S(2)}) async-start(bf16[8,2064,256]{2,1,0:T(8,128)(2,1)} %shard_map.68), calls=%async_computation | async-start | bytes 16908288 | tf_op jit(solution)/shard_map/all_to_all | solution.py:407
  11.2 5.7 %fusion.44 = f32[128,128]{1,0:T(8,128)S(1)} fusion(f32[4096,128]{1,0:T(8,128)} %param.9), kind=kOutput, calls=%fused_computation.82 | convolution fusion | flops 805306368 | bytes 2162688 | tf_op jit(solution)/shard_map/dot_general | solution.py:415
  16.9 2.9 %collective-permute-start.7 = (f32[128,128]{1,0:T(8,128)S(1)}, f32[128,128]{1,0:T(8,128)S(1)}, u32[]{:S(2)}, u32[]{:S(2)}) collective-permute-start(f32[128,128]{1,0:T(8,128)S(1)} %fusion.44), channel_id=1, source_target_pairs={{0,2},{2,0},{4,6},{6,4},{1,3},{3,1},{5,7},{7,5},{8,10},{10,8},{12,... | collective-permute-start | bytes 196616 | tf_op jit(solution)/shard_map/ppermute | solution.py:352
  19.8 2.9 %copy.7 = f32[4096,128]{0,1:T(8,128)} copy(f32[4096,128]{1,0:T(8,128)} %param.9) | data formatting | bytes 4194304 | tf_op jit(solution)/shard_map/optimization_barrier | solution.py:406
  24.1 2.5 %collective-permute-start.2 = (bf16[64,4096]{1,0:T(8,128)(2,1)S(1)}, bf16[64,4096]{1,0:T(8,128)(2,1)}, u32[]{:S(2)}, u32[]{:S(2)}) collective-permute-start(bf16[64,4096]{1,0:T(8,128)(2,1)S(1)} %fusion.4.refs_0_), channel_id=1, source_target_pairs={{0,6},{2,4},{4,2},{6,0},{1,7},{3,5},{5,3},{7,1},{8,14},{10,12},{12... | collective-permute-start | bytes 1572872 | tf_op jit(solution)/shard_map/ppermute | solution.py:352
  26.8 1.7 collective-permute-start
  28.5 1.8 collective-permute-start.8
  30.4 45.3 %collective-permute-done.8 = f32[128,128]{1,0:T(8,128)S(1)} collective-permute-done((f32[128,128]{1,0:T(8,128)S(1)}, f32[128,128]{1,0:T(8,128)S(1)}, u32[]{:S(2)}, u32[]{:S(2)}) %collective-permute-start.8) | collective-permute-done | bytes 65568 | tf_op jit(solution)/shard_map/ppermute | solution.py:352
  75.7 1.9 collective-permute-start.9
  77.8 28.9 %collective-permute-done.9 = f32[128,128]{1,0:T(8,128)S(1)} collective-permute-done((f32[128,128]{1,0:T(8,128)S(1)}, f32[128,128]{1,0:T(8,128)S(1)}, u32[]{:S(2)}, u32[]{:S(2)}) %collective-permute-start.9) | collective-permute-done | bytes 65568 | tf_op jit(solution)/shard_map/ppermute | solution.py:352
  112.3 8.1 %shard_map.69 = (f32[2,4,80,512]{3,2,1,0:T(8,128)S(1)}, f32[4,2,48,512]{3,2,1,0:T(8,128)S(1)}, bf16[8,2048,256]{2,1,0:T(8,128)(2,1)S(1)}) custom-call(s32[8,8]{1,0:T(8,128)S(1)} %bitcast.143, s32[4]{0:T(128)S(1)} %pad_add_fusion.me_ref, bf16[8,2064,256]{2,1,0:T(8,128)(2,1)} %all-to-all-done.inbox_ref, bf16[64,4096]{1,0:T(8,128)(2,1)S(1)} %fusion.4.refs_0_, ...), custom_call_target="tpu_custom_call" | custom-call | tf_op jit(solution)/shard_map/pallas_call | solution.py:183
  120.6 2.3 collective-permute-start.14
  122.9 2.6 %collective-permute-start.16 = (f16[2,48,512]{2,1,0:T(8,128)(2,1)S(1)}, f16[2,48,512]{2,1,0:T(8,128)(2,1)S(1)}, u32[]{:S(2)}, u32[]{:S(2)}) collective-permute-start(f16[2,48,512]{2,1,0:T(8,128)(2,1)S(1)} %get-tuple-element.49), channel_id=1, source_target_pairs={{0,6},{2,4},{4,2},{6,0},{1,7},{3,5},{5,3},{7,1},{8,14},{10,12},{12... | collective-permute-start | bytes 294920 | tf_op jit(solution)/shard_map/ppermute | solution.py:352
  126.3 5.0 %collective-permute-done.16 = f16[2,48,512]{2,1,0:T(8,128)(2,1)S(1)} collective-permute-done((f16[2,48,512]{2,1,0:T(8,128)(2,1)S(1)}, f16[2,48,512]{2,1,0:T(8,128)(2,1)S(1)}, u32[]{:S(2)}, u32[]{:S(2)}) %collective-permute-start.16) | collective-permute-done | bytes 98336 | tf_op jit(solution)/shard_map/ppermute | solution.py:352
  131.3 3.8 %collective-permute-done.15 = f16[2,48,512]{2,1,0:T(8,128)(2,1)S(1)} collective-permute-done((f16[2,48,512]{2,1,0:T(8,128)(2,1)S(1)}, f16[2,48,512]{2,1,0:T(8,128)(2,1)S(1)}, u32[]{:S(2)}, u32[]{:S(2)}) %collective-permute-start.15) | collective-permute-done | bytes 98336 | tf_op jit(solution)/shard_map/ppermute | solution.py:352
  135.7 1.4 collective-permute-start.11
  137.1 3.0 %collective-permute-start.13 = (f16[80,512]{1,0:T(8,128)(2,1)S(1)}, f16[80,512]{1,0:T(8,128)(2,1)S(1)}, u32[]{:S(2)}, u32[]{:S(2)}) collective-permute-start(f16[80,512]{1,0:T(8,128)(2,1)S(1)} %get-tuple-element.52), channel_id=1, source_target_pairs={{0,6},{2,4},{4,2},{6,0},{1,7},{3,5},{5,3},{7,1},{8,14},{10,12},{12... | collective-permute-start | bytes 245768 | tf_op jit(solution)/shard_map/ppermute | solution.py:352
  141.1 2.9 %collective-permute-done.13 = f16[80,512]{1,0:T(8,128)(2,1)S(1)} collective-permute-done((f16[80,512]{1,0:T(8,128)(2,1)S(1)}, f16[80,512]{1,0:T(8,128)(2,1)S(1)}, u32[]{:S(2)}, u32[]{:S(2)}) %collective-permute-start.13) | collective-permute-done | bytes 81952 | tf_op jit(solution)/shard_map/ppermute | solution.py:352
  143.9 2.3 collective-permute-done.12
  146.4 1.4 shard_map.71.refs_0_
  147.8 2.4 %collective-permute-start.23 = (bf16[128,512]{1,0:T(8,128)(2,1)S(1)}, bf16[128,512]{1,0:T(8,128)(2,1)S(1)}, u32[]{:S(2)}, u32[]{:S(2)}) collective-permute-start(bf16[128,512]{1,0:T(8,128)(2,1)S(1)} %shard_map.71.refs_0_), channel_id=1, source_target_pairs={{0,6},{2,4},{4,2},{6,0},{1,7},{3,5},{5,3},{7,1},{8,14},{10,12},{12... | collective-permute-start | bytes 393224 | tf_op jit(solution)/shard_map/ppermute | solution.py:352
  150.2 2.0 collective-permute-start.19
  152.3 2.0 collective-permute-start.18
  154.2 1.9 collective-permute-done.23.refs_6_
  156.1 1.9 collective-permute-start.24
  158.1 2.2 collective-permute-done.21.refs_4_
  160.2 2.1 collective-permute-start.22
  162.4 4.3 %collective-permute-done.22.refs_5_ = bf16[128,512]{1,0:T(8,128)(2,1)S(1)} collective-permute-done((bf16[128,512]{1,0:T(8,128)(2,1)S(1)}, bf16[128,512]{1,0:T(8,128)(2,1)S(1)}, u32[]{:S(2)}, u32[]{:S(2)}) %collective-permute-start.22) | collective-permute-done | bytes 131104 | tf_op jit(solution)/shard_map/ppermute | solution.py:352
  166.7 2.0 collective-permute-done.20.refs_3_
  168.7 6.3 %shard_map.72 = (f32[2,4,80,1024]{3,2,1,0:T(8,128)S(1)}, f32[4,2,48,1024]{3,2,1,0:T(8,128)S(1)}, f32[2,4,80,1024]{3,2,1,0:T(8,128)S(1)}, f32[4,2,48,1024]{3,2,1,0:T(8,128)S(1)}, f32[128,128]{1,0:T(8,128)S(1)}) custom-call(s32[8,8]{1,0:T(8,128)S(1)} %bitcast.144, s32[4]{0:T(128)S(1)} %pad_add_fusion.me_ref, ...), custom_call_target="tpu_custom_call" | custom-call | tf_op jit(solution)/shard_map/pallas_call | solution.py:253
  176.0 3.9 %collective-permute-done.26 = f32[128,128]{1,0:T(8,128)S(1)} collective-permute-done((f32[128,128]{1,0:T(8,128)S(1)}, f32[128,128]{1,0:T(8,128)S(1)}, u32[]{:S(2)}, u32[]{:S(2)}) %collective-permute-start.26) | collective-permute-done | bytes 65568 | tf_op jit(solution)/shard_map/ppermute | solution.py:352
  179.9 2.4 %collective-permute-done.27 = f32[128,128]{1,0:T(8,128)S(1)} collective-permute-done((f32[128,128]{1,0:T(8,128)S(1)}, f32[128,128]{1,0:T(8,128)S(1)}, u32[]{:S(2)}, u32[]{:S(2)}) %collective-permute-start.27) | collective-permute-done | bytes 65568 | tf_op jit(solution)/shard_map/ppermute | solution.py:352
  183.7 2.3 collective-permute-start.35
  187.8 1.5 copy-done.4
  191.1 1.7 shard_map.73
  193.4 3.0 %collective-permute-done.35 = f16[2,48,1024]{2,1,0:T(8,128)(2,1)} collective-permute-done((f16[2,48,1024]{2,1,0:T(8,128)(2,1)}, f16[2,48,1024]{2,1,0:T(8,128)(2,1)}, u32[]{:S(2)}, u32[]{:S(2)}) %collective-permute-start.35) | collective-permute-done | bytes 196640 | tf_op jit(solution)/shard_map/ppermute | solution.py:352
  196.4 8.4 %collective-permute-done.34 = f16[2,48,1024]{2,1,0:T(8,128)(2,1)} collective-permute-done((f16[2,48,1024]{2,1,0:T(8,128)(2,1)}, f16[2,48,1024]{2,1,0:T(8,128)(2,1)}, u32[]{:S(2)}, u32[]{:S(2)}) %collective-permute-start.34) | collective-permute-done | bytes 196640 | tf_op jit(solution)/shard_map/ppermute | solution.py:352
  206.6 1.3 fusion.2
  208.4 2.0 collective-permute-start.31
  211.8 3.3 %collective-permute-done.29 = f16[80,1024]{1,0:T(8,128)(2,1)S(1)} collective-permute-done((f16[80,1024]{1,0:T(8,128)(2,1)S(1)}, f16[80,1024]{1,0:T(8,128)(2,1)S(1)}, u32[]{:S(2)}, u32[]{:S(2)}) %collective-permute-start.29) | collective-permute-done | bytes 163872 | tf_op jit(solution)/shard_map/ppermute | solution.py:352
  215.1 3.3 %collective-permute-done.31 = f16[80,1024]{1,0:T(8,128)(2,1)S(1)} collective-permute-done((f16[80,1024]{1,0:T(8,128)(2,1)S(1)}, f16[80,1024]{1,0:T(8,128)(2,1)S(1)}, u32[]{:S(2)}, u32[]{:S(2)}) %collective-permute-start.31) | collective-permute-done | bytes 163872 | tf_op jit(solution)/shard_map/ppermute | solution.py:352
  218.4 6.3 %collective-permute-done.30 = f16[80,1024]{1,0:T(8,128)(2,1)S(1)} collective-permute-done((f16[80,1024]{1,0:T(8,128)(2,1)S(1)}, f16[80,1024]{1,0:T(8,128)(2,1)S(1)}, u32[]{:S(2)}, u32[]{:S(2)}) %collective-permute-start.30) | collective-permute-done | bytes 163872 | tf_op jit(solution)/shard_map/ppermute | solution.py:352
  224.9 2.2 shard_map.75.refs_0_
  227.1 1.7 collective-permute-start.38
  228.8 5.3 %collective-permute-done.38.refs_2_ = bf16[1024,128]{1,0:T(8,128)(2,1)S(1)} collective-permute-done((bf16[1024,128]{1,0:T(8,128)(2,1)S(1)}, bf16[1024,128]{1,0:T(8,128)(2,1)S(1)}, u32[]{:S(2)}, u32[]{:S(2)}) %collective-permute-start.38) | collective-permute-done | bytes 262176 | tf_op jit(solution)/shard_map/ppermute | solution.py:352
  234.1 1.5 collective-permute-done.39.refs_3_
  235.6 1.5 shard_map.76
  (94 shorter events, 20.3 us)
Async XLA Ops:
  0.6 29.7 %copy-start = (f32[4096,128]{1,0:T(8,128)S(1)}, f32[4096,128]{1,0:T(8,128)}, u32[]{:S(2)}) copy-start(f32[4096,128]{1,0:T(8,128)} %param.8) | copy-start | bytes 6291460
  6.0 102.6 %all-to-all-start = ((bf16[8,2064,256]{2,1,0:T(8,128)(2,1)}), bf16[8,2064,256]{2,1,0:T(8,128)(2,1)}, u32[]{:S(2)}, u32[]{:S(2)}) async-start(bf16[8,2064,256]{2,1,0:T(8,128)(2,1)} %shard_map.68), calls=%async_computation | async-start | bytes 16908288 | tf_op jit(solution)/shard_map/all_to_all | solution.py:407
  16.9 11.6 %collective-permute-start.7 = (f32[128,128]{1,0:T(8,128)S(1)}, f32[128,128]{1,0:T(8,128)S(1)}, u32[]{:S(2)}, u32[]{:S(2)}) collective-permute-start(f32[128,128]{1,0:T(8,128)S(1)} %fusion.44), channel_id=1, source_target_pairs={{0,2},{2,0},{4,6},{6,4},{1,3},{3,1},{5,7},{7,5},{8,10},{10,8},{12,... | collective-permute-start | bytes 196616 | tf_op jit(solution)/shard_map/ppermute | solution.py:352
  24.0 85.4 %collective-permute-start.3 = (bf16[64,4096]{1,0:T(8,128)(2,1)S(1)}, bf16[64,4096]{1,0:T(8,128)(2,1)S(1)}, u32[]{:S(2)}, u32[]{:S(2)}) collective-permute-start(bf16[64,4096]{1,0:T(8,128)(2,1)S(1)} %fusion.4.refs_0_), channel_id=1, source_target_pairs={{0,8},{8,0},{1,9},{9,1},{2,10},{10,2},{3,11},{11,3},{4,12},{12,4},... | collective-permute-start | bytes 1572872 | tf_op jit(solution)/shard_map/ppermute | solution.py:352
  24.1 82.7 %collective-permute-start.2 = (bf16[64,4096]{1,0:T(8,128)(2,1)S(1)}, bf16[64,4096]{1,0:T(8,128)(2,1)}, u32[]{:S(2)}, u32[]{:S(2)}) collective-permute-start(bf16[64,4096]{1,0:T(8,128)(2,1)S(1)} %fusion.4.refs_0_), channel_id=1, source_target_pairs={{0,6},{2,4},{4,2},{6,0},{1,7},{3,5},{5,3},{7,1},{8,14},{10,12},{12... | collective-permute-start | bytes 1572872 | tf_op jit(solution)/shard_map/ppermute | solution.py:352
  26.6 80.3 %collective-permute-start.1 = (bf16[64,4096]{1,0:T(8,128)(2,1)S(1)}, bf16[64,4096]{1,0:T(8,128)(2,1)}, u32[]{:S(2)}, u32[]{:S(2)}) collective-permute-start(bf16[64,4096]{1,0:T(8,128)(2,1)S(1)} %fusion.4.refs_0_), channel_id=1, source_target_pairs={{0,4},{2,6},{4,0},{6,2},{1,5},{3,7},{5,1},{7,3},{8,12},{10,14},{12... | collective-permute-start | bytes 1572872 | tf_op jit(solution)/shard_map/ppermute | solution.py:352
  26.8 80.6 %collective-permute-start = (bf16[64,4096]{1,0:T(8,128)(2,1)S(1)}, bf16[64,4096]{1,0:T(8,128)(2,1)}, u32[]{:S(2)}, u32[]{:S(2)}) collective-permute-start(bf16[64,4096]{1,0:T(8,128)(2,1)S(1)} %fusion.4.refs_0_), channel_id=1, source_target_pairs={{0,2},{2,0},{4,6},{6,4},{1,3},{3,1},{5,7},{7,5},{8,10},{10,8},{12,... | collective-permute-start | bytes 1572872 | tf_op jit(solution)/shard_map/ppermute | solution.py:352
  28.5 47.2 %collective-permute-start.8 = (f32[128,128]{1,0:T(8,128)S(1)}, f32[128,128]{1,0:T(8,128)S(1)}, u32[]{:S(2)}, u32[]{:S(2)}) collective-permute-start(f32[128,128]{1,0:T(8,128)S(1)} %add.87), channel_id=1, source_target_pairs={{0,4},{2,6},{4,0},{6,2},{1,5},{3,7},{5,1},{7,3},{8,12},{10,14},{12... | collective-permute-start | bytes 196616 | tf_op jit(solution)/shard_map/ppermute | solution.py:352
  75.7 30.9 %collective-permute-start.9 = (f32[128,128]{1,0:T(8,128)S(1)}, f32[128,128]{1,0:T(8,128)S(1)}, u32[]{:S(2)}, u32[]{:S(2)}) collective-permute-start(f32[128,128]{1,0:T(8,128)S(1)} %add.88), channel_id=1, source_target_pairs={{0,1},{1,0},{2,3},{3,2},{4,5},{5,4},{6,7},{7,6},{8,9},{9,8},{10,11... | collective-permute-start | bytes 196616 | tf_op jit(solution)/shard_map/ppermute | solution.py:352
  106.8 2.5 %collective-permute-start.6 = (bf16[64,4096]{1,0:T(8,128)(2,1)}, bf16[64,4096]{1,0:T(8,128)(2,1)S(1)}, u32[]{:S(2)}, u32[]{:S(2)}) collective-permute-start(bf16[64,4096]{1,0:T(8,128)(2,1)} %collective-permute-done.2.refs_3_), channel_id=1, source_target_pairs={{0,8},{8,0},{1,9},{9,1},{2,10},{10,2},{3,11},{11,3},{4,12},{12,4},... | collective-permute-start | bytes 1572872 | tf_op jit(solution)/shard_map/ppermute | solution.py:352
  106.9 2.8 %collective-permute-start.5 = (bf16[64,4096]{1,0:T(8,128)(2,1)}, bf16[64,4096]{1,0:T(8,128)(2,1)S(1)}, u32[]{:S(2)}, u32[]{:S(2)}) collective-permute-start(bf16[64,4096]{1,0:T(8,128)(2,1)} %collective-permute-done.1.refs_2_), channel_id=1, source_target_pairs={{0,8},{8,0},{1,9},{9,1},{2,10},{10,2},{3,11},{11,3},{4,12},{12,4},... | collective-permute-start | bytes 1572872 | tf_op jit(solution)/shard_map/ppermute | solution.py:352
  107.4 3.1 %collective-permute-start.4 = (bf16[64,4096]{1,0:T(8,128)(2,1)}, bf16[64,4096]{1,0:T(8,128)(2,1)S(1)}, u32[]{:S(2)}, u32[]{:S(2)}) collective-permute-start(bf16[64,4096]{1,0:T(8,128)(2,1)} %collective-permute-done.refs_1_), channel_id=1, source_target_pairs={{0,8},{8,0},{1,9},{9,1},{2,10},{10,2},{3,11},{11,3},{4,12},{12,4},... | collective-permute-start | bytes 1572872 | tf_op jit(solution)/shard_map/ppermute | solution.py:352
  110.5 0.8 copy-start.2
  111.3 1.0 copy-start.3
  120.4 15.0 %copy-start.6 = (f32[80]{0:T(128)S(1)}, f32[80]{0:T(128)}, u32[]{:S(2)}) copy-start(f32[80]{0:T(128)} %get-tuple-element.60) | copy-start | bytes 964
  120.6 5.7 %collective-permute-start.14 = (f16[2,48,512]{2,1,0:T(8,128)(2,1)S(1)}, f16[2,48,512]{2,1,0:T(8,128)(2,1)S(1)}, u32[]{:S(2)}, u32[]{:S(2)}) collective-permute-start(f16[2,48,512]{2,1,0:T(8,128)(2,1)S(1)} %get-tuple-element.48), channel_id=1, source_target_pairs={{0,2},{2,0},{4,6},{6,4},{1,3},{3,1},{5,7},{7,5},{8,10},{10,8},{12,... | collective-permute-start | bytes 294920 | tf_op jit(solution)/shard_map/ppermute | solution.py:352
  122.9 8.4 %collective-permute-start.16 = (f16[2,48,512]{2,1,0:T(8,128)(2,1)S(1)}, f16[2,48,512]{2,1,0:T(8,128)(2,1)S(1)}, u32[]{:S(2)}, u32[]{:S(2)}) collective-permute-start(f16[2,48,512]{2,1,0:T(8,128)(2,1)S(1)} %get-tuple-element.49), channel_id=1, source_target_pairs={{0,6},{2,4},{4,2},{6,0},{1,7},{3,5},{5,3},{7,1},{8,14},{10,12},{12... | collective-permute-start | bytes 294920 | tf_op jit(solution)/shard_map/ppermute | solution.py:352
  125.5 9.6 %collective-permute-start.15 = (f16[2,48,512]{2,1,0:T(8,128)(2,1)S(1)}, f16[2,48,512]{2,1,0:T(8,128)(2,1)S(1)}, u32[]{:S(2)}, u32[]{:S(2)}) collective-permute-start(f16[2,48,512]{2,1,0:T(8,128)(2,1)S(1)} %get-tuple-element.50), channel_id=1, source_target_pairs={{0,4},{2,6},{4,0},{6,2},{1,5},{3,7},{5,1},{7,3},{8,12},{10,14},{12... | collective-permute-start | bytes 294920 | tf_op jit(solution)/shard_map/ppermute | solution.py:352
  125.7 9.7 %collective-permute-start.10 = (f16[4,80,512]{2,1,0:T(8,128)(2,1)S(1)}, f16[4,80,512]{2,1,0:T(8,128)(2,1)S(1)}, u32[]{:S(2)}, u32[]{:S(2)}) collective-permute-start(f16[4,80,512]{2,1,0:T(8,128)(2,1)S(1)} %fusion.3), channel_id=1, source_target_pairs={{0,1},{1,0},{2,3},{3,2},{4,5},{5,4},{6,7},{7,6},{8,9},{9,8},{10,11... | collective-permute-start | bytes 983048 | tf_op jit(solution)/shard_map/ppermute | solution.py:352
  135.3 4.8 %collective-permute-start.17 = (f16[48,512]{1,0:T(8,128)(2,1)S(1)}, f16[48,512]{1,0:T(8,128)(2,1)S(1)}, u32[]{:S(2)}, u32[]{:S(2)}) collective-permute-start(f16[48,512]{1,0:T(8,128)(2,1)S(1)} %fusion.37), channel_id=1, source_target_pairs={{0,1},{1,0},{2,3},{3,2},{4,5},{5,4},{6,7},{7,6},{8,9},{9,8},{10,11... | collective-permute-start | bytes 147464 | tf_op jit(solution)/shard_map/ppermute | solution.py:352
  135.7 5.4 %collective-permute-start.11 = (f16[80,512]{1,0:T(8,128)(2,1)S(1)}, f16[80,512]{1,0:T(8,128)(2,1)S(1)}, u32[]{:S(2)}, u32[]{:S(2)}) collective-permute-start(f16[80,512]{1,0:T(8,128)(2,1)S(1)} %get-tuple-element.51), channel_id=1, source_target_pairs={{0,2},{2,0},{4,6},{6,4},{1,3},{3,1},{5,7},{7,5},{8,10},{10,8},{12,... | collective-permute-start | bytes 245768 | tf_op jit(solution)/shard_map/ppermute | solution.py:352
  137.1 6.9 %collective-permute-start.13 = (f16[80,512]{1,0:T(8,128)(2,1)S(1)}, f16[80,512]{1,0:T(8,128)(2,1)S(1)}, u32[]{:S(2)}, u32[]{:S(2)}) collective-permute-start(f16[80,512]{1,0:T(8,128)(2,1)S(1)} %get-tuple-element.52), channel_id=1, source_target_pairs={{0,6},{2,4},{4,2},{6,0},{1,7},{3,5},{5,3},{7,1},{8,14},{10,12},{12... | collective-permute-start | bytes 245768 | tf_op jit(solution)/shard_map/ppermute | solution.py:352
  140.1 6.2 %collective-permute-start.12 = (f16[80,512]{1,0:T(8,128)(2,1)S(1)}, f16[80,512]{1,0:T(8,128)(2,1)S(1)}, u32[]{:S(2)}, u32[]{:S(2)}) collective-permute-start(f16[80,512]{1,0:T(8,128)(2,1)S(1)} %get-tuple-element.53), channel_id=1, source_target_pairs={{0,4},{2,6},{4,0},{6,2},{1,5},{3,7},{5,1},{7,3},{8,12},{10,14},{12... | collective-permute-start | bytes 245768 | tf_op jit(solution)/shard_map/ppermute | solution.py:352
  147.8 8.3 %collective-permute-start.23 = (bf16[128,512]{1,0:T(8,128)(2,1)S(1)}, bf16[128,512]{1,0:T(8,128)(2,1)S(1)}, u32[]{:S(2)}, u32[]{:S(2)}) collective-permute-start(bf16[128,512]{1,0:T(8,128)(2,1)S(1)} %shard_map.71.refs_0_), channel_id=1, source_target_pairs={{0,6},{2,4},{4,2},{6,0},{1,7},{3,5},{5,3},{7,1},{8,14},{10,12},{12... | collective-permute-start | bytes 393224 | tf_op jit(solution)/shard_map/ppermute | solution.py:352
  150.2 10.0 %collective-permute-start.21 = (bf16[128,512]{1,0:T(8,128)(2,1)S(1)}, bf16[128,512]{1,0:T(8,128)(2,1)S(1)}, u32[]{:S(2)}, u32[]{:S(2)}) collective-permute-start(bf16[128,512]{1,0:T(8,128)(2,1)S(1)} %shard_map.71.refs_0_), channel_id=1, source_target_pairs={{0,4},{2,6},{4,0},{6,2},{1,5},{3,7},{5,1},{7,3},{8,12},{10,14},{12... | collective-permute-start | bytes 393224 | tf_op jit(solution)/shard_map/ppermute | solution.py:352
  150.2 12.1 %collective-permute-start.19 = (bf16[128,512]{1,0:T(8,128)(2,1)S(1)}, bf16[128,512]{1,0:T(8,128)(2,1)S(1)}, u32[]{:S(2)}, u32[]{:S(2)}) collective-permute-start(bf16[128,512]{1,0:T(8,128)(2,1)S(1)} %shard_map.71.refs_0_), channel_id=1, source_target_pairs={{0,2},{2,0},{4,6},{6,4},{1,3},{3,1},{5,7},{7,5},{8,10},{10,8},{12,... | collective-permute-start | bytes 393224 | tf_op jit(solution)/shard_map/ppermute | solution.py:352
  152.3 10.1 %collective-permute-start.18 = (bf16[128,512]{1,0:T(8,128)(2,1)S(1)}, bf16[128,512]{1,0:T(8,128)(2,1)S(1)}, u32[]{:S(2)}, u32[]{:S(2)}) collective-permute-start(bf16[128,512]{1,0:T(8,128)(2,1)S(1)} %shard_map.71.refs_0_), channel_id=1, source_target_pairs={{0,1},{1,0},{2,3},{3,2},{4,5},{5,4},{6,7},{7,6},{8,9},{9,8},{10,11... | collective-permute-start | bytes 393224 | tf_op jit(solution)/shard_map/ppermute | solution.py:352
  156.1 6.2 %collective-permute-start.24 = (bf16[128,512]{1,0:T(8,128)(2,1)S(1)}, bf16[128,512]{1,0:T(8,128)(2,1)S(1)}, u32[]{:S(2)}, u32[]{:S(2)}) collective-permute-start(bf16[128,512]{1,0:T(8,128)(2,1)S(1)} %collective-permute-done.23.refs_6_), channel_id=1, source_target_pairs={{0,1},{1,0},{2,3},{3,2},{4,5},{5,4},{6,7},{7,6},{8,9},{9,8},{10,11... | collective-permute-start | bytes 393224 | tf_op jit(solution)/shard_map/ppermute | solution.py:352
  160.2 6.4 %collective-permute-start.22 = (bf16[128,512]{1,0:T(8,128)(2,1)S(1)}, bf16[128,512]{1,0:T(8,128)(2,1)S(1)}, u32[]{:S(2)}, u32[]{:S(2)}) collective-permute-start(bf16[128,512]{1,0:T(8,128)(2,1)S(1)} %collective-permute-done.21.refs_4_), channel_id=1, source_target_pairs={{0,1},{1,0},{2,3},{3,2},{4,5},{5,4},{6,7},{7,6},{8,9},{9,8},{10,11... | collective-permute-start | bytes 393224 | tf_op jit(solution)/shard_map/ppermute | solution.py:352
  162.3 6.3 %collective-permute-start.20 = (bf16[128,512]{1,0:T(8,128)(2,1)S(1)}, bf16[128,512]{1,0:T(8,128)(2,1)S(1)}, u32[]{:S(2)}, u32[]{:S(2)}) collective-permute-start(bf16[128,512]{1,0:T(8,128)(2,1)S(1)} %collective-permute-done.19.refs_2_), channel_id=1, source_target_pairs={{0,1},{1,0},{2,3},{3,2},{4,5},{5,4},{6,7},{7,6},{8,9},{9,8},{10,11... | collective-permute-start | bytes 393224 | tf_op jit(solution)/shard_map/ppermute | solution.py:352
  175.0 12.3 %collective-permute-start.25 = (f32[2,4,80,1024]{3,2,1,0:T(8,128)S(1)}, f32[2,4,80,1024]{3,2,1,0:T(8,128)S(1)}, u32[]{:S(2)}, u32[]{:S(2)}) collective-permute-start(f32[2,4,80,1024]{3,2,1,0:T(8,128)S(1)} %get-tuple-element.29), channel_id=1, source_target_pairs={{0,8},{8,0},{1,9},{9,1},{2,10},{10,2},{3,11},{11,3},{4,12},{12,4},... | collective-permute-start | bytes 7864328 | tf_op jit(solution)/shard_map/ppermute | solution.py:352
  175.1 7.4 %collective-permute-start.32 = (f32[4,2,48,1024]{3,2,1,0:T(8,128)S(1)}, f32[4,2,48,1024]{3,2,1,0:T(8,128)S(1)}, u32[]{:S(2)}, u32[]{:S(2)}) collective-permute-start(f32[4,2,48,1024]{3,2,1,0:T(8,128)S(1)} %get-tuple-element.34), channel_id=1, source_target_pairs={{0,8},{8,0},{1,9},{9,1},{2,10},{10,2},{3,11},{11,3},{4,12},{12,4},... | collective-permute-start | bytes 4718600 | tf_op jit(solution)/shard_map/ppermute | solution.py:352
  175.6 4.3 %collective-permute-start.26 = (f32[128,128]{1,0:T(8,128)S(1)}, f32[128,128]{1,0:T(8,128)S(1)}, u32[]{:S(2)}, u32[]{:S(2)}) collective-permute-start(f32[128,128]{1,0:T(8,128)S(1)} %get-tuple-element.30), channel_id=1, source_target_pairs={{0,16},{16,0},{1,17},{17,1},{2,18},{18,2},{3,19},{19,3},{4,20},{20... | collective-permute-start | bytes 196616 | tf_op jit(solution)/shard_map/ppermute | solution.py:352
  179.8 2.5 %collective-permute-start.27 = (f32[128,128]{1,0:T(8,128)S(1)}, f32[128,128]{1,0:T(8,128)S(1)}, u32[]{:S(2)}, u32[]{:S(2)}) collective-permute-start(f32[128,128]{1,0:T(8,128)S(1)} %add.99), channel_id=1, source_target_pairs={{0,8},{8,0},{1,9},{9,1},{2,10},{10,2},{3,11},{11,3},{4,12},{12,4},... | collective-permute-start | bytes 196616 | tf_op jit(solution)/shard_map/ppermute | solution.py:352
  183.7 9.6 %collective-permute-start.33 = (f16[2,48,1024]{2,1,0:T(8,128)(2,1)}, f16[2,48,1024]{2,1,0:T(8,128)(2,1)S(1)}, u32[]{:S(2)}, u32[]{:S(2)}) collective-permute-start(f16[2,48,1024]{2,1,0:T(8,128)(2,1)} %get-tuple-element.42), channel_id=1, source_target_pairs={{0,2},{2,0},{4,6},{6,4},{1,3},{3,1},{5,7},{7,5},{8,10},{10,8},{12,... | collective-permute-start | bytes 589832 | tf_op jit(solution)/shard_map/ppermute | solution.py:352
  183.7 12.7 %collective-permute-start.35 = (f16[2,48,1024]{2,1,0:T(8,128)(2,1)}, f16[2,48,1024]{2,1,0:T(8,128)(2,1)}, u32[]{:S(2)}, u32[]{:S(2)}) collective-permute-start(f16[2,48,1024]{2,1,0:T(8,128)(2,1)} %get-tuple-element.43), channel_id=1, source_target_pairs={{0,6},{2,4},{4,2},{6,0},{1,7},{3,5},{5,3},{7,1},{8,14},{10,12},{12... | collective-permute-start | bytes 589832 | tf_op jit(solution)/shard_map/ppermute | solution.py:352
  186.1 18.8 %collective-permute-start.34 = (f16[2,48,1024]{2,1,0:T(8,128)(2,1)}, f16[2,48,1024]{2,1,0:T(8,128)(2,1)}, u32[]{:S(2)}, u32[]{:S(2)}) collective-permute-start(f16[2,48,1024]{2,1,0:T(8,128)(2,1)} %get-tuple-element.44), channel_id=1, source_target_pairs={{0,4},{2,6},{4,0},{6,2},{1,5},{3,7},{5,1},{7,3},{8,12},{10,14},{12... | collective-permute-start | bytes 589832 | tf_op jit(solution)/shard_map/ppermute | solution.py:352
  187.8 1.5 copy-start.4
  189.5 17.1 %collective-permute-start.28 = (f16[4,80,1024]{2,1,0:T(8,128)(2,1)S(1)}, f16[4,80,1024]{2,1,0:T(8,128)(2,1)}, u32[]{:S(2)}, u32[]{:S(2)}) collective-permute-start(f16[4,80,1024]{2,1,0:T(8,128)(2,1)S(1)} %fusion.1), channel_id=1, source_target_pairs={{0,16},{16,0},{1,17},{17,1},{2,18},{18,2},{3,19},{19,3},{4,20},{20... | collective-permute-start | bytes 1966088 | tf_op jit(solution)/shard_map/ppermute | solution.py:352
  191.1 15.5 %copy-start.5 = (f32[2,4,80,1024]{3,2,1,0:T(8,128)S(1)}, f32[2,4,80,1024]{3,2,1,0:T(8,128)}, u32[]{:S(2)}) copy-start(f32[2,4,80,1024]{3,2,1,0:T(8,128)} %copy-done.4) | copy-start | bytes 7864324
  206.1 5.5 %collective-permute-start.36 = (f16[48,1024]{1,0:T(8,128)(2,1)S(1)}, f16[48,1024]{1,0:T(8,128)(2,1)S(1)}, u32[]{:S(2)}, u32[]{:S(2)}) collective-permute-start(f16[48,1024]{1,0:T(8,128)(2,1)S(1)} %fusion.20), channel_id=1, source_target_pairs={{0,16},{16,0},{1,17},{17,1},{2,18},{18,2},{3,19},{19,3},{4,20},{20... | collective-permute-start | bytes 294920 | tf_op jit(solution)/shard_map/ppermute | solution.py:352
  208.1 7.0 %collective-permute-start.29 = (f16[80,1024]{1,0:T(8,128)(2,1)S(1)}, f16[80,1024]{1,0:T(8,128)(2,1)S(1)}, u32[]{:S(2)}, u32[]{:S(2)}) collective-permute-start(f16[80,1024]{1,0:T(8,128)(2,1)S(1)} %get-tuple-element.45), channel_id=1, source_target_pairs={{0,2},{2,0},{4,6},{6,4},{1,3},{3,1},{5,7},{7,5},{8,10},{10,8},{12,... | collective-permute-start | bytes 491528 | tf_op jit(solution)/shard_map/ppermute | solution.py:352
  208.4 10.1 %collective-permute-start.31 = (f16[80,1024]{1,0:T(8,128)(2,1)S(1)}, f16[80,1024]{1,0:T(8,128)(2,1)S(1)}, u32[]{:S(2)}, u32[]{:S(2)}) collective-permute-start(f16[80,1024]{1,0:T(8,128)(2,1)S(1)} %get-tuple-element.46), channel_id=1, source_target_pairs={{0,6},{2,4},{4,2},{6,0},{1,7},{3,5},{5,3},{7,1},{8,14},{10,12},{12... | collective-permute-start | bytes 491528 | tf_op jit(solution)/shard_map/ppermute | solution.py:352
  210.4 14.3 %collective-permute-start.30 = (f16[80,1024]{1,0:T(8,128)(2,1)S(1)}, f16[80,1024]{1,0:T(8,128)(2,1)S(1)}, u32[]{:S(2)}, u32[]{:S(2)}) collective-permute-start(f16[80,1024]{1,0:T(8,128)(2,1)S(1)} %get-tuple-element.47), channel_id=1, source_target_pairs={{0,4},{2,6},{4,0},{6,2},{1,5},{3,7},{5,1},{7,3},{8,12},{10,14},{12... | collective-permute-start | bytes 491528 | tf_op jit(solution)/shard_map/ppermute | solution.py:352
  224.9 12.2 %copy-start.1 = (f32[4096,128]{1,0:T(8,128)S(1)}, f32[4096,128]{1,0:T(8,128)}, u32[]{:S(2)}) copy-start(f32[4096,128]{1,0:T(8,128)} %param.8) | copy-start | bytes 6291460
  227.1 7.0 %collective-permute-start.38 = (bf16[1024,128]{1,0:T(8,128)(2,1)S(1)}, bf16[1024,128]{1,0:T(8,128)(2,1)S(1)}, u32[]{:S(2)}, u32[]{:S(2)}) collective-permute-start(bf16[1024,128]{1,0:T(8,128)(2,1)S(1)} %shard_map.75.refs_0_), channel_id=1, source_target_pairs={{0,16},{16,0},{1,17},{17,1},{2,18},{18,2},{3,19},{19,3},{4,20},{20... | collective-permute-start | bytes 786440 | tf_op jit(solution)/shard_map/ppermute | solution.py:352
  228.7 5.3 %collective-permute-start.37 = (bf16[1024,128]{1,0:T(8,128)(2,1)S(1)}, bf16[1024,128]{1,0:T(8,128)(2,1)S(1)}, u32[]{:S(2)}, u32[]{:S(2)}) collective-permute-start(bf16[1024,128]{1,0:T(8,128)(2,1)S(1)} %shard_map.75.refs_0_), channel_id=1, source_target_pairs={{0,8},{8,0},{1,9},{9,1},{2,10},{10,2},{3,11},{11,3},{4,12},{12,4},... | collective-permute-start | bytes 786440 | tf_op jit(solution)/shard_map/ppermute | solution.py:352
  234.0 1.5 collective-permute-start.39

commit v5 on v4

--- a/solution.py
+++ b/solution.py
@@ -17,7 +17,7 @@
 DEPTH = 8
 PEAK = 256.0
 CUT = 80
-VMEM_LIMIT = 32 * 2**20
+VMEM_LIMIT = 24 * 2**20
 
 
 def params(limit=VMEM_LIMIT):
@@ -183,7 +183,7 @@
     return pl.pallas_call(
         kernel,
         out_shape=out_shape + out_tiles,
-        in_specs=[smem(), smem(), hbm()] + [hbm()] * len(pieces),
+        in_specs=[smem(), smem(), hbm()] + [vmem()] * len(pieces),
         out_specs=[vmem()] * (2 + keep),
         scratch_shapes=([] if keep else [pltpu.VMEM(tiles, inbox.dtype)])
         + [
@@ -203,8 +203,8 @@
     chunks = his * los
 
     def kernel(meta_ref, me_ref, source_ref, *refs):
-        piece_refs, outs, gram_ref = refs[:chunks], refs[chunks : chunks + 4], refs[chunks + 4]
-        panel_ref, terms_ref, *rest = refs[chunks + 5 :]
+        piece_refs, outs = refs[:chunks], refs[chunks : chunks + 4]
+        panel_ref, terms_ref, *rest = refs[chunks + 4 :]
         tiles_ref, sems = (source_ref, None) if kept else rest
         my_far, my_core, my_hi, my_lo = (me_ref[i] for i in range(4))
 
@@ -218,7 +218,14 @@
                 gram += lax.dot_general(
                     piece, piece, (((1,), (1,)), ((), ())), preferred_element_type=F32
                 )
-            gram_ref[...] = gram
+            shape = (rank, rank)
+            diag = lax.broadcasted_iota(jnp.int32, shape, 0) == lax.broadcasted_iota(jnp.int32, shape, 1)
+            norms = jnp.sum(jnp.where(diag, gram, 0.0), axis=1, keepdims=True)[CUT:]
+            lines = rank * rank // out_width
+            for out in (outs[1], outs[3]):
+                out[his * fars] = jnp.broadcast_to(norms, out.shape[1:])
+                for j in range(rank // lines):
+                    out[his * fars + 1, :lines, j * rank : (j + 1) * rank] = gram[j * lines : (j + 1) * lines]
 
         def product(slot, spot, tile):
             trow = spot // CT
@@ -237,12 +244,12 @@
                 @pl.when((owner ^ my_core) % 2 == side)
                 def _():
                     top_ref[far, hi, :, place] += terms_ref[slot, :CUT]
-                    bot_ref[hi, far, :, place] += terms_ref[slot, CUT:]
+                    bot_ref[hi * fars + far, :, place] += terms_ref[slot, CUT:]
 
         each_tile(meta_ref, source_ref, tiles_ref, terms_ref, sems, product, add, ready)
 
-    tops, bots = (fars, his, CUT, out_width), (his, fars, rank - CUT, out_width)
-    out_shape = [tops, bots, tops, bots, (rank, rank)]
+    tops, bots = (fars, his, CUT, out_width), (his * fars + 2, rank - CUT, out_width)
+    out_shape = [tops, bots, tops, bots]
     scratch = [
         pltpu.VMEM((chunks, rank, width), jnp.bfloat16),
         pltpu.VMEM((held, rank, size), F32),
@@ -267,7 +274,7 @@
     def kernel(place_ref, *refs):
         for j in range(count):
             piece = refs[j][...].astype(F32)
-            refs[count][j ^ place_ref[0]] = jnp.transpose(piece) if turned else piece
+            refs[-1][j ^ place_ref[0]] = jnp.transpose(piece) if turned else piece
 
     return pl.pallas_call(
         kernel,
@@ -381,10 +388,13 @@
     return total
 
 
+def bound(squares, terms, size):
+    return jnp.sqrt(jnp.maximum(squares, 1e-24)) * (terms * PEAK * size**0.5 / 32768.0)
+
+
 def scales(gram, terms, size):
     rank = gram.shape[0]
-    norm = jnp.sqrt(jnp.maximum(jnp.sum(gram * jnp.eye(rank, dtype=F32), axis=1, keepdims=True), 1e-24))
-    down = norm * (terms * PEAK * size**0.5 / 32768.0)
+    down = bound(jnp.sum(gram * jnp.eye(rank, dtype=F32), axis=1, keepdims=True), terms, size)
     return [(1.0 / d, d) for d in (down[:CUT], down[CUT:])]
 
 
@@ -410,11 +420,15 @@
     h_t = h_init.T
     piece = lax.dynamic_slice_in_dim(h_t, core * (rank // 2), rank // 2, 0).astype(jnp.bfloat16)
     pieces = spread([piece], "hi")
+    w_t = lax.dynamic_slice_in_dim(w_init, my_col * width, width, 0).T
+    own_t = lax.dynamic_slice_in_dim(h_init, my_row * length, length, 0).T
+    w_t, own_t, *pieces = lax.optimization_barrier((w_t, own_t, *pieces))
     pieces += [swap(piece, "core", 1) for piece in pieces]
 
     gram_h = lax.dot_general(h_t, h_t, (((1,), (1,)), ((), ())), precision=HIGH)
-    gram_h = everywhere(gram_h, col_axes, jnp.add)
-    w_t = lax.dynamic_slice_in_dim(w_init, my_col * width, width, 0).T
+    gram_h = everywhere(gram_h, ("hi",), jnp.add)
+    gram_h, meta, *pieces = lax.optimization_barrier((gram_h, meta, *pieces))
+    gram_h = everywhere(gram_h, ("lo",), jnp.add)
     prepared = prepare(w_t, gram_h)
     parts = row_products(inbox, meta, me, pieces, his, los, width)
     parts, kept = parts[:2], parts[2:]
@@ -424,20 +438,28 @@
     w_low = sweep(w_t, top, bottom, prepared, False)
     pieces = spread(spread([w_low], "hi"), "lo")
 
-    *parts, gram_w = column_products(inbox, kept, meta, me, pieces, his, los, fars, length)
-    gram_w = everywhere(gram_w, row_axes, jnp.add)
-    w_new = assemble(pieces, my_col[None].astype(jnp.int32), True)
-    own_t = lax.dynamic_slice_in_dim(h_init, my_row * length, length, 0).T
+    parts = column_products(inbox, kept, meta, me, pieces, his, los, fars, length)
+
+    bottom = parts[1] + swap(parts[3], "core", 1)
+    bottom, away = lax.optimization_barrier((bottom, parts[2]))
+    top = parts[0] + swap(away, "core", 1)
+    lines = rank * rank // length
+    gram_w = bottom[-1, :lines].reshape(lines, length // rank, rank)
+    gram_w = gram_w.transpose(1, 0, 2).reshape(rank, rank)
+    gram_w = everywhere(gram_w, ("far",), jnp.add)
     prepared = prepare(own_t, gram_w)
     high, low = scales(gram_w, slots * rows * his, size)
-    bottom = parts[1] + swap(parts[3], "core", 1)
-    top = parts[0] + swap(parts[2], "core", 1)
-    bottom = gather(gather(bottom, "hi", *low), "far", *low)
-    top = gather(top, "far", *high)
-    top, w_new = lax.optimization_barrier((top, w_new))
-    top = gather(top, "hi", *high)
+    down = bound(bottom[-2], slots * 2, size)
+    bottom = bottom[:-2].reshape(his, fars, *bottom.shape[1:])
+    bottom = gather(bottom, "hi", 1.0 / down, down)
+    bottom = gather(bottom, "far", *low)
+    top = gather(gather(top, "far", *high), "hi", *high)
     h_low = sweep(own_t, top, bottom, prepared, True)
-    h_new = assemble(spread(spread([h_low], "far"), "core"), my_row[None].astype(jnp.int32), False)
+    h_low, *pieces = lax.optimization_barrier((h_low, *pieces))
+    w_new = assemble(pieces, my_col[None].astype(jnp.int32), True)
+    pieces = spread([h_low], "far")
+    pieces[0], w_new = lax.optimization_barrier((pieces[0], w_new))
+    h_new = assemble(spread(pieces, "core"), my_row[None].astype(jnp.int32), False)
     return w_new, h_new
 
 

time: 238 us -> 230 us (0.966)
  starting transfers between devices: 47.7 us -> 43.4 us
  other arithmetic: 7.71 us -> 4.36 us
    all_to_all x1, waiting for transfers between devices: 0.01 us -> 23.2 us  [local(): lax.all_to_all(outbox, plane, split_axis=0, concat_axis=0, tiled=True)]
    ppermute x40 -> x39, waiting for transfers between devices: 139 us -> 117 us  [swap(): return lax.ppermute(x, axis, [(i, i ^ bit) for i in range(size)])]
    ppermute x40 -> x39, starting transfers between devices: 42.5 us -> 38.2 us  [swap(): return lax.ppermute(x, axis, [(i, i ^ bit) for i in range(size)])]
  transfers between devices with their start and end apart: 41 -> 40, of which waited for: 23 -> 24; matrix products, arithmetic and copies ran while one was open for 8% -> 6% of each run, Pallas kernels for 1% -> 5%
where the time goes in v5:
time: 230 us; the launch traced here: 229 us
  waiting for transfers between devices  140 us (61%)
  starting transfers between devices  43.4 us (19%)
  Pallas kernels  27.7 us (12%)
  local copies, waits for them, and re-layouts  7.27 us (3%)
  matrix products  5.66 us (2%)
  other arithmetic  4.36 us (2%)
    ppermute x39, waiting for transfers between devices, swap(): return lax.ppermute(x, axis, [(i, i ^ bit) for i in range(size)])  117 us
    ppermute x39, starting transfers between devices, swap(): return lax.ppermute(x, axis, [(i, i ^ bit) for i in range(size)])  38.2 us
    all_to_all x1, waiting for transfers between devices, local(): lax.all_to_all(outbox, plane, split_axis=0, concat_axis=0, tiled=True)  23.2 us
    pallas_call x1, Pallas kernels, row_products(): pl.pallas_call(kernel, out_shape=out_shape + out_tiles, in_specs=[smem(),...  8.5 us
    pallas_call x1, Pallas kernels, column_products(): pl.pallas_call(kernel, out_shape=[jax.ShapeDtypeStruct(shape, F32) for sh...  6.01 us
    dot_general x1, matrix products, local(): gram_h = lax.dot_general(h_t, h_t, (((1,), (1,)), ((), ())), precision=HIGH)  5.66 us
    pallas_call x1, Pallas kernels, pack(): pl.pallas_call(kernel, out_shape=jax.ShapeDtypeStruct((peers, held * size...  5.37 us
    all_to_all x1, starting transfers between devices, local(): lax.all_to_all(outbox, plane, split_axis=0, concat_axis=0, tiled=True)  5.18 us
  transfers between devices with their start and end apart: 40, of which 24 were waited for; matrix products, arithmetic and copies ran while one was open for 6% of the time, Pallas kernels for 5%

profile of v5, /device:TPU:0, one launch (start us, length us, event | category | flops | bytes accessed | tf_op | source)
XLA Modules:
  0.0 229.4 jit_solution(5166208803135801302)
XLA Ops:
  0.6 5.4 %shard_map.68 = bf16[8,2064,256]{2,1,0:T(8,128)(2,1)} custom-call(s32[32]{0:T(128)} %bitcast.144, s32[32]{0:T(128)} %spot_ref.1, bf16[32,256,256]{2,1,0:T(8,128)(2,1)} %tiles_ref.1), custom_call_target="tpu_custom_call" | custom-call | tf_op jit(solution)/shard_map/pallas_call | solution.py:68
  6.0 5.2 %all-to-all-start = ((bf16[8,2064,256]{2,1,0:T(8,128)(2,1)}), bf16[8,2064,256]{2,1,0:T(8,128)(2,1)}, u32[]{:S(2)}, u32[]{:S(2)}) async-start(bf16[8,2064,256]{2,1,0:T(8,128)(2,1)} %shard_map.68), calls=%async_computation | async-start | bytes 16908288 | tf_op jit(solution)/shard_map/all_to_all | solution.py:417
  11.2 2.9 %copy.8 = f32[4096,128]{0,1:T(8,128)} copy(f32[4096,128]{1,0:T(8,128)} %param.9) | data formatting | bytes 4194304 | tf_op jit(solution)/shard_map/optimization_barrier | solution.py:416
  14.1 1.3 fusion.4.refs_0_
  15.4 5.0 %collective-permute-start.2 = (bf16[64,4096]{1,0:T(8,128)(2,1)S(1)}, bf16[64,4096]{1,0:T(8,128)(2,1)S(1)}, u32[]{:S(2)}, u32[]{:S(2)}) collective-permute-start(bf16[64,4096]{1,0:T(8,128)(2,1)S(1)} %fusion.4.refs_0_), channel_id=1, source_target_pairs={{0,6},{2,4},{4,2},{6,0},{1,7},{3,5},{5,3},{7,1},{8,14},{10,12},{12... | collective-permute-start | bytes 1572872 | tf_op jit(solution)/shard_map/ppermute | solution.py:359
  22.2 11.0 %collective-permute-done.2.refs_3_ = bf16[64,4096]{1,0:T(8,128)(2,1)S(1)} collective-permute-done((bf16[64,4096]{1,0:T(8,128)(2,1)S(1)}, bf16[64,4096]{1,0:T(8,128)(2,1)S(1)}, u32[]{:S(2)}, u32[]{:S(2)}) %collective-permute-start.2) | collective-permute-done | bytes 524320 | tf_op jit(solution)/shard_map/ppermute | solution.py:359
  33.2 32.5 %collective-permute-done.1.refs_2_ = bf16[64,4096]{1,0:T(8,128)(2,1)} collective-permute-done((bf16[64,4096]{1,0:T(8,128)(2,1)S(1)}, bf16[64,4096]{1,0:T(8,128)(2,1)}, u32[]{:S(2)}, u32[]{:S(2)}) %collective-permute-start.1) | collective-permute-done | bytes 524320 | tf_op jit(solution)/shard_map/ppermute | solution.py:359
  66.8 5.7 %fusion.40 = f32[128,128]{1,0:T(8,128)S(1)} fusion(f32[4096,128]{1,0:T(8,128)} %param.9), kind=kOutput, calls=%fused_computation.82 | convolution fusion | flops 805306368 | bytes 2162688 | tf_op jit(solution)/shard_map/dot_general | solution.py:428
  72.5 4.3 %collective-permute-done.3 = f32[128,128]{1,0:T(8,128)S(1)} collective-permute-done((f32[128,128]{1,0:T(8,128)S(1)}, f32[128,128]{1,0:T(8,128)S(1)}, u32[]{:S(2)}, u32[]{:S(2)}) %collective-permute-start.3) | collective-permute-done | bytes 65568 | tf_op jit(solution)/shard_map/ppermute | solution.py:359
  77.9 4.4 %collective-permute-done.4 = f32[128,128]{1,0:T(8,128)S(1)} collective-permute-done((f32[128,128]{1,0:T(8,128)S(1)}, f32[128,128]{1,0:T(8,128)S(1)}, u32[]{:S(2)}, u32[]{:S(2)}) %collective-permute-start.4) | collective-permute-done | bytes 65568 | tf_op jit(solution)/shard_map/ppermute | solution.py:359
  82.3 23.2 %all-to-all-done.inbox_ref = bf16[8,2064,256]{2,1,0:T(8,128)(2,1)} async-done(((bf16[8,2064,256]{2,1,0:T(8,128)(2,1)}), bf16[8,2064,256]{2,1,0:T(8,128)(2,1)}, u32[]{:S(2)}, u32[]{:S(2)}) %all-to-all-start) | async-done | bytes 8454176 | tf_op jit(solution)/shard_map/all_to_all | solution.py:417
  107.1 1.6 collective-permute-start.9
  109.8 8.5 %shard_map.69 = (f32[2,4,80,512]{3,2,1,0:T(8,128)S(1)}, f32[4,2,48,512]{3,2,1,0:T(8,128)S(1)}, bf16[8,2048,256]{2,1,0:T(8,128)(2,1)S(1)}) custom-call(s32[8,8]{1,0:T(8,128)S(1)} %bitcast.138, s32[4]{0:T(128)S(1)} %pad_add_fusion.me_ref, bf16[8,2064,256]{2,1,0:T(8,128)(2,1)} %all-to-all-done.inbox_ref, bf16[64,4096]{1,0:T(8,128)(2,1)S(1)} %fusion.4.refs_0_, ...), custom_call_target="tpu_custom_call" | custom-call | tf_op jit(solution)/shard_map/pallas_call | solution.py:183
  118.6 2.4 %collective-permute-start.14 = (f16[2,48,512]{2,1,0:T(8,128)(2,1)S(1)}, f16[2,48,512]{2,1,0:T(8,128)(2,1)S(1)}, u32[]{:S(2)}, u32[]{:S(2)}) collective-permute-start(f16[2,48,512]{2,1,0:T(8,128)(2,1)S(1)} %get-tuple-element.102), channel_id=1, source_target_pairs={{0,2},{2,0},{4,6},{6,4},{1,3},{3,1},{5,7},{7,5},{8,10},{10,8},{12,... | collective-permute-start | bytes 294920 | tf_op jit(solution)/shard_map/ppermute | solution.py:359
  121.0 2.4 %collective-permute-start.16 = (f16[2,48,512]{2,1,0:T(8,128)(2,1)S(1)}, f16[2,48,512]{2,1,0:T(8,128)(2,1)S(1)}, u32[]{:S(2)}, u32[]{:S(2)}) collective-permute-start(f16[2,48,512]{2,1,0:T(8,128)(2,1)S(1)} %get-tuple-element.103), channel_id=1, source_target_pairs={{0,6},{2,4},{4,2},{6,0},{1,7},{3,5},{5,3},{7,1},{8,14},{10,12},{12... | collective-permute-start | bytes 294920 | tf_op jit(solution)/shard_map/ppermute | solution.py:359
  124.7 3.8 %collective-permute-done.16 = f16[2,48,512]{2,1,0:T(8,128)(2,1)S(1)} collective-permute-done((f16[2,48,512]{2,1,0:T(8,128)(2,1)S(1)}, f16[2,48,512]{2,1,0:T(8,128)(2,1)S(1)}, u32[]{:S(2)}, u32[]{:S(2)}) %collective-permute-start.16) | collective-permute-done | bytes 98336 | tf_op jit(solution)/shard_map/ppermute | solution.py:359
  128.5 3.3 %collective-permute-done.15 = f16[2,48,512]{2,1,0:T(8,128)(2,1)S(1)} collective-permute-done((f16[2,48,512]{2,1,0:T(8,128)(2,1)S(1)}, f16[2,48,512]{2,1,0:T(8,128)(2,1)S(1)}, u32[]{:S(2)}, u32[]{:S(2)}) %collective-permute-start.15) | collective-permute-done | bytes 98336 | tf_op jit(solution)/shard_map/ppermute | solution.py:359
  132.0 1.6 collective-permute-start.17
  133.9 2.8 %collective-permute-start.13 = (f16[80,512]{1,0:T(8,128)(2,1)S(1)}, f16[80,512]{1,0:T(8,128)(2,1)S(1)}, u32[]{:S(2)}, u32[]{:S(2)}) collective-permute-start(f16[80,512]{1,0:T(8,128)(2,1)S(1)} %get-tuple-element.106), channel_id=1, source_target_pairs={{0,6},{2,4},{4,2},{6,0},{1,7},{3,5},{5,3},{7,1},{8,14},{10,12},{12... | collective-permute-start | bytes 245768 | tf_op jit(solution)/shard_map/ppermute | solution.py:359
  137.5 1.9 collective-permute-done.11
  139.4 2.1 collective-permute-done.13
  141.4 3.0 %collective-permute-done.12 = f16[80,512]{1,0:T(8,128)(2,1)S(1)} collective-permute-done((f16[80,512]{1,0:T(8,128)(2,1)S(1)}, f16[80,512]{1,0:T(8,128)(2,1)S(1)}, u32[]{:S(2)}, u32[]{:S(2)}) %collective-permute-start.12) | collective-permute-done | bytes 81952 | tf_op jit(solution)/shard_map/ppermute | solution.py:359
  144.5 1.4 shard_map.71.refs_0_
  145.9 2.0 collective-permute-start.23
  148.0 2.4 %collective-permute-start.19 = (bf16[128,512]{1,0:T(8,128)(2,1)S(1)}, bf16[128,512]{1,0:T(8,128)(2,1)S(1)}, u32[]{:S(2)}, u32[]{:S(2)}) collective-permute-start(bf16[128,512]{1,0:T(8,128)(2,1)S(1)} %shard_map.71.refs_0_), channel_id=1, source_target_pairs={{0,2},{2,0},{4,6},{6,4},{1,3},{3,1},{5,7},{7,5},{8,10},{10,8},{12,... | collective-permute-start | bytes 393224 | tf_op jit(solution)/shard_map/ppermute | solution.py:359
  150.6 3.7 %collective-permute-done.23.refs_6_ = bf16[128,512]{1,0:T(8,128)(2,1)S(1)} collective-permute-done((bf16[128,512]{1,0:T(8,128)(2,1)S(1)}, bf16[128,512]{1,0:T(8,128)(2,1)S(1)}, u32[]{:S(2)}, u32[]{:S(2)}) %collective-permute-start.23) | collective-permute-done | bytes 131104 | tf_op jit(solution)/shard_map/ppermute | solution.py:359
  154.4 4.1 %collective-permute-done.21.refs_4_ = bf16[128,512]{1,0:T(8,128)(2,1)S(1)} collective-permute-done((bf16[128,512]{1,0:T(8,128)(2,1)S(1)}, bf16[128,512]{1,0:T(8,128)(2,1)S(1)}, u32[]{:S(2)}, u32[]{:S(2)}) %collective-permute-start.21) | collective-permute-done | bytes 131104 | tf_op jit(solution)/shard_map/ppermute | solution.py:359
  158.5 2.0 collective-permute-start.20
  160.6 4.2 %collective-permute-done.22.refs_5_ = bf16[128,512]{1,0:T(8,128)(2,1)S(1)} collective-permute-done((bf16[128,512]{1,0:T(8,128)(2,1)S(1)}, bf16[128,512]{1,0:T(8,128)(2,1)S(1)}, u32[]{:S(2)}, u32[]{:S(2)}) %collective-permute-start.22) | collective-permute-done | bytes 131104 | tf_op jit(solution)/shard_map/ppermute | solution.py:359
  164.8 1.4 collective-permute-done.20.refs_3_
  166.2 6.0 %shard_map.72 = (f32[2,4,80,1024]{3,2,1,0:T(8,128)S(1)}, f32[10,48,1024]{2,1,0:T(8,128)S(1)}, f32[2,4,80,1024]{3,2,1,0:T(8,128)S(1)}, f32[10,48,1024]{2,1,0:T(8,128)S(1)}) custom-call(s32[8,8]{1,0:T(8,128)S(1)} %bitcast.139, s32[4]{0:T(128)S(1)} %pad_add_fusion.me_ref, bf16[8,2048,256]{2,1,0:T(8,128)(2,1)S(1)} %get-tuple-element.62.source_ref, ...), custom_call_target="tpu_custom_call" | custom-call | tf_op jit(solution)/shard_map/pallas_call | solution.py:260
  172.3 4.0 %collective-permute-done.25 = f32[10,48,1024]{2,1,0:T(8,128)S(1)} collective-permute-done((f32[10,48,1024]{2,1,0:T(8,128)S(1)}, f32[10,48,1024]{2,1,0:T(8,128)S(1)}, u32[]{:S(2)}, u32[]{:S(2)}) %collective-permute-start.25) | collective-permute-done | bytes 1966112 | tf_op jit(solution)/shard_map/ppermute | solution.py:359
  177.7 1.8 collective-permute-start.34
  179.5 1.2 collective-permute-start.33
  182.8 1.5 collective-permute-start.28
  184.7 4.8 %collective-permute-done.34 = f16[2,48,1024]{2,1,0:T(8,128)(2,1)S(1)} collective-permute-done((f16[2,48,1024]{2,1,0:T(8,128)(2,1)S(1)}, f16[2,48,1024]{2,1,0:T(8,128)(2,1)S(1)}, u32[]{:S(2)}, u32[]{:S(2)}) %collective-permute-start.34) | collective-permute-done | bytes 196640 | tf_op jit(solution)/shard_map/ppermute | solution.py:359
  189.5 8.7 %collective-permute-done.33 = f16[2,48,1024]{2,1,0:T(8,128)(2,1)S(1)} collective-permute-done((f16[2,48,1024]{2,1,0:T(8,128)(2,1)S(1)}, f16[2,48,1024]{2,1,0:T(8,128)(2,1)S(1)}, u32[]{:S(2)}, u32[]{:S(2)}) %collective-permute-start.33) | collective-permute-done | bytes 196640 | tf_op jit(solution)/shard_map/ppermute | solution.py:359
  198.5 1.8 collective-permute-start.35
  200.8 2.0 collective-permute-start.31
  202.8 1.5 collective-permute-start.30
  204.4 3.4 %collective-permute-done.29 = f16[80,1024]{1,0:T(8,128)(2,1)S(1)} collective-permute-done((f16[80,1024]{1,0:T(8,128)(2,1)S(1)}, f16[80,1024]{1,0:T(8,128)(2,1)S(1)}, u32[]{:S(2)}, u32[]{:S(2)}) %collective-permute-start.29) | collective-permute-done | bytes 163872 | tf_op jit(solution)/shard_map/ppermute | solution.py:359
  207.8 3.1 %collective-permute-done.31 = f16[80,1024]{1,0:T(8,128)(2,1)S(1)} collective-permute-done((f16[80,1024]{1,0:T(8,128)(2,1)S(1)}, f16[80,1024]{1,0:T(8,128)(2,1)S(1)}, u32[]{:S(2)}, u32[]{:S(2)}) %collective-permute-start.31) | collective-permute-done | bytes 163872 | tf_op jit(solution)/shard_map/ppermute | solution.py:359
  211.0 6.3 %collective-permute-done.30 = f16[80,1024]{1,0:T(8,128)(2,1)S(1)} collective-permute-done((f16[80,1024]{1,0:T(8,128)(2,1)S(1)}, f16[80,1024]{1,0:T(8,128)(2,1)S(1)}, u32[]{:S(2)}, u32[]{:S(2)}) %collective-permute-start.30) | collective-permute-done | bytes 163872 | tf_op jit(solution)/shard_map/ppermute | solution.py:359
  217.4 2.2 shard_map.74.refs_0_
  220.3 1.7 shard_map.75
  222.0 4.5 %collective-permute-done.37.refs_2_ = bf16[1024,128]{1,0:T(8,128)(2,1)S(1)} collective-permute-done((bf16[1024,128]{1,0:T(8,128)(2,1)S(1)}, bf16[1024,128]{1,0:T(8,128)(2,1)S(1)}, u32[]{:S(2)}, u32[]{:S(2)}) %collective-permute-start.37) | collective-permute-done | bytes 262176 | tf_op jit(solution)/shard_map/ppermute | solution.py:359
  226.5 1.5 collective-permute-done.38.refs_3_
  228.0 1.5 shard_map.76
  (89 shorter events, 15.7 us)
Async XLA Ops:
  0.6 20.3 %copy-start = (f32[4096,128]{1,0:T(8,128)S(1)}, f32[4096,128]{1,0:T(8,128)}, u32[]{:S(2)}) copy-start(f32[4096,128]{1,0:T(8,128)} %param.8) | copy-start | bytes 6291460
  6.0 99.5 %all-to-all-start = ((bf16[8,2064,256]{2,1,0:T(8,128)(2,1)}), bf16[8,2064,256]{2,1,0:T(8,128)(2,1)}, u32[]{:S(2)}, u32[]{:S(2)}) async-start(bf16[8,2064,256]{2,1,0:T(8,128)(2,1)} %shard_map.68), calls=%async_computation | async-start | bytes 16908288 | tf_op jit(solution)/shard_map/all_to_all | solution.py:417
  15.4 17.9 %collective-permute-start.2 = (bf16[64,4096]{1,0:T(8,128)(2,1)S(1)}, bf16[64,4096]{1,0:T(8,128)(2,1)S(1)}, u32[]{:S(2)}, u32[]{:S(2)}) collective-permute-start(bf16[64,4096]{1,0:T(8,128)(2,1)S(1)} %fusion.4.refs_0_), channel_id=1, source_target_pairs={{0,6},{2,4},{4,2},{6,0},{1,7},{3,5},{5,3},{7,1},{8,14},{10,12},{12... | collective-permute-start | bytes 1572872 | tf_op jit(solution)/shard_map/ppermute | solution.py:359
  20.3 45.4 %collective-permute-start.1 = (bf16[64,4096]{1,0:T(8,128)(2,1)S(1)}, bf16[64,4096]{1,0:T(8,128)(2,1)}, u32[]{:S(2)}, u32[]{:S(2)}) collective-permute-start(bf16[64,4096]{1,0:T(8,128)(2,1)S(1)} %fusion.4.refs_0_), channel_id=1, source_target_pairs={{0,4},{2,6},{4,0},{6,2},{1,5},{3,7},{5,1},{7,3},{8,12},{10,14},{12... | collective-permute-start | bytes 1572872 | tf_op jit(solution)/shard_map/ppermute | solution.py:359
  20.3 45.4 %collective-permute-start = (bf16[64,4096]{1,0:T(8,128)(2,1)S(1)}, bf16[64,4096]{1,0:T(8,128)(2,1)}, u32[]{:S(2)}, u32[]{:S(2)}) collective-permute-start(bf16[64,4096]{1,0:T(8,128)(2,1)S(1)} %fusion.4.refs_0_), channel_id=1, source_target_pairs={{0,2},{2,0},{4,6},{6,4},{1,3},{3,1},{5,7},{7,5},{8,10},{10,8},{12,... | collective-permute-start | bytes 1572872 | tf_op jit(solution)/shard_map/ppermute | solution.py:359
  65.7 40.5 %collective-permute-start.5 = (bf16[64,4096]{1,0:T(8,128)(2,1)S(1)}, bf16[64,4096]{1,0:T(8,128)(2,1)S(1)}, u32[]{:S(2)}, u32[]{:S(2)}) collective-permute-start(bf16[64,4096]{1,0:T(8,128)(2,1)S(1)} %fusion.4.refs_0_), channel_id=1, source_target_pairs={{0,8},{8,0},{1,9},{9,1},{2,10},{10,2},{3,11},{11,3},{4,12},{12,4},... | collective-permute-start | bytes 1572872 | tf_op jit(solution)/shard_map/ppermute | solution.py:359
  65.7 40.5 %collective-permute-start.6 = (bf16[64,4096]{1,0:T(8,128)(2,1)}, bf16[64,4096]{1,0:T(8,128)(2,1)S(1)}, u32[]{:S(2)}, u32[]{:S(2)}) collective-permute-start(bf16[64,4096]{1,0:T(8,128)(2,1)} %collective-permute-done.refs_1_), channel_id=1, source_target_pairs={{0,8},{8,0},{1,9},{9,1},{2,10},{10,2},{3,11},{11,3},{4,12},{12,4},... | collective-permute-start | bytes 1572872 | tf_op jit(solution)/shard_map/ppermute | solution.py:359
  66.3 40.8 %collective-permute-start.7 = (bf16[64,4096]{1,0:T(8,128)(2,1)}, bf16[64,4096]{1,0:T(8,128)(2,1)}, u32[]{:S(2)}, u32[]{:S(2)}) collective-permute-start(bf16[64,4096]{1,0:T(8,128)(2,1)} %collective-permute-done.1.refs_2_), channel_id=1, source_target_pairs={{0,8},{8,0},{1,9},{9,1},{2,10},{10,2},{3,11},{11,3},{4,12},{12,4},... | collective-permute-start | bytes 1572872 | tf_op jit(solution)/shard_map/ppermute | solution.py:359
  66.3 40.8 %collective-permute-start.8 = (bf16[64,4096]{1,0:T(8,128)(2,1)S(1)}, bf16[64,4096]{1,0:T(8,128)(2,1)}, u32[]{:S(2)}, u32[]{:S(2)}) collective-permute-start(bf16[64,4096]{1,0:T(8,128)(2,1)S(1)} %collective-permute-done.2.refs_3_), channel_id=1, source_target_pairs={{0,8},{8,0},{1,9},{9,1},{2,10},{10,2},{3,11},{11,3},{4,12},{12,4},... | collective-permute-start | bytes 1572872 | tf_op jit(solution)/shard_map/ppermute | solution.py:359
  72.4 4.3 %collective-permute-start.3 = (f32[128,128]{1,0:T(8,128)S(1)}, f32[128,128]{1,0:T(8,128)S(1)}, u32[]{:S(2)}, u32[]{:S(2)}) collective-permute-start(f32[128,128]{1,0:T(8,128)S(1)} %fusion.40), channel_id=1, source_target_pairs={{0,2},{2,0},{4,6},{6,4},{1,3},{3,1},{5,7},{7,5},{8,10},{10,8},{12,... | collective-permute-start | bytes 196616 | tf_op jit(solution)/shard_map/ppermute | solution.py:359
  76.8 5.5 %collective-permute-start.4 = (f32[128,128]{1,0:T(8,128)S(1)}, f32[128,128]{1,0:T(8,128)S(1)}, u32[]{:S(2)}, u32[]{:S(2)}) collective-permute-start(f32[128,128]{1,0:T(8,128)S(1)} %add.86), channel_id=1, source_target_pairs={{0,4},{2,6},{4,0},{6,2},{1,5},{3,7},{5,1},{7,3},{8,12},{10,14},{12... | collective-permute-start | bytes 196616 | tf_op jit(solution)/shard_map/ppermute | solution.py:359
  106.3 0.8 copy-start.2
  107.1 11.2 %collective-permute-start.9 = (f32[128,128]{1,0:T(8,128)S(1)}, f32[128,128]{1,0:T(8,128)S(1)}, u32[]{:S(2)}, u32[]{:S(2)}) collective-permute-start(f32[128,128]{1,0:T(8,128)S(1)} %add.87), channel_id=1, source_target_pairs={{0,1},{1,0},{2,3},{3,2},{4,5},{5,4},{6,7},{7,6},{8,9},{9,8},{10,11... | collective-permute-start | bytes 196616 | tf_op jit(solution)/shard_map/ppermute | solution.py:359
  108.7 1.0 copy-start.3
  118.6 6.0 %collective-permute-start.14 = (f16[2,48,512]{2,1,0:T(8,128)(2,1)S(1)}, f16[2,48,512]{2,1,0:T(8,128)(2,1)S(1)}, u32[]{:S(2)}, u32[]{:S(2)}) collective-permute-start(f16[2,48,512]{2,1,0:T(8,128)(2,1)S(1)} %get-tuple-element.102), channel_id=1, source_target_pairs={{0,2},{2,0},{4,6},{6,4},{1,3},{3,1},{5,7},{7,5},{8,10},{10,8},{12,... | collective-permute-start | bytes 294920 | tf_op jit(solution)/shard_map/ppermute | solution.py:359
  121.0 7.5 %collective-permute-start.16 = (f16[2,48,512]{2,1,0:T(8,128)(2,1)S(1)}, f16[2,48,512]{2,1,0:T(8,128)(2,1)S(1)}, u32[]{:S(2)}, u32[]{:S(2)}) collective-permute-start(f16[2,48,512]{2,1,0:T(8,128)(2,1)S(1)} %get-tuple-element.103), channel_id=1, source_target_pairs={{0,6},{2,4},{4,2},{6,0},{1,7},{3,5},{5,3},{7,1},{8,14},{10,12},{12... | collective-permute-start | bytes 294920 | tf_op jit(solution)/shard_map/ppermute | solution.py:359
  123.4 8.4 %collective-permute-start.15 = (f16[2,48,512]{2,1,0:T(8,128)(2,1)S(1)}, f16[2,48,512]{2,1,0:T(8,128)(2,1)S(1)}, u32[]{:S(2)}, u32[]{:S(2)}) collective-permute-start(f16[2,48,512]{2,1,0:T(8,128)(2,1)S(1)} %get-tuple-element.104), channel_id=1, source_target_pairs={{0,4},{2,6},{4,0},{6,2},{1,5},{3,7},{5,1},{7,3},{8,12},{10,14},{12... | collective-permute-start | bytes 294920 | tf_op jit(solution)/shard_map/ppermute | solution.py:359
  123.7 9.9 %collective-permute-start.10 = (f16[4,80,512]{2,1,0:T(8,128)(2,1)S(1)}, f16[4,80,512]{2,1,0:T(8,128)(2,1)S(1)}, u32[]{:S(2)}, u32[]{:S(2)}) collective-permute-start(f16[4,80,512]{2,1,0:T(8,128)(2,1)S(1)} %fusion.3), channel_id=1, source_target_pairs={{0,1},{1,0},{2,3},{3,2},{4,5},{5,4},{6,7},{7,6},{8,9},{9,8},{10,11... | collective-permute-start | bytes 983048 | tf_op jit(solution)/shard_map/ppermute | solution.py:359
  132.0 5.4 %collective-permute-start.17 = (f16[48,512]{1,0:T(8,128)(2,1)S(1)}, f16[48,512]{1,0:T(8,128)(2,1)S(1)}, u32[]{:S(2)}, u32[]{:S(2)}) collective-permute-start(f16[48,512]{1,0:T(8,128)(2,1)S(1)} %fusion.33), channel_id=1, source_target_pairs={{0,1},{1,0},{2,3},{3,2},{4,5},{5,4},{6,7},{7,6},{8,9},{9,8},{10,11... | collective-permute-start | bytes 147464 | tf_op jit(solution)/shard_map/ppermute | solution.py:359
  133.8 5.5 %collective-permute-start.11 = (f16[80,512]{1,0:T(8,128)(2,1)S(1)}, f16[80,512]{1,0:T(8,128)(2,1)S(1)}, u32[]{:S(2)}, u32[]{:S(2)}) collective-permute-start(f16[80,512]{1,0:T(8,128)(2,1)S(1)} %get-tuple-element.105), channel_id=1, source_target_pairs={{0,2},{2,0},{4,6},{6,4},{1,3},{3,1},{5,7},{7,5},{8,10},{10,8},{12,... | collective-permute-start | bytes 245768 | tf_op jit(solution)/shard_map/ppermute | solution.py:359
  133.9 7.5 %collective-permute-start.13 = (f16[80,512]{1,0:T(8,128)(2,1)S(1)}, f16[80,512]{1,0:T(8,128)(2,1)S(1)}, u32[]{:S(2)}, u32[]{:S(2)}) collective-permute-start(f16[80,512]{1,0:T(8,128)(2,1)S(1)} %get-tuple-element.106), channel_id=1, source_target_pairs={{0,6},{2,4},{4,2},{6,0},{1,7},{3,5},{5,3},{7,1},{8,14},{10,12},{12... | collective-permute-start | bytes 245768 | tf_op jit(solution)/shard_map/ppermute | solution.py:359
  136.7 7.6 %collective-permute-start.12 = (f16[80,512]{1,0:T(8,128)(2,1)S(1)}, f16[80,512]{1,0:T(8,128)(2,1)S(1)}, u32[]{:S(2)}, u32[]{:S(2)}) collective-permute-start(f16[80,512]{1,0:T(8,128)(2,1)S(1)} %get-tuple-element.107), channel_id=1, source_target_pairs={{0,4},{2,6},{4,0},{6,2},{1,5},{3,7},{5,1},{7,3},{8,12},{10,14},{12... | collective-permute-start | bytes 245768 | tf_op jit(solution)/shard_map/ppermute | solution.py:359
  145.9 8.3 %collective-permute-start.23 = (bf16[128,512]{1,0:T(8,128)(2,1)S(1)}, bf16[128,512]{1,0:T(8,128)(2,1)S(1)}, u32[]{:S(2)}, u32[]{:S(2)}) collective-permute-start(bf16[128,512]{1,0:T(8,128)(2,1)S(1)} %shard_map.71.refs_0_), channel_id=1, source_target_pairs={{0,6},{2,4},{4,2},{6,0},{1,7},{3,5},{5,3},{7,1},{8,14},{10,12},{12... | collective-permute-start | bytes 393224 | tf_op jit(solution)/shard_map/ppermute | solution.py:359
  148.0 10.6 %collective-permute-start.21 = (bf16[128,512]{1,0:T(8,128)(2,1)S(1)}, bf16[128,512]{1,0:T(8,128)(2,1)S(1)}, u32[]{:S(2)}, u32[]{:S(2)}) collective-permute-start(bf16[128,512]{1,0:T(8,128)(2,1)S(1)} %shard_map.71.refs_0_), channel_id=1, source_target_pairs={{0,4},{2,6},{4,0},{6,2},{1,5},{3,7},{5,1},{7,3},{8,12},{10,14},{12... | collective-permute-start | bytes 393224 | tf_op jit(solution)/shard_map/ppermute | solution.py:359
  148.0 10.6 %collective-permute-start.19 = (bf16[128,512]{1,0:T(8,128)(2,1)S(1)}, bf16[128,512]{1,0:T(8,128)(2,1)S(1)}, u32[]{:S(2)}, u32[]{:S(2)}) collective-permute-start(bf16[128,512]{1,0:T(8,128)(2,1)S(1)} %shard_map.71.refs_0_), channel_id=1, source_target_pairs={{0,2},{2,0},{4,6},{6,4},{1,3},{3,1},{5,7},{7,5},{8,10},{10,8},{12,... | collective-permute-start | bytes 393224 | tf_op jit(solution)/shard_map/ppermute | solution.py:359
  150.4 10.2 %collective-permute-start.18 = (bf16[128,512]{1,0:T(8,128)(2,1)S(1)}, bf16[128,512]{1,0:T(8,128)(2,1)S(1)}, u32[]{:S(2)}, u32[]{:S(2)}) collective-permute-start(bf16[128,512]{1,0:T(8,128)(2,1)S(1)} %shard_map.71.refs_0_), channel_id=1, source_target_pairs={{0,1},{1,0},{2,3},{3,2},{4,5},{5,4},{6,7},{7,6},{8,9},{9,8},{10,11... | collective-permute-start | bytes 393224 | tf_op jit(solution)/shard_map/ppermute | solution.py:359
  154.2 6.3 %collective-permute-start.24 = (bf16[128,512]{1,0:T(8,128)(2,1)S(1)}, bf16[128,512]{1,0:T(8,128)(2,1)S(1)}, u32[]{:S(2)}, u32[]{:S(2)}) collective-permute-start(bf16[128,512]{1,0:T(8,128)(2,1)S(1)} %collective-permute-done.23.refs_6_), channel_id=1, source_target_pairs={{0,1},{1,0},{2,3},{3,2},{4,5},{5,4},{6,7},{7,6},{8,9},{9,8},{10,11... | collective-permute-start | bytes 393224 | tf_op jit(solution)/shard_map/ppermute | solution.py:359
  158.5 6.3 %collective-permute-start.22 = (bf16[128,512]{1,0:T(8,128)(2,1)S(1)}, bf16[128,512]{1,0:T(8,128)(2,1)S(1)}, u32[]{:S(2)}, u32[]{:S(2)}) collective-permute-start(bf16[128,512]{1,0:T(8,128)(2,1)S(1)} %collective-permute-done.21.refs_4_), channel_id=1, source_target_pairs={{0,1},{1,0},{2,3},{3,2},{4,5},{5,4},{6,7},{7,6},{8,9},{9,8},{10,11... | collective-permute-start | bytes 393224 | tf_op jit(solution)/shard_map/ppermute | solution.py:359
  158.5 7.7 %collective-permute-start.20 = (bf16[128,512]{1,0:T(8,128)(2,1)S(1)}, bf16[128,512]{1,0:T(8,128)(2,1)S(1)}, u32[]{:S(2)}, u32[]{:S(2)}) collective-permute-start(bf16[128,512]{1,0:T(8,128)(2,1)S(1)} %collective-permute-done.19.refs_2_), channel_id=1, source_target_pairs={{0,1},{1,0},{2,3},{3,2},{4,5},{5,4},{6,7},{7,6},{8,9},{9,8},{10,11... | collective-permute-start | bytes 393224 | tf_op jit(solution)/shard_map/ppermute | solution.py:359
  172.2 4.0 %collective-permute-start.25 = (f32[10,48,1024]{2,1,0:T(8,128)S(1)}, f32[10,48,1024]{2,1,0:T(8,128)S(1)}, u32[]{:S(2)}, u32[]{:S(2)}) collective-permute-start(f32[10,48,1024]{2,1,0:T(8,128)S(1)} %get-tuple-element.72), channel_id=1, source_target_pairs={{0,8},{8,0},{1,9},{9,1},{2,10},{10,2},{3,11},{11,3},{4,12},{12,4},... | collective-permute-start | bytes 5898248 | tf_op jit(solution)/shard_map/ppermute | solution.py:359
  176.6 5.5 %collective-permute-start.26 = (f32[2,4,80,1024]{3,2,1,0:T(8,128)S(1)}, f32[2,4,80,1024]{3,2,1,0:T(8,128)S(1)}, u32[]{:S(2)}, u32[]{:S(2)}) collective-permute-start(f32[2,4,80,1024]{3,2,1,0:T(8,128)S(1)} %get-tuple-element.74), channel_id=1, source_target_pairs={{0,8},{8,0},{1,9},{9,1},{2,10},{10,2},{3,11},{11,3},{4,12},{12,4},... | collective-permute-start | bytes 7864328 | tf_op jit(solution)/shard_map/ppermute | solution.py:359
  176.9 4.4 %collective-permute-start.27 = (f32[128,128]{1,0:T(8,128)S(1)}, f32[128,128]{1,0:T(8,128)S(1)}, u32[]{:S(2)}, u32[]{:S(2)}) collective-permute-start(f32[128,128]{1,0:T(8,128)S(1)} %bitcast.142), channel_id=1, source_target_pairs={{0,16},{16,0},{1,17},{17,1},{2,18},{18,2},{3,19},{19,3},{4,20},{20... | collective-permute-start | bytes 196616 | tf_op jit(solution)/shard_map/ppermute | solution.py:359
  177.2 7.5 %collective-permute-start.32 = (f16[2,48,1024]{2,1,0:T(8,128)(2,1)S(1)}, f16[2,48,1024]{2,1,0:T(8,128)(2,1)S(1)}, u32[]{:S(2)}, u32[]{:S(2)}) collective-permute-start(f16[2,48,1024]{2,1,0:T(8,128)(2,1)S(1)} %get-tuple-element.94), channel_id=1, source_target_pairs={{0,2},{2,0},{4,6},{6,4},{1,3},{3,1},{5,7},{7,5},{8,10},{10,8},{12,... | collective-permute-start | bytes 589832 | tf_op jit(solution)/shard_map/ppermute | solution.py:359
  177.7 11.8 %collective-permute-start.34 = (f16[2,48,1024]{2,1,0:T(8,128)(2,1)S(1)}, f16[2,48,1024]{2,1,0:T(8,128)(2,1)S(1)}, u32[]{:S(2)}, u32[]{:S(2)}) collective-permute-start(f16[2,48,1024]{2,1,0:T(8,128)(2,1)S(1)} %get-tuple-element.95), channel_id=1, source_target_pairs={{0,6},{2,4},{4,2},{6,0},{1,7},{3,5},{5,3},{7,1},{8,14},{10,12},{12... | collective-permute-start | bytes 589832 | tf_op jit(solution)/shard_map/ppermute | solution.py:359
  179.5 18.7 %collective-permute-start.33 = (f16[2,48,1024]{2,1,0:T(8,128)(2,1)S(1)}, f16[2,48,1024]{2,1,0:T(8,128)(2,1)S(1)}, u32[]{:S(2)}, u32[]{:S(2)}) collective-permute-start(f16[2,48,1024]{2,1,0:T(8,128)(2,1)S(1)} %get-tuple-element.96), channel_id=1, source_target_pairs={{0,4},{2,6},{4,0},{6,2},{1,5},{3,7},{5,1},{7,3},{8,12},{10,14},{12... | collective-permute-start | bytes 589832 | tf_op jit(solution)/shard_map/ppermute | solution.py:359
  182.8 17.4 %collective-permute-start.28 = (f16[4,80,1024]{2,1,0:T(8,128)(2,1)S(1)}, f16[4,80,1024]{2,1,0:T(8,128)(2,1)S(1)}, u32[]{:S(2)}, u32[]{:S(2)}) collective-permute-start(f16[4,80,1024]{2,1,0:T(8,128)(2,1)S(1)} %fusion.1), channel_id=1, source_target_pairs={{0,16},{16,0},{1,17},{17,1},{2,18},{18,2},{3,19},{19,3},{4,20},{20... | collective-permute-start | bytes 1966088 | tf_op jit(solution)/shard_map/ppermute | solution.py:359
  198.5 5.8 %collective-permute-start.35 = (f16[48,1024]{1,0:T(8,128)(2,1)S(1)}, f16[48,1024]{1,0:T(8,128)(2,1)S(1)}, u32[]{:S(2)}, u32[]{:S(2)}) collective-permute-start(f16[48,1024]{1,0:T(8,128)(2,1)S(1)} %fusion.15), channel_id=1, source_target_pairs={{0,16},{16,0},{1,17},{17,1},{2,18},{18,2},{3,19},{19,3},{4,20},{20... | collective-permute-start | bytes 294920 | tf_op jit(solution)/shard_map/ppermute | solution.py:359
  200.7 7.1 %collective-permute-start.29 = (f16[80,1024]{1,0:T(8,128)(2,1)S(1)}, f16[80,1024]{1,0:T(8,128)(2,1)S(1)}, u32[]{:S(2)}, u32[]{:S(2)}) collective-permute-start(f16[80,1024]{1,0:T(8,128)(2,1)S(1)} %get-tuple-element.99), channel_id=1, source_target_pairs={{0,2},{2,0},{4,6},{6,4},{1,3},{3,1},{5,7},{7,5},{8,10},{10,8},{12,... | collective-permute-start | bytes 491528 | tf_op jit(solution)/shard_map/ppermute | solution.py:359
  200.8 10.2 %collective-permute-start.31 = (f16[80,1024]{1,0:T(8,128)(2,1)S(1)}, f16[80,1024]{1,0:T(8,128)(2,1)S(1)}, u32[]{:S(2)}, u32[]{:S(2)}) collective-permute-start(f16[80,1024]{1,0:T(8,128)(2,1)S(1)} %get-tuple-element.100), channel_id=1, source_target_pairs={{0,6},{2,4},{4,2},{6,0},{1,7},{3,5},{5,3},{7,1},{8,14},{10,12},{12... | collective-permute-start | bytes 491528 | tf_op jit(solution)/shard_map/ppermute | solution.py:359
  202.8 14.5 %collective-permute-start.30 = (f16[80,1024]{1,0:T(8,128)(2,1)S(1)}, f16[80,1024]{1,0:T(8,128)(2,1)S(1)}, u32[]{:S(2)}, u32[]{:S(2)}) collective-permute-start(f16[80,1024]{1,0:T(8,128)(2,1)S(1)} %get-tuple-element.101), channel_id=1, source_target_pairs={{0,4},{2,6},{4,0},{6,2},{1,5},{3,7},{5,1},{7,3},{8,12},{10,14},{12... | collective-permute-start | bytes 491528 | tf_op jit(solution)/shard_map/ppermute | solution.py:359
  219.6 6.8 %collective-permute-start.37 = (bf16[1024,128]{1,0:T(8,128)(2,1)S(1)}, bf16[1024,128]{1,0:T(8,128)(2,1)S(1)}, u32[]{:S(2)}, u32[]{:S(2)}) collective-permute-start(bf16[1024,128]{1,0:T(8,128)(2,1)S(1)} %shard_map.74.refs_0_), channel_id=1, source_target_pairs={{0,16},{16,0},{1,17},{17,1},{2,18},{18,2},{3,19},{19,3},{4,20},{20... | collective-permute-start | bytes 786440 | tf_op jit(solution)/shard_map/ppermute | solution.py:359
  220.3 9.1 %copy-start.1 = (f32[4096,128]{1,0:T(8,128)S(1)}, f32[4096,128]{1,0:T(8,128)}, u32[]{:S(2)}) copy-start(f32[4096,128]{1,0:T(8,128)} %param.8) | copy-start | bytes 6291460
  222.0 4.5 %collective-permute-start.36 = (bf16[1024,128]{1,0:T(8,128)(2,1)S(1)}, bf16[1024,128]{1,0:T(8,128)(2,1)S(1)}, u32[]{:S(2)}, u32[]{:S(2)}) collective-permute-start(bf16[1024,128]{1,0:T(8,128)(2,1)S(1)} %shard_map.74.refs_0_), channel_id=1, source_target_pairs={{0,8},{8,0},{1,9},{9,1},{2,10},{10,2},{3,11},{11,3},{4,12},{12,4},... | collective-permute-start | bytes 786440 | tf_op jit(solution)/shard_map/ppermute | solution.py:359
  226.4 1.5 collective-permute-start.38

commit v6 on v5

--- a/solution.py
+++ b/solution.py
@@ -131,33 +131,37 @@
     return pl.BlockSpec(memory_space=pltpu.SMEM)
 
 
-def row_products(inbox, meta, me, pieces, his, los, width):
+def join(pieces, me, his):
+    part, length = pieces[0].shape
+
+    def kernel(me_ref, *refs):
+        for side in range(2):
+            rows = pl.ds(pl.multiple_of((me_ref[1] ^ side) * part, part), part)
+            for j in range(his):
+                refs[-1][j, rows, :] = refs[side * his + j][...]
+
+    return pl.pallas_call(
+        kernel,
+        out_shape=jax.ShapeDtypeStruct((his, 2 * part, length), pieces[0].dtype),
+        in_specs=[smem()] + [vmem()] * len(pieces),
+        out_specs=vmem(),
+        compiler_params=params(),
+    )(me, *pieces)
+
+
+def row_products(inbox, meta, me, panels, his, los, width):
     peers, size, held = inbox.shape[0], inbox.shape[2], meta.shape[1]
-    part, length = pieces[0].shape
-    rank = 2 * part
+    _, rank, length = panels.shape
     per_chunk = width // size
     keep = peers <= DEPTH
 
-    def kernel(meta_ref, me_ref, inbox_ref, *refs):
-        piece_refs, (top_ref, bot_ref) = refs[: 2 * his], refs[2 * his : 2 * his + 2]
-        tiles_ref, panel_ref, terms_ref, sems, more_sems = refs[2 * his + 2 :]
-        my_core, my_hi, my_lo = me_ref[1], me_ref[2], me_ref[3]
-        copies = []
-        for side in range(2):
-            rows = pl.ds(pl.multiple_of((my_core ^ side) * part, part), part)
-            for j in range(his):
-                at = side * his + j
-                copies.append(
-                    pltpu.make_async_copy(piece_refs[at], panel_ref.at[j, rows], more_sems.at[at])
-                )
-        for copy in copies:
-            copy.start()
+    def kernel(meta_ref, me_ref, inbox_ref, panel_ref, *refs):
+        top_ref, bot_ref, tiles_ref, terms_ref, sems = refs
+        my_hi, my_lo = me_ref[2], me_ref[3]
 
         def ready():
             top_ref[...] = jnp.zeros_like(top_ref)
             bot_ref[...] = jnp.zeros_like(bot_ref)
-            for copy in copies:
-                copy.wait()
 
         def product(slot, spot, tile):
             place = pl.ds(pl.multiple_of((spot % CT) * size, size), size)
@@ -183,17 +187,15 @@
     return pl.pallas_call(
         kernel,
         out_shape=out_shape + out_tiles,
-        in_specs=[smem(), smem(), hbm()] + [vmem()] * len(pieces),
+        in_specs=[smem(), smem(), hbm(), vmem()],
         out_specs=[vmem()] * (2 + keep),
         scratch_shapes=([] if keep else [pltpu.VMEM(tiles, inbox.dtype)])
         + [
-            pltpu.VMEM((his, rank, length), jnp.bfloat16),
             pltpu.VMEM((held, rank, size), F32),
             pltpu.SemaphoreType.DMA((tiles[0],)),
-            pltpu.SemaphoreType.DMA((2 * his,)),
         ],
         compiler_params=params(),
-    )(meta, me, inbox, *pieces)
+    )(meta, me, inbox, panels)
 
 
 def column_products(inbox, kept, meta, me, pieces, his, los, fars, out_width):
@@ -425,12 +427,14 @@
     w_t, own_t, *pieces = lax.optimization_barrier((w_t, own_t, *pieces))
     pieces += [swap(piece, "core", 1) for piece in pieces]
 
+    panels = join(pieces, me, his)
+    h_t, panels = lax.optimization_barrier((h_t, panels))
     gram_h = lax.dot_general(h_t, h_t, (((1,), (1,)), ((), ())), precision=HIGH)
     gram_h = everywhere(gram_h, ("hi",), jnp.add)
-    gram_h, meta, *pieces = lax.optimization_barrier((gram_h, meta, *pieces))
+    gram_h, meta = lax.optimization_barrier((gram_h, meta))
     gram_h = everywhere(gram_h, ("lo",), jnp.add)
     prepared = prepare(w_t, gram_h)
-    parts = row_products(inbox, meta, me, pieces, his, los, width)
+    parts = row_products(inbox, meta, me, panels, his, los, width)
     parts, kept = parts[:2], parts[2:]
     high, low = scales(gram_h, slots * cols, size)
     top = gather(gather(parts[0], "lo", *high), "hi", *high)
@@ -446,12 +450,16 @@
     lines = rank * rank // length
     gram_w = bottom[-1, :lines].reshape(lines, length // rank, rank)
     gram_w = gram_w.transpose(1, 0, 2).reshape(rank, rank)
+    down = bound(bottom[-2], slots * 2, size)
+    bottom = bottom[:-2].reshape(his, fars, *bottom.shape[1:])
+    sends = [(bottom[j] * (1.0 / down)).astype(LINK) for j in range(1, his)]
+    *sends, gram_w = lax.optimization_barrier((*sends, gram_w))
     gram_w = everywhere(gram_w, ("far",), jnp.add)
     prepared = prepare(own_t, gram_w)
     high, low = scales(gram_w, slots * rows * his, size)
-    down = bound(bottom[-2], slots * 2, size)
-    bottom = bottom[:-2].reshape(his, fars, *bottom.shape[1:])
-    bottom = gather(bottom, "hi", 1.0 / down, down)
+    bottom = bottom[0]
+    for j, send in enumerate(sends, 1):
+        bottom = bottom + swap(send, "hi", j).astype(F32) * down
     bottom = gather(bottom, "far", *low)
     top = gather(gather(top, "far", *high), "hi", *high)
     h_low = sweep(own_t, top, bottom, prepared, True)

time: 230 us -> 229 us (level)
  starting transfers between devices: 43.4 us -> 47.3 us
  waiting for transfers between devices: 140 us -> 137 us
    ppermute x39, starting transfers between devices: 38.2 us -> 42.1 us  [swap(): return lax.ppermute(x, axis, [(i, i ^ bit) for i in range(size)])]
    all_to_all x1, waiting for transfers between devices: 23.2 us -> 20 us  [local(): lax.all_to_all(outbox, plane, split_axis=0, concat_axis=0, tiled=True)]
  transfers between devices with their start and end apart: 40 -> 40, of which waited for: 24 -> 26; matrix products, arithmetic and copies ran while one was open for 6% -> 5% of each run, Pallas kernels for 5% -> 5%
where the time goes in v6:
time: 229 us
  waiting for transfers between devices  137 us (60%)
  starting transfers between devices  47.3 us (21%)
  Pallas kernels  27.7 us (12%)
  local copies, waits for them, and re-layouts  7.89 us (3%)
  other arithmetic  4.65 us (2%)
  matrix products  3.45 us (2%)
    ppermute x39, waiting for transfers between devices, swap(): return lax.ppermute(x, axis, [(i, i ^ bit) for i in range(size)])  117 us
    ppermute x39, starting transfers between devices, swap(): return lax.ppermute(x, axis, [(i, i ^ bit) for i in range(size)])  42.1 us
    all_to_all x1, waiting for transfers between devices, local(): lax.all_to_all(outbox, plane, split_axis=0, concat_axis=0, tiled=True)  20 us
    pallas_call x1, Pallas kernels, row_products(): pl.pallas_call(kernel, out_shape=out_shape + out_tiles, in_specs=[smem(),...  7.06 us
    pallas_call x1, Pallas kernels, column_products(): pl.pallas_call(kernel, out_shape=[jax.ShapeDtypeStruct(shape, F32) for sh...  5.85 us
    pallas_call x1, Pallas kernels, pack(): pl.pallas_call(kernel, out_shape=jax.ShapeDtypeStruct((peers, held * size...  5.36 us
    all_to_all x1, starting transfers between devices, local(): lax.all_to_all(outbox, plane, split_axis=0, concat_axis=0, tiled=True)  5.19 us
  transfers between devices with their start and end apart: 40, of which 26 were waited for; matrix products, arithmetic and copies ran while one was open for 5% of the time, Pallas kernels for 5%

profile of v6, /device:TPU:0, one launch (start us, length us, event | category | flops | bytes accessed | tf_op | source)
XLA Modules:
  0.0 229.1 jit_solution(12735280875637125536)
XLA Ops:
  0.6 5.4 %shard_map.68 = bf16[8,2064,256]{2,1,0:T(8,128)(2,1)} custom-call(s32[32]{0:T(128)} %bitcast.145, s32[32]{0:T(128)} %spot_ref.1, bf16[32,256,256]{2,1,0:T(8,128)(2,1)} %tiles_ref.1), custom_call_target="tpu_custom_call" | custom-call | tf_op jit(solution)/shard_map/pallas_call | solution.py:68
  6.0 5.2 %all-to-all-start = ((bf16[8,2064,256]{2,1,0:T(8,128)(2,1)}), bf16[8,2064,256]{2,1,0:T(8,128)(2,1)}, u32[]{:S(2)}, u32[]{:S(2)}) async-start(bf16[8,2064,256]{2,1,0:T(8,128)(2,1)} %shard_map.68), calls=%async_computation | async-start | bytes 16908288 | tf_op jit(solution)/shard_map/all_to_all | solution.py:419
  11.2 2.9 %copy.8 = f32[4096,128]{0,1:T(8,128)} copy(f32[4096,128]{1,0:T(8,128)} %param.9) | data formatting | bytes 4194304 | tf_op jit(solution)/shard_map/optimization_barrier | solution.py:418
  15.4 4.9 %collective-permute-start.2 = (bf16[64,4096]{1,0:T(8,128)(2,1)S(1)}, bf16[64,4096]{1,0:T(8,128)(2,1)S(1)}, u32[]{:S(2)}, u32[]{:S(2)}) collective-permute-start(bf16[64,4096]{1,0:T(8,128)(2,1)S(1)} %fusion.4.refs_0_), channel_id=1, source_target_pairs={{0,6},{2,4},{4,2},{6,0},{1,7},{3,5},{5,3},{7,1},{8,14},{10,12},{12... | collective-permute-start | bytes 1572872 | tf_op jit(solution)/shard_map/ppermute | solution.py:361
  22.2 11.0 %collective-permute-done.2.refs_3_ = bf16[64,4096]{1,0:T(8,128)(2,1)S(1)} collective-permute-done((bf16[64,4096]{1,0:T(8,128)(2,1)S(1)}, bf16[64,4096]{1,0:T(8,128)(2,1)S(1)}, u32[]{:S(2)}, u32[]{:S(2)}) %collective-permute-start.2) | collective-permute-done | bytes 524320 | tf_op jit(solution)/shard_map/ppermute | solution.py:361
  33.2 32.5 %collective-permute-done.1.refs_2_ = bf16[64,4096]{1,0:T(8,128)(2,1)} collective-permute-done((bf16[64,4096]{1,0:T(8,128)(2,1)S(1)}, bf16[64,4096]{1,0:T(8,128)(2,1)}, u32[]{:S(2)}, u32[]{:S(2)}) %collective-permute-start.1) | collective-permute-done | bytes 524320 | tf_op jit(solution)/shard_map/ppermute | solution.py:361
  66.8 1.5 collective-permute-done.3.refs_4_
  68.6 1.5 collective-permute-done.5.refs_6_
  70.1 1.6 shard_map.69.panel_ref
  72.0 3.5 %fusion.40 = f32[128,128]{1,0:T(8,128)S(1)} fusion(f32[128,4096]{0,1:T(8,128)S(1)} %bitcast.139), kind=kOutput, calls=%fused_computation.81 | convolution fusion | flops 805306368 | bytes 2162688 | tf_op jit(solution)/shard_map/dot_general | solution.py:432
  75.6 4.3 %collective-permute-done.7 = f32[128,128]{1,0:T(8,128)S(1)} collective-permute-done((f32[128,128]{1,0:T(8,128)S(1)}, f32[128,128]{1,0:T(8,128)S(1)}, u32[]{:S(2)}, u32[]{:S(2)}) %collective-permute-start.7) | collective-permute-done | bytes 65568 | tf_op jit(solution)/shard_map/ppermute | solution.py:361
  81.1 4.4 %collective-permute-done.8 = f32[128,128]{1,0:T(8,128)S(1)} collective-permute-done((f32[128,128]{1,0:T(8,128)S(1)}, f32[128,128]{1,0:T(8,128)S(1)}, u32[]{:S(2)}, u32[]{:S(2)}) %collective-permute-start.8) | collective-permute-done | bytes 65568 | tf_op jit(solution)/shard_map/ppermute | solution.py:361
  85.5 20.0 %all-to-all-done.inbox_ref = bf16[8,2064,256]{2,1,0:T(8,128)(2,1)} async-done(((bf16[8,2064,256]{2,1,0:T(8,128)(2,1)}), bf16[8,2064,256]{2,1,0:T(8,128)(2,1)}, u32[]{:S(2)}, u32[]{:S(2)}) %all-to-all-start) | async-done | bytes 8454176 | tf_op jit(solution)/shard_map/all_to_all | solution.py:419
  106.2 1.6 collective-permute-start.9
  107.8 2.2 copy-done.3
  110.0 7.1 %shard_map.70 = (f32[2,4,80,512]{3,2,1,0:T(8,128)S(1)}, f32[4,2,48,512]{3,2,1,0:T(8,128)S(1)}, bf16[8,2048,256]{2,1,0:T(8,128)(2,1)S(1)}) custom-call(s32[8,8]{1,0:T(8,128)S(1)} %bitcast.137, s32[4]{0:T(128)S(1)} %pad_add_fusion.me_ref, bf16[8,2064,256]{2,1,0:T(8,128)(2,1)} %all-to-all-done.inbox_ref, bf16[4,128,4096]{2,1,0:T(8,128)(2,1)S(1)} %copy-done.3), custom_call_target="tpu_custom_call" | custom-call | tf_op jit(solution)/shard_map/pallas_call | solution.py:187
  117.4 2.4 %collective-permute-start.14 = (f16[2,48,512]{2,1,0:T(8,128)(2,1)S(1)}, f16[2,48,512]{2,1,0:T(8,128)(2,1)S(1)}, u32[]{:S(2)}, u32[]{:S(2)}) collective-permute-start(f16[2,48,512]{2,1,0:T(8,128)(2,1)S(1)} %get-tuple-element.98), channel_id=1, source_target_pairs={{0,2},{2,0},{4,6},{6,4},{1,3},{3,1},{5,7},{7,5},{8,10},{10,8},{12,... | collective-permute-start | bytes 294920 | tf_op jit(solution)/shard_map/ppermute | solution.py:361
  119.8 2.5 %collective-permute-start.16 = (f16[2,48,512]{2,1,0:T(8,128)(2,1)S(1)}, f16[2,48,512]{2,1,0:T(8,128)(2,1)S(1)}, u32[]{:S(2)}, u32[]{:S(2)}) collective-permute-start(f16[2,48,512]{2,1,0:T(8,128)(2,1)S(1)} %get-tuple-element.99), channel_id=1, source_target_pairs={{0,6},{2,4},{4,2},{6,0},{1,7},{3,5},{5,3},{7,1},{8,14},{10,12},{12... | collective-permute-start | bytes 294920 | tf_op jit(solution)/shard_map/ppermute | solution.py:361
  123.7 4.1 %collective-permute-done.16 = f16[2,48,512]{2,1,0:T(8,128)(2,1)S(1)} collective-permute-done((f16[2,48,512]{2,1,0:T(8,128)(2,1)S(1)}, f16[2,48,512]{2,1,0:T(8,128)(2,1)S(1)}, u32[]{:S(2)}, u32[]{:S(2)}) %collective-permute-start.16) | collective-permute-done | bytes 98336 | tf_op jit(solution)/shard_map/ppermute | solution.py:361
  127.8 3.4 %collective-permute-done.15 = f16[2,48,512]{2,1,0:T(8,128)(2,1)S(1)} collective-permute-done((f16[2,48,512]{2,1,0:T(8,128)(2,1)S(1)}, f16[2,48,512]{2,1,0:T(8,128)(2,1)S(1)}, u32[]{:S(2)}, u32[]{:S(2)}) %collective-permute-start.15) | collective-permute-done | bytes 98336 | tf_op jit(solution)/shard_map/ppermute | solution.py:361
  133.1 3.0 %collective-permute-start.13 = (f16[80,512]{1,0:T(8,128)(2,1)S(1)}, f16[80,512]{1,0:T(8,128)(2,1)S(1)}, u32[]{:S(2)}, u32[]{:S(2)}) collective-permute-start(f16[80,512]{1,0:T(8,128)(2,1)S(1)} %get-tuple-element.102), channel_id=1, source_target_pairs={{0,6},{2,4},{4,2},{6,0},{1,7},{3,5},{5,3},{7,1},{8,14},{10,12},{12... | collective-permute-start | bytes 245768 | tf_op jit(solution)/shard_map/ppermute | solution.py:361
  136.2 1.4 collective-permute-done.11
  137.6 2.1 collective-permute-done.13
  139.7 2.7 %collective-permute-done.12 = f16[80,512]{1,0:T(8,128)(2,1)S(1)} collective-permute-done((f16[80,512]{1,0:T(8,128)(2,1)S(1)}, f16[80,512]{1,0:T(8,128)(2,1)S(1)}, u32[]{:S(2)}, u32[]{:S(2)}) %collective-permute-start.12) | collective-permute-done | bytes 81952 | tf_op jit(solution)/shard_map/ppermute | solution.py:361
  142.5 1.4 shard_map.72.refs_0_
  143.9 1.8 collective-permute-start.23
  145.7 2.7 %collective-permute-start.19 = (bf16[128,512]{1,0:T(8,128)(2,1)S(1)}, bf16[128,512]{1,0:T(8,128)(2,1)S(1)}, u32[]{:S(2)}, u32[]{:S(2)}) collective-permute-start(bf16[128,512]{1,0:T(8,128)(2,1)S(1)} %shard_map.72.refs_0_), channel_id=1, source_target_pairs={{0,2},{2,0},{4,6},{6,4},{1,3},{3,1},{5,7},{7,5},{8,10},{10,8},{12,... | collective-permute-start | bytes 393224 | tf_op jit(solution)/shard_map/ppermute | solution.py:361
  149.7 2.6 %collective-permute-done.23.refs_6_ = bf16[128,512]{1,0:T(8,128)(2,1)S(1)} collective-permute-done((bf16[128,512]{1,0:T(8,128)(2,1)S(1)}, bf16[128,512]{1,0:T(8,128)(2,1)S(1)}, u32[]{:S(2)}, u32[]{:S(2)}) %collective-permute-start.23) | collective-permute-done | bytes 131104 | tf_op jit(solution)/shard_map/ppermute | solution.py:361
  153.5 3.0 %collective-permute-done.21.refs_4_ = bf16[128,512]{1,0:T(8,128)(2,1)S(1)} collective-permute-done((bf16[128,512]{1,0:T(8,128)(2,1)S(1)}, bf16[128,512]{1,0:T(8,128)(2,1)S(1)}, u32[]{:S(2)}, u32[]{:S(2)}) %collective-permute-start.21) | collective-permute-done | bytes 131104 | tf_op jit(solution)/shard_map/ppermute | solution.py:361
  158.5 3.7 %collective-permute-done.22.refs_5_ = bf16[128,512]{1,0:T(8,128)(2,1)S(1)} collective-permute-done((bf16[128,512]{1,0:T(8,128)(2,1)S(1)}, bf16[128,512]{1,0:T(8,128)(2,1)S(1)}, u32[]{:S(2)}, u32[]{:S(2)}) %collective-permute-start.22) | collective-permute-done | bytes 131104 | tf_op jit(solution)/shard_map/ppermute | solution.py:361
  163.6 5.8 %shard_map.73 = (f32[2,4,80,1024]{3,2,1,0:T(8,128)S(1)}, f32[10,48,1024]{2,1,0:T(8,128)S(1)}, f32[2,4,80,1024]{3,2,1,0:T(8,128)S(1)}, f32[10,48,1024]{2,1,0:T(8,128)S(1)}) custom-call(s32[8,8]{1,0:T(8,128)S(1)} %bitcast.138, s32[4]{0:T(128)S(1)} %pad_add_fusion.me_ref, bf16[8,2048,256]{2,1,0:T(8,128)(2,1)S(1)} %get-tuple-element.54.source_ref, ...), custom_call_target="tpu_custom_call" | custom-call | tf_op jit(solution)/shard_map/pallas_call | solution.py:262
  169.5 4.0 %collective-permute-done.25 = f32[10,48,1024]{2,1,0:T(8,128)S(1)} collective-permute-done((f32[10,48,1024]{2,1,0:T(8,128)S(1)}, f32[10,48,1024]{2,1,0:T(8,128)S(1)}, u32[]{:S(2)}, u32[]{:S(2)}) %collective-permute-start.25) | collective-permute-done | bytes 1966112 | tf_op jit(solution)/shard_map/ppermute | solution.py:361
  174.4 4.1 %collective-permute-start.27 = (f32[128,128]{1,0:T(8,128)S(1)}, f32[128,128]{1,0:T(8,128)S(1)}, u32[]{:S(2)}, u32[]{:S(2)}) collective-permute-start(f32[128,128]{1,0:T(8,128)S(1)} %bitcast.142), channel_id=1, source_target_pairs={{0,16},{16,0},{1,17},{17,1},{2,18},{18,2},{3,19},{19,3},{4,20},{20... | collective-permute-start | bytes 196616 | tf_op jit(solution)/shard_map/ppermute | solution.py:361
  178.5 2.5 %collective-permute-start.33 = (f16[2,48,1024]{2,1,0:T(8,128)(2,1)S(1)}, f16[2,48,1024]{2,1,0:T(8,128)(2,1)S(1)}, u32[]{:S(2)}, u32[]{:S(2)}) collective-permute-start(f16[2,48,1024]{2,1,0:T(8,128)(2,1)S(1)} %get-tuple-element.70), channel_id=1, source_target_pairs={{0,4},{2,6},{4,0},{6,2},{1,5},{3,7},{5,1},{7,3},{8,12},{10,14},{12... | collective-permute-start | bytes 589832 | tf_op jit(solution)/shard_map/ppermute | solution.py:361
  181.0 1.9 collective-permute-start.34
  184.9 3.9 %collective-permute-done.32 = f16[2,48,1024]{2,1,0:T(8,128)(2,1)S(1)} collective-permute-done((f16[2,48,1024]{2,1,0:T(8,128)(2,1)S(1)}, f16[2,48,1024]{2,1,0:T(8,128)(2,1)S(1)}, u32[]{:S(2)}, u32[]{:S(2)}) %collective-permute-start.32) | collective-permute-done | bytes 196640 | tf_op jit(solution)/shard_map/ppermute | solution.py:361
  188.8 6.8 %collective-permute-done.33 = f16[2,48,1024]{2,1,0:T(8,128)(2,1)S(1)} collective-permute-done((f16[2,48,1024]{2,1,0:T(8,128)(2,1)S(1)}, f16[2,48,1024]{2,1,0:T(8,128)(2,1)S(1)}, u32[]{:S(2)}, u32[]{:S(2)}) %collective-permute-start.33) | collective-permute-done | bytes 196640 | tf_op jit(solution)/shard_map/ppermute | solution.py:361
  196.0 5.6 %collective-permute-done.28 = f16[4,80,1024]{2,1,0:T(8,128)(2,1)S(1)} collective-permute-done((f16[4,80,1024]{2,1,0:T(8,128)(2,1)S(1)}, f16[4,80,1024]{2,1,0:T(8,128)(2,1)S(1)}, u32[]{:S(2)}, u32[]{:S(2)}) %collective-permute-start.28) | collective-permute-done | bytes 655392 | tf_op jit(solution)/shard_map/ppermute | solution.py:361
  202.2 2.0 collective-permute-start.31
  204.2 1.5 collective-permute-start.30
  205.8 2.6 %collective-permute-done.29 = f16[80,1024]{1,0:T(8,128)(2,1)S(1)} collective-permute-done((f16[80,1024]{1,0:T(8,128)(2,1)S(1)}, f16[80,1024]{1,0:T(8,128)(2,1)S(1)}, u32[]{:S(2)}, u32[]{:S(2)}) %collective-permute-start.29) | collective-permute-done | bytes 163872 | tf_op jit(solution)/shard_map/ppermute | solution.py:361
  208.4 3.0 %collective-permute-done.31 = f16[80,1024]{1,0:T(8,128)(2,1)S(1)} collective-permute-done((f16[80,1024]{1,0:T(8,128)(2,1)S(1)}, f16[80,1024]{1,0:T(8,128)(2,1)S(1)}, u32[]{:S(2)}, u32[]{:S(2)}) %collective-permute-start.31) | collective-permute-done | bytes 163872 | tf_op jit(solution)/shard_map/ppermute | solution.py:361
  211.4 5.9 %collective-permute-done.30 = f16[80,1024]{1,0:T(8,128)(2,1)S(1)} collective-permute-done((f16[80,1024]{1,0:T(8,128)(2,1)S(1)}, f16[80,1024]{1,0:T(8,128)(2,1)S(1)}, u32[]{:S(2)}, u32[]{:S(2)}) %collective-permute-start.30) | collective-permute-done | bytes 163872 | tf_op jit(solution)/shard_map/ppermute | solution.py:361
  217.5 2.2 shard_map.75.refs_0_
  220.4 1.7 shard_map.76
  222.1 4.0 %collective-permute-done.37.refs_2_ = bf16[1024,128]{1,0:T(8,128)(2,1)S(1)} collective-permute-done((bf16[1024,128]{1,0:T(8,128)(2,1)S(1)}, bf16[1024,128]{1,0:T(8,128)(2,1)S(1)}, u32[]{:S(2)}, u32[]{:S(2)}) %collective-permute-start.37) | collective-permute-done | bytes 262176 | tf_op jit(solution)/shard_map/ppermute | solution.py:361
  226.1 1.5 collective-permute-done.38.refs_3_
  227.6 1.5 shard_map.77
  (92 shorter events, 21.6 us)
Async XLA Ops:
  0.6 20.3 %copy-start = (f32[4096,128]{1,0:T(8,128)S(1)}, f32[4096,128]{1,0:T(8,128)}, u32[]{:S(2)}) copy-start(f32[4096,128]{1,0:T(8,128)} %param.8) | copy-start | bytes 6291460
  6.0 99.5 %all-to-all-start = ((bf16[8,2064,256]{2,1,0:T(8,128)(2,1)}), bf16[8,2064,256]{2,1,0:T(8,128)(2,1)}, u32[]{:S(2)}, u32[]{:S(2)}) async-start(bf16[8,2064,256]{2,1,0:T(8,128)(2,1)} %shard_map.68), calls=%async_computation | async-start | bytes 16908288 | tf_op jit(solution)/shard_map/all_to_all | solution.py:419
  15.4 17.8 %collective-permute-start.2 = (bf16[64,4096]{1,0:T(8,128)(2,1)S(1)}, bf16[64,4096]{1,0:T(8,128)(2,1)S(1)}, u32[]{:S(2)}, u32[]{:S(2)}) collective-permute-start(bf16[64,4096]{1,0:T(8,128)(2,1)S(1)} %fusion.4.refs_0_), channel_id=1, source_target_pairs={{0,6},{2,4},{4,2},{6,0},{1,7},{3,5},{5,3},{7,1},{8,14},{10,12},{12... | collective-permute-start | bytes 1572872 | tf_op jit(solution)/shard_map/ppermute | solution.py:361
  20.3 45.4 %collective-permute-start.1 = (bf16[64,4096]{1,0:T(8,128)(2,1)S(1)}, bf16[64,4096]{1,0:T(8,128)(2,1)}, u32[]{:S(2)}, u32[]{:S(2)}) collective-permute-start(bf16[64,4096]{1,0:T(8,128)(2,1)S(1)} %fusion.4.refs_0_), channel_id=1, source_target_pairs={{0,4},{2,6},{4,0},{6,2},{1,5},{3,7},{5,1},{7,3},{8,12},{10,14},{12... | collective-permute-start | bytes 1572872 | tf_op jit(solution)/shard_map/ppermute | solution.py:361
  20.3 45.4 %collective-permute-start = (bf16[64,4096]{1,0:T(8,128)(2,1)S(1)}, bf16[64,4096]{1,0:T(8,128)(2,1)}, u32[]{:S(2)}, u32[]{:S(2)}) collective-permute-start(bf16[64,4096]{1,0:T(8,128)(2,1)S(1)} %fusion.4.refs_0_), channel_id=1, source_target_pairs={{0,2},{2,0},{4,6},{6,4},{1,3},{3,1},{5,7},{7,5},{8,10},{10,8},{12,... | collective-permute-start | bytes 1572872 | tf_op jit(solution)/shard_map/ppermute | solution.py:361
  65.7 2.6 %collective-permute-start.3 = (bf16[64,4096]{1,0:T(8,128)(2,1)S(1)}, bf16[64,4096]{1,0:T(8,128)(2,1)S(1)}, u32[]{:S(2)}, u32[]{:S(2)}) collective-permute-start(bf16[64,4096]{1,0:T(8,128)(2,1)S(1)} %fusion.4.refs_0_), channel_id=1, source_target_pairs={{0,8},{8,0},{1,9},{9,1},{2,10},{10,2},{3,11},{11,3},{4,12},{12,4},... | collective-permute-start | bytes 1572872 | tf_op jit(solution)/shard_map/ppermute | solution.py:361
  65.7 2.9 %collective-permute-start.4 = (bf16[64,4096]{1,0:T(8,128)(2,1)}, bf16[64,4096]{1,0:T(8,128)(2,1)S(1)}, u32[]{:S(2)}, u32[]{:S(2)}) collective-permute-start(bf16[64,4096]{1,0:T(8,128)(2,1)} %collective-permute-done.refs_1_), channel_id=1, source_target_pairs={{0,8},{8,0},{1,9},{9,1},{2,10},{10,2},{3,11},{11,3},{4,12},{12,4},... | collective-permute-start | bytes 1572872 | tf_op jit(solution)/shard_map/ppermute | solution.py:361
  66.2 3.9 %collective-permute-start.5 = (bf16[64,4096]{1,0:T(8,128)(2,1)}, bf16[64,4096]{1,0:T(8,128)(2,1)S(1)}, u32[]{:S(2)}, u32[]{:S(2)}) collective-permute-start(bf16[64,4096]{1,0:T(8,128)(2,1)} %collective-permute-done.1.refs_2_), channel_id=1, source_target_pairs={{0,8},{8,0},{1,9},{9,1},{2,10},{10,2},{3,11},{11,3},{4,12},{12,4},... | collective-permute-start | bytes 1572872 | tf_op jit(solution)/shard_map/ppermute | solution.py:361
  66.2 3.9 %collective-permute-start.6 = (bf16[64,4096]{1,0:T(8,128)(2,1)S(1)}, bf16[64,4096]{1,0:T(8,128)(2,1)S(1)}, u32[]{:S(2)}, u32[]{:S(2)}) collective-permute-start(bf16[64,4096]{1,0:T(8,128)(2,1)S(1)} %collective-permute-done.2.refs_3_), channel_id=1, source_target_pairs={{0,8},{8,0},{1,9},{9,1},{2,10},{10,2},{3,11},{11,3},{4,12},{12,4},... | collective-permute-start | bytes 1572872 | tf_op jit(solution)/shard_map/ppermute | solution.py:361
  70.1 1.9 copy-start.4
  71.8 3.7 %copy-start.2 = (bf16[4,128,4096]{2,1,0:T(8,128)(2,1)}, bf16[4,128,4096]{2,1,0:T(8,128)(2,1)S(1)}, u32[]{:S(2)}) copy-start(bf16[4,128,4096]{2,1,0:T(8,128)(2,1)S(1)} %shard_map.69.panel_ref) | copy-start | bytes 12582916
  75.5 4.3 %collective-permute-start.7 = (f32[128,128]{1,0:T(8,128)S(1)}, f32[128,128]{1,0:T(8,128)S(1)}, u32[]{:S(2)}, u32[]{:S(2)}) collective-permute-start(f32[128,128]{1,0:T(8,128)S(1)} %fusion.40), channel_id=1, source_target_pairs={{0,2},{2,0},{4,6},{6,4},{1,3},{3,1},{5,7},{7,5},{8,10},{10,8},{12,... | collective-permute-start | bytes 196616 | tf_op jit(solution)/shard_map/ppermute | solution.py:361
  79.8 5.7 %collective-permute-start.8 = (f32[128,128]{1,0:T(8,128)S(1)}, f32[128,128]{1,0:T(8,128)S(1)}, u32[]{:S(2)}, u32[]{:S(2)}) collective-permute-start(f32[128,128]{1,0:T(8,128)S(1)} %add.86), channel_id=1, source_target_pairs={{0,4},{2,6},{4,0},{6,2},{1,5},{3,7},{5,1},{7,3},{8,12},{10,14},{12... | collective-permute-start | bytes 196616 | tf_op jit(solution)/shard_map/ppermute | solution.py:361
  106.2 10.8 %collective-permute-start.9 = (f32[128,128]{1,0:T(8,128)S(1)}, f32[128,128]{1,0:T(8,128)S(1)}, u32[]{:S(2)}, u32[]{:S(2)}) collective-permute-start(f32[128,128]{1,0:T(8,128)S(1)} %add.87), channel_id=1, source_target_pairs={{0,1},{1,0},{2,3},{3,2},{4,5},{5,4},{6,7},{7,6},{8,9},{9,8},{10,11... | collective-permute-start | bytes 196616 | tf_op jit(solution)/shard_map/ppermute | solution.py:361
  107.8 2.2 copy-start.3
  117.4 6.2 %collective-permute-start.14 = (f16[2,48,512]{2,1,0:T(8,128)(2,1)S(1)}, f16[2,48,512]{2,1,0:T(8,128)(2,1)S(1)}, u32[]{:S(2)}, u32[]{:S(2)}) collective-permute-start(f16[2,48,512]{2,1,0:T(8,128)(2,1)S(1)} %get-tuple-element.98), channel_id=1, source_target_pairs={{0,2},{2,0},{4,6},{6,4},{1,3},{3,1},{5,7},{7,5},{8,10},{10,8},{12,... | collective-permute-start | bytes 294920 | tf_op jit(solution)/shard_map/ppermute | solution.py:361
  119.8 8.0 %collective-permute-start.16 = (f16[2,48,512]{2,1,0:T(8,128)(2,1)S(1)}, f16[2,48,512]{2,1,0:T(8,128)(2,1)S(1)}, u32[]{:S(2)}, u32[]{:S(2)}) collective-permute-start(f16[2,48,512]{2,1,0:T(8,128)(2,1)S(1)} %get-tuple-element.99), channel_id=1, source_target_pairs={{0,6},{2,4},{4,2},{6,0},{1,7},{3,5},{5,3},{7,1},{8,14},{10,12},{12... | collective-permute-start | bytes 294920 | tf_op jit(solution)/shard_map/ppermute | solution.py:361
  122.3 8.8 %collective-permute-start.15 = (f16[2,48,512]{2,1,0:T(8,128)(2,1)S(1)}, f16[2,48,512]{2,1,0:T(8,128)(2,1)S(1)}, u32[]{:S(2)}, u32[]{:S(2)}) collective-permute-start(f16[2,48,512]{2,1,0:T(8,128)(2,1)S(1)} %get-tuple-element.100), channel_id=1, source_target_pairs={{0,4},{2,6},{4,0},{6,2},{1,5},{3,7},{5,1},{7,3},{8,12},{10,14},{12... | collective-permute-start | bytes 294920 | tf_op jit(solution)/shard_map/ppermute | solution.py:361
  122.8 9.1 %collective-permute-start.10 = (f16[4,80,512]{2,1,0:T(8,128)(2,1)S(1)}, f16[4,80,512]{2,1,0:T(8,128)(2,1)S(1)}, u32[]{:S(2)}, u32[]{:S(2)}) collective-permute-start(f16[4,80,512]{2,1,0:T(8,128)(2,1)S(1)} %fusion.3), channel_id=1, source_target_pairs={{0,1},{1,0},{2,3},{3,2},{4,5},{5,4},{6,7},{7,6},{8,9},{9,8},{10,11... | collective-permute-start | bytes 983048 | tf_op jit(solution)/shard_map/ppermute | solution.py:361
  131.3 4.8 %collective-permute-start.17 = (f16[48,512]{1,0:T(8,128)(2,1)S(1)}, f16[48,512]{1,0:T(8,128)(2,1)S(1)}, u32[]{:S(2)}, u32[]{:S(2)}) collective-permute-start(f16[48,512]{1,0:T(8,128)(2,1)S(1)} %fusion.33), channel_id=1, source_target_pairs={{0,1},{1,0},{2,3},{3,2},{4,5},{5,4},{6,7},{7,6},{8,9},{9,8},{10,11... | collective-permute-start | bytes 147464 | tf_op jit(solution)/shard_map/ppermute | solution.py:361
  132.2 5.4 %collective-permute-start.11 = (f16[80,512]{1,0:T(8,128)(2,1)S(1)}, f16[80,512]{1,0:T(8,128)(2,1)S(1)}, u32[]{:S(2)}, u32[]{:S(2)}) collective-permute-start(f16[80,512]{1,0:T(8,128)(2,1)S(1)} %get-tuple-element.101), channel_id=1, source_target_pairs={{0,2},{2,0},{4,6},{6,4},{1,3},{3,1},{5,7},{7,5},{8,10},{10,8},{12,... | collective-permute-start | bytes 245768 | tf_op jit(solution)/shard_map/ppermute | solution.py:361
  133.1 6.6 %collective-permute-start.13 = (f16[80,512]{1,0:T(8,128)(2,1)S(1)}, f16[80,512]{1,0:T(8,128)(2,1)S(1)}, u32[]{:S(2)}, u32[]{:S(2)}) collective-permute-start(f16[80,512]{1,0:T(8,128)(2,1)S(1)} %get-tuple-element.102), channel_id=1, source_target_pairs={{0,6},{2,4},{4,2},{6,0},{1,7},{3,5},{5,3},{7,1},{8,14},{10,12},{12... | collective-permute-start | bytes 245768 | tf_op jit(solution)/shard_map/ppermute | solution.py:361
  136.1 6.3 %collective-permute-start.12 = (f16[80,512]{1,0:T(8,128)(2,1)S(1)}, f16[80,512]{1,0:T(8,128)(2,1)S(1)}, u32[]{:S(2)}, u32[]{:S(2)}) collective-permute-start(f16[80,512]{1,0:T(8,128)(2,1)S(1)} %get-tuple-element.103), channel_id=1, source_target_pairs={{0,4},{2,6},{4,0},{6,2},{1,5},{3,7},{5,1},{7,3},{8,12},{10,14},{12... | collective-permute-start | bytes 245768 | tf_op jit(solution)/shard_map/ppermute | solution.py:361
  143.9 8.3 %collective-permute-start.23 = (bf16[128,512]{1,0:T(8,128)(2,1)S(1)}, bf16[128,512]{1,0:T(8,128)(2,1)S(1)}, u32[]{:S(2)}, u32[]{:S(2)}) collective-permute-start(bf16[128,512]{1,0:T(8,128)(2,1)S(1)} %shard_map.72.refs_0_), channel_id=1, source_target_pairs={{0,6},{2,4},{4,2},{6,0},{1,7},{3,5},{5,3},{7,1},{8,14},{10,12},{12... | collective-permute-start | bytes 393224 | tf_op jit(solution)/shard_map/ppermute | solution.py:361
  145.7 10.8 %collective-permute-start.21 = (bf16[128,512]{1,0:T(8,128)(2,1)S(1)}, bf16[128,512]{1,0:T(8,128)(2,1)S(1)}, u32[]{:S(2)}, u32[]{:S(2)}) collective-permute-start(bf16[128,512]{1,0:T(8,128)(2,1)S(1)} %shard_map.72.refs_0_), channel_id=1, source_target_pairs={{0,4},{2,6},{4,0},{6,2},{1,5},{3,7},{5,1},{7,3},{8,12},{10,14},{12... | collective-permute-start | bytes 393224 | tf_op jit(solution)/shard_map/ppermute | solution.py:361
  145.7 12.1 %collective-permute-start.19 = (bf16[128,512]{1,0:T(8,128)(2,1)S(1)}, bf16[128,512]{1,0:T(8,128)(2,1)S(1)}, u32[]{:S(2)}, u32[]{:S(2)}) collective-permute-start(bf16[128,512]{1,0:T(8,128)(2,1)S(1)} %shard_map.72.refs_0_), channel_id=1, source_target_pairs={{0,2},{2,0},{4,6},{6,4},{1,3},{3,1},{5,7},{7,5},{8,10},{10,8},{12,... | collective-permute-start | bytes 393224 | tf_op jit(solution)/shard_map/ppermute | solution.py:361
  148.4 10.1 %collective-permute-start.18 = (bf16[128,512]{1,0:T(8,128)(2,1)S(1)}, bf16[128,512]{1,0:T(8,128)(2,1)S(1)}, u32[]{:S(2)}, u32[]{:S(2)}) collective-permute-start(bf16[128,512]{1,0:T(8,128)(2,1)S(1)} %shard_map.72.refs_0_), channel_id=1, source_target_pairs={{0,1},{1,0},{2,3},{3,2},{4,5},{5,4},{6,7},{7,6},{8,9},{9,8},{10,11... | collective-permute-start | bytes 393224 | tf_op jit(solution)/shard_map/ppermute | solution.py:361
  152.2 6.3 %collective-permute-start.24 = (bf16[128,512]{1,0:T(8,128)(2,1)S(1)}, bf16[128,512]{1,0:T(8,128)(2,1)S(1)}, u32[]{:S(2)}, u32[]{:S(2)}) collective-permute-start(bf16[128,512]{1,0:T(8,128)(2,1)S(1)} %collective-permute-done.23.refs_6_), channel_id=1, source_target_pairs={{0,1},{1,0},{2,3},{3,2},{4,5},{5,4},{6,7},{7,6},{8,9},{9,8},{10,11... | collective-permute-start | bytes 393224 | tf_op jit(solution)/shard_map/ppermute | solution.py:361
  156.5 5.7 %collective-permute-start.22 = (bf16[128,512]{1,0:T(8,128)(2,1)S(1)}, bf16[128,512]{1,0:T(8,128)(2,1)S(1)}, u32[]{:S(2)}, u32[]{:S(2)}) collective-permute-start(bf16[128,512]{1,0:T(8,128)(2,1)S(1)} %collective-permute-done.21.refs_4_), channel_id=1, source_target_pairs={{0,1},{1,0},{2,3},{3,2},{4,5},{5,4},{6,7},{7,6},{8,9},{9,8},{10,11... | collective-permute-start | bytes 393224 | tf_op jit(solution)/shard_map/ppermute | solution.py:361
  157.8 5.8 %collective-permute-start.20 = (bf16[128,512]{1,0:T(8,128)(2,1)S(1)}, bf16[128,512]{1,0:T(8,128)(2,1)S(1)}, u32[]{:S(2)}, u32[]{:S(2)}) collective-permute-start(bf16[128,512]{1,0:T(8,128)(2,1)S(1)} %collective-permute-done.19.refs_2_), channel_id=1, source_target_pairs={{0,1},{1,0},{2,3},{3,2},{4,5},{5,4},{6,7},{7,6},{8,9},{9,8},{10,11... | collective-permute-start | bytes 393224 | tf_op jit(solution)/shard_map/ppermute | solution.py:361
  169.5 4.0 %collective-permute-start.25 = (f32[10,48,1024]{2,1,0:T(8,128)S(1)}, f32[10,48,1024]{2,1,0:T(8,128)S(1)}, u32[]{:S(2)}, u32[]{:S(2)}) collective-permute-start(f32[10,48,1024]{2,1,0:T(8,128)S(1)} %get-tuple-element.64), channel_id=1, source_target_pairs={{0,8},{8,0},{1,9},{9,1},{2,10},{10,2},{3,11},{11,3},{4,12},{12,4},... | collective-permute-start | bytes 5898248 | tf_op jit(solution)/shard_map/ppermute | solution.py:361
  173.9 9.8 %collective-permute-start.26 = (f32[2,4,80,1024]{3,2,1,0:T(8,128)S(1)}, f32[2,4,80,1024]{3,2,1,0:T(8,128)S(1)}, u32[]{:S(2)}, u32[]{:S(2)}) collective-permute-start(f32[2,4,80,1024]{3,2,1,0:T(8,128)S(1)} %get-tuple-element.66), channel_id=1, source_target_pairs={{0,8},{8,0},{1,9},{9,1},{2,10},{10,2},{3,11},{11,3},{4,12},{12,4},... | collective-permute-start | bytes 7864328 | tf_op jit(solution)/shard_map/ppermute | solution.py:361
  174.4 8.5 %collective-permute-start.27 = (f32[128,128]{1,0:T(8,128)S(1)}, f32[128,128]{1,0:T(8,128)S(1)}, u32[]{:S(2)}, u32[]{:S(2)}) collective-permute-start(f32[128,128]{1,0:T(8,128)S(1)} %bitcast.142), channel_id=1, source_target_pairs={{0,16},{16,0},{1,17},{17,1},{2,18},{18,2},{3,19},{19,3},{4,20},{20... | collective-permute-start | bytes 196616 | tf_op jit(solution)/shard_map/ppermute | solution.py:361
  178.5 10.3 %collective-permute-start.32 = (f16[2,48,1024]{2,1,0:T(8,128)(2,1)S(1)}, f16[2,48,1024]{2,1,0:T(8,128)(2,1)S(1)}, u32[]{:S(2)}, u32[]{:S(2)}) collective-permute-start(f16[2,48,1024]{2,1,0:T(8,128)(2,1)S(1)} %get-tuple-element.69), channel_id=1, source_target_pairs={{0,2},{2,0},{4,6},{6,4},{1,3},{3,1},{5,7},{7,5},{8,10},{10,8},{12,... | collective-permute-start | bytes 589832 | tf_op jit(solution)/shard_map/ppermute | solution.py:361
  178.5 17.1 %collective-permute-start.33 = (f16[2,48,1024]{2,1,0:T(8,128)(2,1)S(1)}, f16[2,48,1024]{2,1,0:T(8,128)(2,1)S(1)}, u32[]{:S(2)}, u32[]{:S(2)}) collective-permute-start(f16[2,48,1024]{2,1,0:T(8,128)(2,1)S(1)} %get-tuple-element.70), channel_id=1, source_target_pairs={{0,4},{2,6},{4,0},{6,2},{1,5},{3,7},{5,1},{7,3},{8,12},{10,14},{12... | collective-permute-start | bytes 589832 | tf_op jit(solution)/shard_map/ppermute | solution.py:361
  181.0 14.7 %collective-permute-start.34 = (f16[2,48,1024]{2,1,0:T(8,128)(2,1)S(1)}, f16[2,48,1024]{2,1,0:T(8,128)(2,1)S(1)}, u32[]{:S(2)}, u32[]{:S(2)}) collective-permute-start(f16[2,48,1024]{2,1,0:T(8,128)(2,1)S(1)} %get-tuple-element.71), channel_id=1, source_target_pairs={{0,6},{2,4},{4,2},{6,0},{1,7},{3,5},{5,3},{7,1},{8,14},{10,12},{12... | collective-permute-start | bytes 589832 | tf_op jit(solution)/shard_map/ppermute | solution.py:361
  184.6 17.0 %collective-permute-start.28 = (f16[4,80,1024]{2,1,0:T(8,128)(2,1)S(1)}, f16[4,80,1024]{2,1,0:T(8,128)(2,1)S(1)}, u32[]{:S(2)}, u32[]{:S(2)}) collective-permute-start(f16[4,80,1024]{2,1,0:T(8,128)(2,1)S(1)} %fusion.1), channel_id=1, source_target_pairs={{0,16},{16,0},{1,17},{17,1},{2,18},{18,2},{3,19},{19,3},{4,20},{20... | collective-permute-start | bytes 1966088 | tf_op jit(solution)/shard_map/ppermute | solution.py:361
  195.9 9.8 %collective-permute-start.35 = (f16[48,1024]{1,0:T(8,128)(2,1)S(1)}, f16[48,1024]{1,0:T(8,128)(2,1)S(1)}, u32[]{:S(2)}, u32[]{:S(2)}) collective-permute-start(f16[48,1024]{1,0:T(8,128)(2,1)S(1)} %fusion.15), channel_id=1, source_target_pairs={{0,16},{16,0},{1,17},{17,1},{2,18},{18,2},{3,19},{19,3},{4,20},{20... | collective-permute-start | bytes 294920 | tf_op jit(solution)/shard_map/ppermute | solution.py:361
  202.2 6.3 %collective-permute-start.29 = (f16[80,1024]{1,0:T(8,128)(2,1)S(1)}, f16[80,1024]{1,0:T(8,128)(2,1)S(1)}, u32[]{:S(2)}, u32[]{:S(2)}) collective-permute-start(f16[80,1024]{1,0:T(8,128)(2,1)S(1)} %get-tuple-element.95), channel_id=1, source_target_pairs={{0,2},{2,0},{4,6},{6,4},{1,3},{3,1},{5,7},{7,5},{8,10},{10,8},{12,... | collective-permute-start | bytes 491528 | tf_op jit(solution)/shard_map/ppermute | solution.py:361
  202.2 9.2 %collective-permute-start.31 = (f16[80,1024]{1,0:T(8,128)(2,1)S(1)}, f16[80,1024]{1,0:T(8,128)(2,1)S(1)}, u32[]{:S(2)}, u32[]{:S(2)}) collective-permute-start(f16[80,1024]{1,0:T(8,128)(2,1)S(1)} %get-tuple-element.96), channel_id=1, source_target_pairs={{0,6},{2,4},{4,2},{6,0},{1,7},{3,5},{5,3},{7,1},{8,14},{10,12},{12... | collective-permute-start | bytes 491528 | tf_op jit(solution)/shard_map/ppermute | solution.py:361
  204.2 13.1 %collective-permute-start.30 = (f16[80,1024]{1,0:T(8,128)(2,1)S(1)}, f16[80,1024]{1,0:T(8,128)(2,1)S(1)}, u32[]{:S(2)}, u32[]{:S(2)}) collective-permute-start(f16[80,1024]{1,0:T(8,128)(2,1)S(1)} %get-tuple-element.97), channel_id=1, source_target_pairs={{0,4},{2,6},{4,0},{6,2},{1,5},{3,7},{5,1},{7,3},{8,12},{10,14},{12... | collective-permute-start | bytes 491528 | tf_op jit(solution)/shard_map/ppermute | solution.py:361
  219.7 6.4 %collective-permute-start.37 = (bf16[1024,128]{1,0:T(8,128)(2,1)S(1)}, bf16[1024,128]{1,0:T(8,128)(2,1)S(1)}, u32[]{:S(2)}, u32[]{:S(2)}) collective-permute-start(bf16[1024,128]{1,0:T(8,128)(2,1)S(1)} %shard_map.75.refs_0_), channel_id=1, source_target_pairs={{0,16},{16,0},{1,17},{17,1},{2,18},{18,2},{3,19},{19,3},{4,20},{20... | collective-permute-start | bytes 786440 | tf_op jit(solution)/shard_map/ppermute | solution.py:361
  220.4 8.7 %copy-start.1 = (f32[4096,128]{1,0:T(8,128)S(1)}, f32[4096,128]{1,0:T(8,128)}, u32[]{:S(2)}) copy-start(f32[4096,128]{1,0:T(8,128)} %param.8) | copy-start | bytes 6291460
  222.1 4.0 %collective-permute-start.36 = (bf16[1024,128]{1,0:T(8,128)(2,1)S(1)}, bf16[1024,128]{1,0:T(8,128)(2,1)S(1)}, u32[]{:S(2)}, u32[]{:S(2)}) collective-permute-start(bf16[1024,128]{1,0:T(8,128)(2,1)S(1)} %shard_map.75.refs_0_), channel_id=1, source_target_pairs={{0,8},{8,0},{1,9},{9,1},{2,10},{10,2},{3,11},{11,3},{4,12},{12,4},... | collective-permute-start | bytes 786440 | tf_op jit(solution)/shard_map/ppermute | solution.py:361
  226.1 1.5 collective-permute-start.38

commit v7 on v6

--- a/solution.py
+++ b/solution.py
@@ -15,6 +15,7 @@
 LINK = jnp.float16
 STEP = 32
 DEPTH = 8
+BATCH = 2
 PEAK = 256.0
 CUT = 80
 VMEM_LIMIT = 24 * 2**20
@@ -94,29 +95,34 @@
             copy(peer).start()
     ready()
 
-    def step(peer, carry):
+    def step(turn, carry):
+        first = turn * BATCH
         if sems is not None:
-            copy(peer).wait()
-        for slot in range(held):
-            spot = jnp.maximum(meta_ref[peer, slot] - 1, 0)
-            tile = tiles_ref[peer % depth, slot * size : (slot + 1) * size]
-            terms_ref[slot] = product(slot, spot, tile)
-        for slot in range(held):
-            spot = meta_ref[peer, slot] - 1
-
-            @pl.when(spot >= 0)
-            def _():
-                add(slot, spot)
+            for b in range(BATCH):
+                copy(first + b).wait()
+        for b in range(BATCH):
+            for slot in range(held):
+                spot = jnp.maximum(meta_ref[first + b, slot] - 1, 0)
+                tile = tiles_ref[(first + b) % depth, slot * size : (slot + 1) * size]
+                terms_ref[b * held + slot] = product(slot, spot, tile)
+        for b in range(BATCH):
+            for slot in range(held):
+                spot = meta_ref[first + b, slot] - 1
+
+                @pl.when(spot >= 0)
+                def _():
+                    add(slot, spot, b * held + slot)
 
         if depth < peers:
-
-            @pl.when(peer + depth < peers)
-            def _():
-                copy(peer + depth).start()
+            for b in range(BATCH):
+
+                @pl.when(first + b + depth < peers)
+                def _():
+                    copy(first + b + depth).start()
 
         return carry
 
-    lax.fori_loop(0, peers, step, 0)
+    lax.fori_loop(0, peers // BATCH, step, 0)
 
 
 def hbm():
@@ -168,13 +174,13 @@
             panel = panel_ref[slot // CAP ^ my_hi, :, place]
             return lax.dot_general(panel, tile, (((1,), (1,)), ((), ())), preferred_element_type=F32)
 
-        def add(slot, spot):
+        def add(slot, spot, at):
             trow = spot // CT
             chunk = trow // per_chunk
             lanes = pl.ds(pl.multiple_of((trow % per_chunk) * size, size), size)
             hi, lo = chunk // los ^ my_hi, chunk % los ^ my_lo
-            top_ref[lo, hi, :, lanes] += terms_ref[slot, :CUT]
-            bot_ref[hi, lo, :, lanes] += terms_ref[slot, CUT:]
+            top_ref[lo, hi, :, lanes] += terms_ref[at, :CUT]
+            bot_ref[hi, lo, :, lanes] += terms_ref[at, CUT:]
 
         each_tile(meta_ref, inbox_ref, tiles_ref, terms_ref, sems, product, add, ready)
 
@@ -191,7 +197,7 @@
         out_specs=[vmem()] * (2 + keep),
         scratch_shapes=([] if keep else [pltpu.VMEM(tiles, inbox.dtype)])
         + [
-            pltpu.VMEM((held, rank, size), F32),
+            pltpu.VMEM((BATCH * held, rank, size), F32),
             pltpu.SemaphoreType.DMA((tiles[0],)),
         ],
         compiler_params=params(),
@@ -236,7 +242,7 @@
             panel = panel_ref[(chunk // los ^ my_hi) * los + (chunk % los ^ my_lo), :, lanes]
             return lax.dot_general(panel, tile, (((1,), (0,)), ((), ())), preferred_element_type=F32)
 
-        def add(slot, spot):
+        def add(slot, spot, at):
             tcol = spot % CT
             owner = tcol // per_out
             place = pl.ds(pl.multiple_of((tcol % per_out) * size, size), size)
@@ -245,8 +251,8 @@
 
                 @pl.when((owner ^ my_core) % 2 == side)
                 def _():
-                    top_ref[far, hi, :, place] += terms_ref[slot, :CUT]
-                    bot_ref[hi * fars + far, :, place] += terms_ref[slot, CUT:]
+                    top_ref[far, hi, :, place] += terms_ref[at, :CUT]
+                    bot_ref[hi * fars + far, :, place] += terms_ref[at, CUT:]
 
         each_tile(meta_ref, source_ref, tiles_ref, terms_ref, sems, product, add, ready)
 
@@ -254,7 +260,7 @@
     out_shape = [tops, bots, tops, bots]
     scratch = [
         pltpu.VMEM((chunks, rank, width), jnp.bfloat16),
-        pltpu.VMEM((held, rank, size), F32),
+        pltpu.VMEM((BATCH * held, rank, size), F32),
     ]
     if not kept:
         scratch.append(pltpu.VMEM((DEPTH, held * size, size), inbox.dtype))

time: 229 us -> 227 us (level)
  no operation moved by 1% of the time
where the time goes in v7:
time: 227 us
  waiting for transfers between devices  136 us (60%)
  starting transfers between devices  47.1 us (21%)
  Pallas kernels  26.5 us (12%)
  local copies, waits for them, and re-layouts  7.89 us (3%)
  other arithmetic  4.65 us (2%)
  matrix products  3.45 us (2%)
    ppermute x39, waiting for transfers between devices, swap(): return lax.ppermute(x, axis, [(i, i ^ bit) for i in range(size)])  117 us
    ppermute x39, starting transfers between devices, swap(): return lax.ppermute(x, axis, [(i, i ^ bit) for i in range(size)])  41.9 us
    all_to_all x1, waiting for transfers between devices, local(): lax.all_to_all(outbox, plane, split_axis=0, concat_axis=0, tiled=True)  19.9 us
    pallas_call x1, Pallas kernels, row_products(): pl.pallas_call(kernel, out_shape=out_shape + out_tiles, in_specs=[smem(),...  6.7 us
    pallas_call x1, Pallas kernels, pack(): pl.pallas_call(kernel, out_shape=jax.ShapeDtypeStruct((peers, held * size...  5.36 us
    all_to_all x1, starting transfers between devices, local(): lax.all_to_all(outbox, plane, split_axis=0, concat_axis=0, tiled=True)  5.18 us
    pallas_call x1, Pallas kernels, column_products(): pl.pallas_call(kernel, out_shape=[jax.ShapeDtypeStruct(shape, F32) for sh...  5.06 us
  transfers between devices with their start and end apart: 40, of which 26 were waited for; matrix products, arithmetic and copies ran while one was open for 5% of the time, Pallas kernels for 5%

profile of v7, /device:TPU:0, one launch (start us, length us, event | category | flops | bytes accessed | tf_op | source)
XLA Modules:
  0.0 227.1 jit_solution(8296793734920529894)
XLA Ops:
  0.6 5.4 %shard_map.68 = bf16[8,2064,256]{2,1,0:T(8,128)(2,1)} custom-call(s32[32]{0:T(128)} %bitcast.145, s32[32]{0:T(128)} %spot_ref.1, bf16[32,256,256]{2,1,0:T(8,128)(2,1)} %tiles_ref.1), custom_call_target="tpu_custom_call" | custom-call | tf_op jit(solution)/shard_map/pallas_call | solution.py:69
  6.0 5.2 %all-to-all-start = ((bf16[8,2064,256]{2,1,0:T(8,128)(2,1)}), bf16[8,2064,256]{2,1,0:T(8,128)(2,1)}, u32[]{:S(2)}, u32[]{:S(2)}) async-start(bf16[8,2064,256]{2,1,0:T(8,128)(2,1)} %shard_map.68), calls=%async_computation | async-start | bytes 16908288 | tf_op jit(solution)/shard_map/all_to_all | solution.py:425
  11.2 2.9 %copy.8 = f32[4096,128]{0,1:T(8,128)} copy(f32[4096,128]{1,0:T(8,128)} %param.9) | data formatting | bytes 4194304 | tf_op jit(solution)/shard_map/optimization_barrier | solution.py:424
  15.4 5.0 %collective-permute-start.2 = (bf16[64,4096]{1,0:T(8,128)(2,1)S(1)}, bf16[64,4096]{1,0:T(8,128)(2,1)S(1)}, u32[]{:S(2)}, u32[]{:S(2)}) collective-permute-start(bf16[64,4096]{1,0:T(8,128)(2,1)S(1)} %fusion.4.refs_0_), channel_id=1, source_target_pairs={{0,6},{2,4},{4,2},{6,0},{1,7},{3,5},{5,3},{7,1},{8,14},{10,12},{12... | collective-permute-start | bytes 1572872 | tf_op jit(solution)/shard_map/ppermute | solution.py:367
  22.2 11.0 %collective-permute-done.2.refs_3_ = bf16[64,4096]{1,0:T(8,128)(2,1)S(1)} collective-permute-done((bf16[64,4096]{1,0:T(8,128)(2,1)S(1)}, bf16[64,4096]{1,0:T(8,128)(2,1)S(1)}, u32[]{:S(2)}, u32[]{:S(2)}) %collective-permute-start.2) | collective-permute-done | bytes 524320 | tf_op jit(solution)/shard_map/ppermute | solution.py:367
  33.2 32.5 %collective-permute-done.1.refs_2_ = bf16[64,4096]{1,0:T(8,128)(2,1)} collective-permute-done((bf16[64,4096]{1,0:T(8,128)(2,1)S(1)}, bf16[64,4096]{1,0:T(8,128)(2,1)}, u32[]{:S(2)}, u32[]{:S(2)}) %collective-permute-start.1) | collective-permute-done | bytes 524320 | tf_op jit(solution)/shard_map/ppermute | solution.py:367
  66.9 1.5 collective-permute-done.3.refs_4_
  68.7 1.5 collective-permute-done.5.refs_6_
  70.1 1.6 shard_map.69.panel_ref
  72.0 3.5 %fusion.40 = f32[128,128]{1,0:T(8,128)S(1)} fusion(f32[128,4096]{0,1:T(8,128)S(1)} %bitcast.139), kind=kOutput, calls=%fused_computation.81 | convolution fusion | flops 805306368 | bytes 2162688 | tf_op jit(solution)/shard_map/dot_general | solution.py:438
  75.6 4.3 %collective-permute-done.7 = f32[128,128]{1,0:T(8,128)S(1)} collective-permute-done((f32[128,128]{1,0:T(8,128)S(1)}, f32[128,128]{1,0:T(8,128)S(1)}, u32[]{:S(2)}, u32[]{:S(2)}) %collective-permute-start.7) | collective-permute-done | bytes 65568 | tf_op jit(solution)/shard_map/ppermute | solution.py:367
  81.0 4.5 %collective-permute-done.8 = f32[128,128]{1,0:T(8,128)S(1)} collective-permute-done((f32[128,128]{1,0:T(8,128)S(1)}, f32[128,128]{1,0:T(8,128)S(1)}, u32[]{:S(2)}, u32[]{:S(2)}) %collective-permute-start.8) | collective-permute-done | bytes 65568 | tf_op jit(solution)/shard_map/ppermute | solution.py:367
  85.5 19.9 %all-to-all-done.inbox_ref = bf16[8,2064,256]{2,1,0:T(8,128)(2,1)} async-done(((bf16[8,2064,256]{2,1,0:T(8,128)(2,1)}), bf16[8,2064,256]{2,1,0:T(8,128)(2,1)}, u32[]{:S(2)}, u32[]{:S(2)}) %all-to-all-start) | async-done | bytes 8454176 | tf_op jit(solution)/shard_map/all_to_all | solution.py:425
  106.2 1.6 collective-permute-start.9
  107.8 2.2 copy-done.3
  110.0 6.7 %shard_map.70 = (f32[2,4,80,512]{3,2,1,0:T(8,128)S(1)}, f32[4,2,48,512]{3,2,1,0:T(8,128)S(1)}, bf16[8,2048,256]{2,1,0:T(8,128)(2,1)S(1)}) custom-call(s32[8,8]{1,0:T(8,128)S(1)} %bitcast.137, s32[4]{0:T(128)S(1)} %pad_add_fusion.me_ref, bf16[8,2064,256]{2,1,0:T(8,128)(2,1)} %all-to-all-done.inbox_ref, bf16[4,128,4096]{2,1,0:T(8,128)(2,1)S(1)} %copy-done.3), custom_call_target="tpu_custom_call" | custom-call | tf_op jit(solution)/shard_map/pallas_call | solution.py:193
  117.1 2.3 %collective-permute-start.14 = (f16[2,48,512]{2,1,0:T(8,128)(2,1)S(1)}, f16[2,48,512]{2,1,0:T(8,128)(2,1)S(1)}, u32[]{:S(2)}, u32[]{:S(2)}) collective-permute-start(f16[2,48,512]{2,1,0:T(8,128)(2,1)S(1)} %get-tuple-element.98), channel_id=1, source_target_pairs={{0,2},{2,0},{4,6},{6,4},{1,3},{3,1},{5,7},{7,5},{8,10},{10,8},{12,... | collective-permute-start | bytes 294920 | tf_op jit(solution)/shard_map/ppermute | solution.py:367
  119.4 2.7 %collective-permute-start.16 = (f16[2,48,512]{2,1,0:T(8,128)(2,1)S(1)}, f16[2,48,512]{2,1,0:T(8,128)(2,1)S(1)}, u32[]{:S(2)}, u32[]{:S(2)}) collective-permute-start(f16[2,48,512]{2,1,0:T(8,128)(2,1)S(1)} %get-tuple-element.99), channel_id=1, source_target_pairs={{0,6},{2,4},{4,2},{6,0},{1,7},{3,5},{5,3},{7,1},{8,14},{10,12},{12... | collective-permute-start | bytes 294920 | tf_op jit(solution)/shard_map/ppermute | solution.py:367
  123.9 4.1 %collective-permute-done.16 = f16[2,48,512]{2,1,0:T(8,128)(2,1)S(1)} collective-permute-done((f16[2,48,512]{2,1,0:T(8,128)(2,1)S(1)}, f16[2,48,512]{2,1,0:T(8,128)(2,1)S(1)}, u32[]{:S(2)}, u32[]{:S(2)}) %collective-permute-start.16) | collective-permute-done | bytes 98336 | tf_op jit(solution)/shard_map/ppermute | solution.py:367
  128.0 3.3 %collective-permute-done.15 = f16[2,48,512]{2,1,0:T(8,128)(2,1)S(1)} collective-permute-done((f16[2,48,512]{2,1,0:T(8,128)(2,1)S(1)}, f16[2,48,512]{2,1,0:T(8,128)(2,1)S(1)}, u32[]{:S(2)}, u32[]{:S(2)}) %collective-permute-start.15) | collective-permute-done | bytes 98336 | tf_op jit(solution)/shard_map/ppermute | solution.py:367
  133.4 3.0 %collective-permute-start.13 = (f16[80,512]{1,0:T(8,128)(2,1)S(1)}, f16[80,512]{1,0:T(8,128)(2,1)S(1)}, u32[]{:S(2)}, u32[]{:S(2)}) collective-permute-start(f16[80,512]{1,0:T(8,128)(2,1)S(1)} %get-tuple-element.102), channel_id=1, source_target_pairs={{0,6},{2,4},{4,2},{6,0},{1,7},{3,5},{5,3},{7,1},{8,14},{10,12},{12... | collective-permute-start | bytes 245768 | tf_op jit(solution)/shard_map/ppermute | solution.py:367
  137.5 2.6 %collective-permute-done.13 = f16[80,512]{1,0:T(8,128)(2,1)S(1)} collective-permute-done((f16[80,512]{1,0:T(8,128)(2,1)S(1)}, f16[80,512]{1,0:T(8,128)(2,1)S(1)}, u32[]{:S(2)}, u32[]{:S(2)}) %collective-permute-start.13) | collective-permute-done | bytes 81952 | tf_op jit(solution)/shard_map/ppermute | solution.py:367
  140.0 2.4 %collective-permute-done.12 = f16[80,512]{1,0:T(8,128)(2,1)S(1)} collective-permute-done((f16[80,512]{1,0:T(8,128)(2,1)S(1)}, f16[80,512]{1,0:T(8,128)(2,1)S(1)}, u32[]{:S(2)}, u32[]{:S(2)}) %collective-permute-start.12) | collective-permute-done | bytes 81952 | tf_op jit(solution)/shard_map/ppermute | solution.py:367
  144.0 2.2 collective-permute-start.23
  146.2 2.2 collective-permute-start.19
  148.5 1.9 collective-permute-start.18
  150.3 2.0 collective-permute-done.23.refs_6_
  152.3 1.9 collective-permute-start.24
  154.2 2.2 collective-permute-done.21.refs_4_
  156.4 2.1 collective-permute-start.22
  158.5 4.3 %collective-permute-done.22.refs_5_ = bf16[128,512]{1,0:T(8,128)(2,1)S(1)} collective-permute-done((bf16[128,512]{1,0:T(8,128)(2,1)S(1)}, bf16[128,512]{1,0:T(8,128)(2,1)S(1)}, u32[]{:S(2)}, u32[]{:S(2)}) %collective-permute-start.22) | collective-permute-done | bytes 131104 | tf_op jit(solution)/shard_map/ppermute | solution.py:367
  162.9 1.5 collective-permute-done.20.refs_3_
  164.4 5.1 %shard_map.73 = (f32[2,4,80,1024]{3,2,1,0:T(8,128)S(1)}, f32[10,48,1024]{2,1,0:T(8,128)S(1)}, f32[2,4,80,1024]{3,2,1,0:T(8,128)S(1)}, f32[10,48,1024]{2,1,0:T(8,128)S(1)}) custom-call(s32[8,8]{1,0:T(8,128)S(1)} %bitcast.138, s32[4]{0:T(128)S(1)} %pad_add_fusion.me_ref, bf16[8,2048,256]{2,1,0:T(8,128)(2,1)S(1)} %get-tuple-element.54.source_ref, ...), custom_call_target="tpu_custom_call" | custom-call | tf_op jit(solution)/shard_map/pallas_call | solution.py:268
  169.5 4.0 %collective-permute-done.25 = f32[10,48,1024]{2,1,0:T(8,128)S(1)} collective-permute-done((f32[10,48,1024]{2,1,0:T(8,128)S(1)}, f32[10,48,1024]{2,1,0:T(8,128)S(1)}, u32[]{:S(2)}, u32[]{:S(2)}) %collective-permute-start.25) | collective-permute-done | bytes 1966112 | tf_op jit(solution)/shard_map/ppermute | solution.py:367
  174.4 1.8 collective-permute-start.27
  176.7 2.0 collective-permute-start.33
  178.8 1.8 collective-permute-start.34
  182.8 3.5 %collective-permute-done.32 = f16[2,48,1024]{2,1,0:T(8,128)(2,1)S(1)} collective-permute-done((f16[2,48,1024]{2,1,0:T(8,128)(2,1)S(1)}, f16[2,48,1024]{2,1,0:T(8,128)(2,1)S(1)}, u32[]{:S(2)}, u32[]{:S(2)}) %collective-permute-start.32) | collective-permute-done | bytes 196640 | tf_op jit(solution)/shard_map/ppermute | solution.py:367
  186.3 7.6 %collective-permute-done.33 = f16[2,48,1024]{2,1,0:T(8,128)(2,1)S(1)} collective-permute-done((f16[2,48,1024]{2,1,0:T(8,128)(2,1)S(1)}, f16[2,48,1024]{2,1,0:T(8,128)(2,1)S(1)}, u32[]{:S(2)}, u32[]{:S(2)}) %collective-permute-start.33) | collective-permute-done | bytes 196640 | tf_op jit(solution)/shard_map/ppermute | solution.py:367
  194.4 4.9 %collective-permute-done.28 = f16[4,80,1024]{2,1,0:T(8,128)(2,1)S(1)} collective-permute-done((f16[4,80,1024]{2,1,0:T(8,128)(2,1)S(1)}, f16[4,80,1024]{2,1,0:T(8,128)(2,1)S(1)}, u32[]{:S(2)}, u32[]{:S(2)}) %collective-permute-start.28) | collective-permute-done | bytes 655392 | tf_op jit(solution)/shard_map/ppermute | solution.py:367
  200.0 2.0 collective-permute-start.31
  203.5 1.9 collective-permute-done.29
  205.4 3.5 %collective-permute-done.31 = f16[80,1024]{1,0:T(8,128)(2,1)S(1)} collective-permute-done((f16[80,1024]{1,0:T(8,128)(2,1)S(1)}, f16[80,1024]{1,0:T(8,128)(2,1)S(1)}, u32[]{:S(2)}, u32[]{:S(2)}) %collective-permute-start.31) | collective-permute-done | bytes 163872 | tf_op jit(solution)/shard_map/ppermute | solution.py:367
  208.9 6.2 %collective-permute-done.30 = f16[80,1024]{1,0:T(8,128)(2,1)S(1)} collective-permute-done((f16[80,1024]{1,0:T(8,128)(2,1)S(1)}, f16[80,1024]{1,0:T(8,128)(2,1)S(1)}, u32[]{:S(2)}, u32[]{:S(2)}) %collective-permute-start.30) | collective-permute-done | bytes 163872 | tf_op jit(solution)/shard_map/ppermute | solution.py:367
  215.2 2.2 shard_map.75.refs_0_
  217.9 1.7 shard_map.76
  219.6 4.6 %collective-permute-done.37.refs_2_ = bf16[1024,128]{1,0:T(8,128)(2,1)S(1)} collective-permute-done((bf16[1024,128]{1,0:T(8,128)(2,1)S(1)}, bf16[1024,128]{1,0:T(8,128)(2,1)S(1)}, u32[]{:S(2)}, u32[]{:S(2)}) %collective-permute-start.37) | collective-permute-done | bytes 262176 | tf_op jit(solution)/shard_map/ppermute | solution.py:367
  224.1 1.5 collective-permute-done.38.refs_3_
  (92 shorter events, 22.1 us)
Async XLA Ops:
  0.6 20.3 %copy-start = (f32[4096,128]{1,0:T(8,128)S(1)}, f32[4096,128]{1,0:T(8,128)}, u32[]{:S(2)}) copy-start(f32[4096,128]{1,0:T(8,128)} %param.8) | copy-start | bytes 6291460
  6.0 99.5 %all-to-all-start = ((bf16[8,2064,256]{2,1,0:T(8,128)(2,1)}), bf16[8,2064,256]{2,1,0:T(8,128)(2,1)}, u32[]{:S(2)}, u32[]{:S(2)}) async-start(bf16[8,2064,256]{2,1,0:T(8,128)(2,1)} %shard_map.68), calls=%async_computation | async-start | bytes 16908288 | tf_op jit(solution)/shard_map/all_to_all | solution.py:425
  15.4 17.9 %collective-permute-start.2 = (bf16[64,4096]{1,0:T(8,128)(2,1)S(1)}, bf16[64,4096]{1,0:T(8,128)(2,1)S(1)}, u32[]{:S(2)}, u32[]{:S(2)}) collective-permute-start(bf16[64,4096]{1,0:T(8,128)(2,1)S(1)} %fusion.4.refs_0_), channel_id=1, source_target_pairs={{0,6},{2,4},{4,2},{6,0},{1,7},{3,5},{5,3},{7,1},{8,14},{10,12},{12... | collective-permute-start | bytes 1572872 | tf_op jit(solution)/shard_map/ppermute | solution.py:367
  20.3 45.4 %collective-permute-start.1 = (bf16[64,4096]{1,0:T(8,128)(2,1)S(1)}, bf16[64,4096]{1,0:T(8,128)(2,1)}, u32[]{:S(2)}, u32[]{:S(2)}) collective-permute-start(bf16[64,4096]{1,0:T(8,128)(2,1)S(1)} %fusion.4.refs_0_), channel_id=1, source_target_pairs={{0,4},{2,6},{4,0},{6,2},{1,5},{3,7},{5,1},{7,3},{8,12},{10,14},{12... | collective-permute-start | bytes 1572872 | tf_op jit(solution)/shard_map/ppermute | solution.py:367
  20.3 45.4 %collective-permute-start = (bf16[64,4096]{1,0:T(8,128)(2,1)S(1)}, bf16[64,4096]{1,0:T(8,128)(2,1)}, u32[]{:S(2)}, u32[]{:S(2)}) collective-permute-start(bf16[64,4096]{1,0:T(8,128)(2,1)S(1)} %fusion.4.refs_0_), channel_id=1, source_target_pairs={{0,2},{2,0},{4,6},{6,4},{1,3},{3,1},{5,7},{7,5},{8,10},{10,8},{12,... | collective-permute-start | bytes 1572872 | tf_op jit(solution)/shard_map/ppermute | solution.py:367
  65.8 2.6 %collective-permute-start.3 = (bf16[64,4096]{1,0:T(8,128)(2,1)S(1)}, bf16[64,4096]{1,0:T(8,128)(2,1)S(1)}, u32[]{:S(2)}, u32[]{:S(2)}) collective-permute-start(bf16[64,4096]{1,0:T(8,128)(2,1)S(1)} %fusion.4.refs_0_), channel_id=1, source_target_pairs={{0,8},{8,0},{1,9},{9,1},{2,10},{10,2},{3,11},{11,3},{4,12},{12,4},... | collective-permute-start | bytes 1572872 | tf_op jit(solution)/shard_map/ppermute | solution.py:367
  65.8 2.9 %collective-permute-start.4 = (bf16[64,4096]{1,0:T(8,128)(2,1)}, bf16[64,4096]{1,0:T(8,128)(2,1)S(1)}, u32[]{:S(2)}, u32[]{:S(2)}) collective-permute-start(bf16[64,4096]{1,0:T(8,128)(2,1)} %collective-permute-done.refs_1_), channel_id=1, source_target_pairs={{0,8},{8,0},{1,9},{9,1},{2,10},{10,2},{3,11},{11,3},{4,12},{12,4},... | collective-permute-start | bytes 1572872 | tf_op jit(solution)/shard_map/ppermute | solution.py:367
  66.3 3.9 %collective-permute-start.5 = (bf16[64,4096]{1,0:T(8,128)(2,1)}, bf16[64,4096]{1,0:T(8,128)(2,1)S(1)}, u32[]{:S(2)}, u32[]{:S(2)}) collective-permute-start(bf16[64,4096]{1,0:T(8,128)(2,1)} %collective-permute-done.1.refs_2_), channel_id=1, source_target_pairs={{0,8},{8,0},{1,9},{9,1},{2,10},{10,2},{3,11},{11,3},{4,12},{12,4},... | collective-permute-start | bytes 1572872 | tf_op jit(solution)/shard_map/ppermute | solution.py:367
  66.3 3.9 %collective-permute-start.6 = (bf16[64,4096]{1,0:T(8,128)(2,1)S(1)}, bf16[64,4096]{1,0:T(8,128)(2,1)S(1)}, u32[]{:S(2)}, u32[]{:S(2)}) collective-permute-start(bf16[64,4096]{1,0:T(8,128)(2,1)S(1)} %collective-permute-done.2.refs_3_), channel_id=1, source_target_pairs={{0,8},{8,0},{1,9},{9,1},{2,10},{10,2},{3,11},{11,3},{4,12},{12,4},... | collective-permute-start | bytes 1572872 | tf_op jit(solution)/shard_map/ppermute | solution.py:367
  70.1 1.9 copy-start.4
  71.8 3.7 %copy-start.2 = (bf16[4,128,4096]{2,1,0:T(8,128)(2,1)}, bf16[4,128,4096]{2,1,0:T(8,128)(2,1)S(1)}, u32[]{:S(2)}) copy-start(bf16[4,128,4096]{2,1,0:T(8,128)(2,1)S(1)} %shard_map.69.panel_ref) | copy-start | bytes 12582916
  75.5 4.3 %collective-permute-start.7 = (f32[128,128]{1,0:T(8,128)S(1)}, f32[128,128]{1,0:T(8,128)S(1)}, u32[]{:S(2)}, u32[]{:S(2)}) collective-permute-start(f32[128,128]{1,0:T(8,128)S(1)} %fusion.40), channel_id=1, source_target_pairs={{0,2},{2,0},{4,6},{6,4},{1,3},{3,1},{5,7},{7,5},{8,10},{10,8},{12,... | collective-permute-start | bytes 196616 | tf_op jit(solution)/shard_map/ppermute | solution.py:367
  79.8 5.7 %collective-permute-start.8 = (f32[128,128]{1,0:T(8,128)S(1)}, f32[128,128]{1,0:T(8,128)S(1)}, u32[]{:S(2)}, u32[]{:S(2)}) collective-permute-start(f32[128,128]{1,0:T(8,128)S(1)} %add.86), channel_id=1, source_target_pairs={{0,4},{2,6},{4,0},{6,2},{1,5},{3,7},{5,1},{7,3},{8,12},{10,14},{12... | collective-permute-start | bytes 196616 | tf_op jit(solution)/shard_map/ppermute | solution.py:367
  106.2 10.5 %collective-permute-start.9 = (f32[128,128]{1,0:T(8,128)S(1)}, f32[128,128]{1,0:T(8,128)S(1)}, u32[]{:S(2)}, u32[]{:S(2)}) collective-permute-start(f32[128,128]{1,0:T(8,128)S(1)} %add.87), channel_id=1, source_target_pairs={{0,1},{1,0},{2,3},{3,2},{4,5},{5,4},{6,7},{7,6},{8,9},{9,8},{10,11... | collective-permute-start | bytes 196616 | tf_op jit(solution)/shard_map/ppermute | solution.py:367
  107.8 2.2 copy-start.3
  117.1 6.8 %collective-permute-start.14 = (f16[2,48,512]{2,1,0:T(8,128)(2,1)S(1)}, f16[2,48,512]{2,1,0:T(8,128)(2,1)S(1)}, u32[]{:S(2)}, u32[]{:S(2)}) collective-permute-start(f16[2,48,512]{2,1,0:T(8,128)(2,1)S(1)} %get-tuple-element.98), channel_id=1, source_target_pairs={{0,2},{2,0},{4,6},{6,4},{1,3},{3,1},{5,7},{7,5},{8,10},{10,8},{12,... | collective-permute-start | bytes 294920 | tf_op jit(solution)/shard_map/ppermute | solution.py:367
  119.4 8.6 %collective-permute-start.16 = (f16[2,48,512]{2,1,0:T(8,128)(2,1)S(1)}, f16[2,48,512]{2,1,0:T(8,128)(2,1)S(1)}, u32[]{:S(2)}, u32[]{:S(2)}) collective-permute-start(f16[2,48,512]{2,1,0:T(8,128)(2,1)S(1)} %get-tuple-element.99), channel_id=1, source_target_pairs={{0,6},{2,4},{4,2},{6,0},{1,7},{3,5},{5,3},{7,1},{8,14},{10,12},{12... | collective-permute-start | bytes 294920 | tf_op jit(solution)/shard_map/ppermute | solution.py:367
  122.1 9.1 %collective-permute-start.15 = (f16[2,48,512]{2,1,0:T(8,128)(2,1)S(1)}, f16[2,48,512]{2,1,0:T(8,128)(2,1)S(1)}, u32[]{:S(2)}, u32[]{:S(2)}) collective-permute-start(f16[2,48,512]{2,1,0:T(8,128)(2,1)S(1)} %get-tuple-element.100), channel_id=1, source_target_pairs={{0,4},{2,6},{4,0},{6,2},{1,5},{3,7},{5,1},{7,3},{8,12},{10,14},{12... | collective-permute-start | bytes 294920 | tf_op jit(solution)/shard_map/ppermute | solution.py:367
  122.3 9.5 %collective-permute-start.10 = (f16[4,80,512]{2,1,0:T(8,128)(2,1)S(1)}, f16[4,80,512]{2,1,0:T(8,128)(2,1)S(1)}, u32[]{:S(2)}, u32[]{:S(2)}) collective-permute-start(f16[4,80,512]{2,1,0:T(8,128)(2,1)S(1)} %fusion.3), channel_id=1, source_target_pairs={{0,1},{1,0},{2,3},{3,2},{4,5},{5,4},{6,7},{7,6},{8,9},{9,8},{10,11... | collective-permute-start | bytes 983048 | tf_op jit(solution)/shard_map/ppermute | solution.py:367
  131.5 4.9 %collective-permute-start.17 = (f16[48,512]{1,0:T(8,128)(2,1)S(1)}, f16[48,512]{1,0:T(8,128)(2,1)S(1)}, u32[]{:S(2)}, u32[]{:S(2)}) collective-permute-start(f16[48,512]{1,0:T(8,128)(2,1)S(1)} %fusion.33), channel_id=1, source_target_pairs={{0,1},{1,0},{2,3},{3,2},{4,5},{5,4},{6,7},{7,6},{8,9},{9,8},{10,11... | collective-permute-start | bytes 147464 | tf_op jit(solution)/shard_map/ppermute | solution.py:367
  132.0 5.4 %collective-permute-start.11 = (f16[80,512]{1,0:T(8,128)(2,1)S(1)}, f16[80,512]{1,0:T(8,128)(2,1)S(1)}, u32[]{:S(2)}, u32[]{:S(2)}) collective-permute-start(f16[80,512]{1,0:T(8,128)(2,1)S(1)} %get-tuple-element.101), channel_id=1, source_target_pairs={{0,2},{2,0},{4,6},{6,4},{1,3},{3,1},{5,7},{7,5},{8,10},{10,8},{12,... | collective-permute-start | bytes 245768 | tf_op jit(solution)/shard_map/ppermute | solution.py:367
  133.4 6.6 %collective-permute-start.13 = (f16[80,512]{1,0:T(8,128)(2,1)S(1)}, f16[80,512]{1,0:T(8,128)(2,1)S(1)}, u32[]{:S(2)}, u32[]{:S(2)}) collective-permute-start(f16[80,512]{1,0:T(8,128)(2,1)S(1)} %get-tuple-element.102), channel_id=1, source_target_pairs={{0,6},{2,4},{4,2},{6,0},{1,7},{3,5},{5,3},{7,1},{8,14},{10,12},{12... | collective-permute-start | bytes 245768 | tf_op jit(solution)/shard_map/ppermute | solution.py:367
  136.4 6.1 %collective-permute-start.12 = (f16[80,512]{1,0:T(8,128)(2,1)S(1)}, f16[80,512]{1,0:T(8,128)(2,1)S(1)}, u32[]{:S(2)}, u32[]{:S(2)}) collective-permute-start(f16[80,512]{1,0:T(8,128)(2,1)S(1)} %get-tuple-element.103), channel_id=1, source_target_pairs={{0,4},{2,6},{4,0},{6,2},{1,5},{3,7},{5,1},{7,3},{8,12},{10,14},{12... | collective-permute-start | bytes 245768 | tf_op jit(solution)/shard_map/ppermute | solution.py:367
  144.0 8.3 %collective-permute-start.23 = (bf16[128,512]{1,0:T(8,128)(2,1)S(1)}, bf16[128,512]{1,0:T(8,128)(2,1)S(1)}, u32[]{:S(2)}, u32[]{:S(2)}) collective-permute-start(bf16[128,512]{1,0:T(8,128)(2,1)S(1)} %shard_map.72.refs_0_), channel_id=1, source_target_pairs={{0,6},{2,4},{4,2},{6,0},{1,7},{3,5},{5,3},{7,1},{8,14},{10,12},{12... | collective-permute-start | bytes 393224 | tf_op jit(solution)/shard_map/ppermute | solution.py:367
  146.2 10.2 %collective-permute-start.21 = (bf16[128,512]{1,0:T(8,128)(2,1)S(1)}, bf16[128,512]{1,0:T(8,128)(2,1)S(1)}, u32[]{:S(2)}, u32[]{:S(2)}) collective-permute-start(bf16[128,512]{1,0:T(8,128)(2,1)S(1)} %shard_map.72.refs_0_), channel_id=1, source_target_pairs={{0,4},{2,6},{4,0},{6,2},{1,5},{3,7},{5,1},{7,3},{8,12},{10,14},{12... | collective-permute-start | bytes 393224 | tf_op jit(solution)/shard_map/ppermute | solution.py:367
  146.2 12.3 %collective-permute-start.19 = (bf16[128,512]{1,0:T(8,128)(2,1)S(1)}, bf16[128,512]{1,0:T(8,128)(2,1)S(1)}, u32[]{:S(2)}, u32[]{:S(2)}) collective-permute-start(bf16[128,512]{1,0:T(8,128)(2,1)S(1)} %shard_map.72.refs_0_), channel_id=1, source_target_pairs={{0,2},{2,0},{4,6},{6,4},{1,3},{3,1},{5,7},{7,5},{8,10},{10,8},{12,... | collective-permute-start | bytes 393224 | tf_op jit(solution)/shard_map/ppermute | solution.py:367
  148.5 10.1 %collective-permute-start.18 = (bf16[128,512]{1,0:T(8,128)(2,1)S(1)}, bf16[128,512]{1,0:T(8,128)(2,1)S(1)}, u32[]{:S(2)}, u32[]{:S(2)}) collective-permute-start(bf16[128,512]{1,0:T(8,128)(2,1)S(1)} %shard_map.72.refs_0_), channel_id=1, source_target_pairs={{0,1},{1,0},{2,3},{3,2},{4,5},{5,4},{6,7},{7,6},{8,9},{9,8},{10,11... | collective-permute-start | bytes 393224 | tf_op jit(solution)/shard_map/ppermute | solution.py:367
  152.3 6.2 %collective-permute-start.24 = (bf16[128,512]{1,0:T(8,128)(2,1)S(1)}, bf16[128,512]{1,0:T(8,128)(2,1)S(1)}, u32[]{:S(2)}, u32[]{:S(2)}) collective-permute-start(bf16[128,512]{1,0:T(8,128)(2,1)S(1)} %collective-permute-done.23.refs_6_), channel_id=1, source_target_pairs={{0,1},{1,0},{2,3},{3,2},{4,5},{5,4},{6,7},{7,6},{8,9},{9,8},{10,11... | collective-permute-start | bytes 393224 | tf_op jit(solution)/shard_map/ppermute | solution.py:367
  156.4 6.5 %collective-permute-start.22 = (bf16[128,512]{1,0:T(8,128)(2,1)S(1)}, bf16[128,512]{1,0:T(8,128)(2,1)S(1)}, u32[]{:S(2)}, u32[]{:S(2)}) collective-permute-start(bf16[128,512]{1,0:T(8,128)(2,1)S(1)} %collective-permute-done.21.refs_4_), channel_id=1, source_target_pairs={{0,1},{1,0},{2,3},{3,2},{4,5},{5,4},{6,7},{7,6},{8,9},{9,8},{10,11... | collective-permute-start | bytes 393224 | tf_op jit(solution)/shard_map/ppermute | solution.py:367
  158.5 5.9 %collective-permute-start.20 = (bf16[128,512]{1,0:T(8,128)(2,1)S(1)}, bf16[128,512]{1,0:T(8,128)(2,1)S(1)}, u32[]{:S(2)}, u32[]{:S(2)}) collective-permute-start(bf16[128,512]{1,0:T(8,128)(2,1)S(1)} %collective-permute-done.19.refs_2_), channel_id=1, source_target_pairs={{0,1},{1,0},{2,3},{3,2},{4,5},{5,4},{6,7},{7,6},{8,9},{9,8},{10,11... | collective-permute-start | bytes 393224 | tf_op jit(solution)/shard_map/ppermute | solution.py:367
  169.5 4.0 %collective-permute-start.25 = (f32[10,48,1024]{2,1,0:T(8,128)S(1)}, f32[10,48,1024]{2,1,0:T(8,128)S(1)}, u32[]{:S(2)}, u32[]{:S(2)}) collective-permute-start(f32[10,48,1024]{2,1,0:T(8,128)S(1)} %get-tuple-element.64), channel_id=1, source_target_pairs={{0,8},{8,0},{1,9},{9,1},{2,10},{10,2},{3,11},{11,3},{4,12},{12,4},... | collective-permute-start | bytes 5898248 | tf_op jit(solution)/shard_map/ppermute | solution.py:367
  173.9 7.5 %collective-permute-start.26 = (f32[2,4,80,1024]{3,2,1,0:T(8,128)S(1)}, f32[2,4,80,1024]{3,2,1,0:T(8,128)S(1)}, u32[]{:S(2)}, u32[]{:S(2)}) collective-permute-start(f32[2,4,80,1024]{3,2,1,0:T(8,128)S(1)} %get-tuple-element.66), channel_id=1, source_target_pairs={{0,8},{8,0},{1,9},{9,1},{2,10},{10,2},{3,11},{11,3},{4,12},{12,4},... | collective-permute-start | bytes 7864328 | tf_op jit(solution)/shard_map/ppermute | solution.py:367
  174.4 6.2 %collective-permute-start.27 = (f32[128,128]{1,0:T(8,128)S(1)}, f32[128,128]{1,0:T(8,128)S(1)}, u32[]{:S(2)}, u32[]{:S(2)}) collective-permute-start(f32[128,128]{1,0:T(8,128)S(1)} %bitcast.142), channel_id=1, source_target_pairs={{0,16},{16,0},{1,17},{17,1},{2,18},{18,2},{3,19},{19,3},{4,20},{20... | collective-permute-start | bytes 196616 | tf_op jit(solution)/shard_map/ppermute | solution.py:367
  176.2 10.1 %collective-permute-start.32 = (f16[2,48,1024]{2,1,0:T(8,128)(2,1)S(1)}, f16[2,48,1024]{2,1,0:T(8,128)(2,1)S(1)}, u32[]{:S(2)}, u32[]{:S(2)}) collective-permute-start(f16[2,48,1024]{2,1,0:T(8,128)(2,1)S(1)} %get-tuple-element.69), channel_id=1, source_target_pairs={{0,2},{2,0},{4,6},{6,4},{1,3},{3,1},{5,7},{7,5},{8,10},{10,8},{12,... | collective-permute-start | bytes 589832 | tf_op jit(solution)/shard_map/ppermute | solution.py:367
  176.7 17.1 %collective-permute-start.33 = (f16[2,48,1024]{2,1,0:T(8,128)(2,1)S(1)}, f16[2,48,1024]{2,1,0:T(8,128)(2,1)S(1)}, u32[]{:S(2)}, u32[]{:S(2)}) collective-permute-start(f16[2,48,1024]{2,1,0:T(8,128)(2,1)S(1)} %get-tuple-element.70), channel_id=1, source_target_pairs={{0,4},{2,6},{4,0},{6,2},{1,5},{3,7},{5,1},{7,3},{8,12},{10,14},{12... | collective-permute-start | bytes 589832 | tf_op jit(solution)/shard_map/ppermute | solution.py:367
  178.8 15.1 %collective-permute-start.34 = (f16[2,48,1024]{2,1,0:T(8,128)(2,1)S(1)}, f16[2,48,1024]{2,1,0:T(8,128)(2,1)S(1)}, u32[]{:S(2)}, u32[]{:S(2)}) collective-permute-start(f16[2,48,1024]{2,1,0:T(8,128)(2,1)S(1)} %get-tuple-element.71), channel_id=1, source_target_pairs={{0,6},{2,4},{4,2},{6,0},{1,7},{3,5},{5,3},{7,1},{8,14},{10,12},{12... | collective-permute-start | bytes 589832 | tf_op jit(solution)/shard_map/ppermute | solution.py:367
  182.4 17.0 %collective-permute-start.28 = (f16[4,80,1024]{2,1,0:T(8,128)(2,1)S(1)}, f16[4,80,1024]{2,1,0:T(8,128)(2,1)S(1)}, u32[]{:S(2)}, u32[]{:S(2)}) collective-permute-start(f16[4,80,1024]{2,1,0:T(8,128)(2,1)S(1)} %fusion.1), channel_id=1, source_target_pairs={{0,16},{16,0},{1,17},{17,1},{2,18},{18,2},{3,19},{19,3},{4,20},{20... | collective-permute-start | bytes 1966088 | tf_op jit(solution)/shard_map/ppermute | solution.py:367
  194.1 9.3 %collective-permute-start.35 = (f16[48,1024]{1,0:T(8,128)(2,1)S(1)}, f16[48,1024]{1,0:T(8,128)(2,1)S(1)}, u32[]{:S(2)}, u32[]{:S(2)}) collective-permute-start(f16[48,1024]{1,0:T(8,128)(2,1)S(1)} %fusion.15), channel_id=1, source_target_pairs={{0,16},{16,0},{1,17},{17,1},{2,18},{18,2},{3,19},{19,3},{4,20},{20... | collective-permute-start | bytes 294920 | tf_op jit(solution)/shard_map/ppermute | solution.py:367
  199.9 5.5 %collective-permute-start.29 = (f16[80,1024]{1,0:T(8,128)(2,1)S(1)}, f16[80,1024]{1,0:T(8,128)(2,1)S(1)}, u32[]{:S(2)}, u32[]{:S(2)}) collective-permute-start(f16[80,1024]{1,0:T(8,128)(2,1)S(1)} %get-tuple-element.95), channel_id=1, source_target_pairs={{0,2},{2,0},{4,6},{6,4},{1,3},{3,1},{5,7},{7,5},{8,10},{10,8},{12,... | collective-permute-start | bytes 491528 | tf_op jit(solution)/shard_map/ppermute | solution.py:367
  200.0 8.9 %collective-permute-start.31 = (f16[80,1024]{1,0:T(8,128)(2,1)S(1)}, f16[80,1024]{1,0:T(8,128)(2,1)S(1)}, u32[]{:S(2)}, u32[]{:S(2)}) collective-permute-start(f16[80,1024]{1,0:T(8,128)(2,1)S(1)} %get-tuple-element.96), channel_id=1, source_target_pairs={{0,6},{2,4},{4,2},{6,0},{1,7},{3,5},{5,3},{7,1},{8,14},{10,12},{12... | collective-permute-start | bytes 491528 | tf_op jit(solution)/shard_map/ppermute | solution.py:367
  202.0 13.0 %collective-permute-start.30 = (f16[80,1024]{1,0:T(8,128)(2,1)S(1)}, f16[80,1024]{1,0:T(8,128)(2,1)S(1)}, u32[]{:S(2)}, u32[]{:S(2)}) collective-permute-start(f16[80,1024]{1,0:T(8,128)(2,1)S(1)} %get-tuple-element.97), channel_id=1, source_target_pairs={{0,4},{2,6},{4,0},{6,2},{1,5},{3,7},{5,1},{7,3},{8,12},{10,14},{12... | collective-permute-start | bytes 491528 | tf_op jit(solution)/shard_map/ppermute | solution.py:367
  217.4 6.7 %collective-permute-start.37 = (bf16[1024,128]{1,0:T(8,128)(2,1)S(1)}, bf16[1024,128]{1,0:T(8,128)(2,1)S(1)}, u32[]{:S(2)}, u32[]{:S(2)}) collective-permute-start(bf16[1024,128]{1,0:T(8,128)(2,1)S(1)} %shard_map.75.refs_0_), channel_id=1, source_target_pairs={{0,16},{16,0},{1,17},{17,1},{2,18},{18,2},{3,19},{19,3},{4,20},{20... | collective-permute-start | bytes 786440 | tf_op jit(solution)/shard_map/ppermute | solution.py:367
  217.9 9.2 %copy-start.1 = (f32[4096,128]{1,0:T(8,128)S(1)}, f32[4096,128]{1,0:T(8,128)}, u32[]{:S(2)}) copy-start(f32[4096,128]{1,0:T(8,128)} %param.8) | copy-start | bytes 6291460
  219.6 4.6 %collective-permute-start.36 = (bf16[1024,128]{1,0:T(8,128)(2,1)S(1)}, bf16[1024,128]{1,0:T(8,128)(2,1)S(1)}, u32[]{:S(2)}, u32[]{:S(2)}) collective-permute-start(bf16[1024,128]{1,0:T(8,128)(2,1)S(1)} %shard_map.75.refs_0_), channel_id=1, source_target_pairs={{0,8},{8,0},{1,9},{9,1},{2,10},{10,2},{3,11},{11,3},{4,12},{12,4},... | collective-permute-start | bytes 786440 | tf_op jit(solution)/shard_map/ppermute | solution.py:367
  224.1 1.5 collective-permute-start.38
